TPU v7x, 128 devices: a whole 4x4x4 slice. The times are simulated.
128 devices in a mesh: tm: 16 (over x, y), space: 8 (over z, core).
Axes of the slice: x: 4, y: 4, z: 4, core: 2. Of those that a mesh axis runs over, the one named last changes fastest.
Arguments:
- video: bfloat16 [64, 1152, 1536], P('tm', 'space'), may hold values from -6 to 6
- frame_count: int32 [1], replicated, may hold values from 16 to 64
- qkv_space: bfloat16 [1536, 3072], replicated, may hold values from -0.15625 to 0.15625
- out_space: bfloat16 [1024, 1536], replicated, may hold values from -0.1875 to 0.1875
- qkv_time: bfloat16 [1536, 3072], replicated, may hold values from -0.15625 to 0.15625
- out_time: bfloat16 [1024, 1536], replicated, may hold values from -0.1875 to 0.1875
Outputs:
- encoded: bfloat16 [64, 1152, 1536], P('tm', 'space')
All inputs are finite; a program needn't handle non-finite values.
Results may differ from a plain program's by a relative error of at most 0.0085.
Values may be sent and summed in bfloat16 or wider, within the bound.
No kernel may reach another device: no remote copies, remote signals or barrier semaphores. Data moves between devices by JAX's collectives and lax.ppermute only.
A program may use at most 192 MiB of HBM per device.

v0:
```python
import jax
import jax.numpy as jnp
from jax import lax
from jax.sharding import PartitionSpec as P

H = 16
HD = 64


def layer_norm(values):
    wide = values.astype(jnp.float32)
    center = wide - jnp.mean(wide, axis=-1, keepdims=True)
    spread = jnp.mean(center * center, axis=-1, keepdims=True)
    return (center * lax.rsqrt(spread + 1e-06)).astype(jnp.bfloat16)


def spatial_attend(items):
    count = items.shape[0]
    total = items.shape[1]
    local_heads = items.shape[3] // HD
    parts = items.reshape(count, total, 3, local_heads, HD)
    scores = (
        jnp.einsum(
            "fqhd,fkhd->fhqk", parts[:, :, 0], parts[:, :, 1], preferred_element_type=jnp.float32
        )
        * 0.125
    )
    weights = jax.nn.softmax(scores, axis=-1).astype(jnp.bfloat16)
    result = jnp.einsum(
        "fhqk,fkhd->fqhd", weights, parts[:, :, 2], preferred_element_type=jnp.float32
    )
    result = result.astype(jnp.bfloat16).reshape(count, total, local_heads * HD)
    return lax.all_to_all(result, "space", split_axis=1, concat_axis=2, tiled=True)


def per_device(video, frame_count, qkv_space, out_space, qkv_time, out_time):
    frames, patches, width = video.shape
    first = lax.axis_index("tm") * frames
    limit = frame_count[0]
    valid = (first + jnp.arange(frames) < limit).astype(jnp.float32)[:, None, None]
    norm1 = layer_norm(video)
    qkv1 = jnp.dot(
        norm1.reshape(frames * patches, width), qkv_space, preferred_element_type=jnp.float32
    )
    qkv1 = qkv1.astype(jnp.bfloat16).reshape(frames, patches, 3, H * HD)
    spatial = spatial_attend(lax.all_to_all(qkv1, "space", split_axis=3, concat_axis=1, tiled=True))
    branch = jnp.dot(
        spatial.reshape(frames * patches, H * HD), out_space, preferred_element_type=jnp.float32
    )
    middle = (video.astype(jnp.float32) + valid * branch.reshape(frames, patches, width)).astype(
        jnp.bfloat16
    )
    norm2 = layer_norm(middle)
    qkv2 = jnp.dot(
        norm2.reshape(frames * patches, width), qkv_time, preferred_element_type=jnp.float32
    )
    qkv2 = qkv2.astype(jnp.bfloat16).reshape(frames, patches, 3 * H * HD)
    gathered = lax.all_to_all(qkv2, "tm", split_axis=1, concat_axis=0, tiled=True)
    all_frames, few_patches = (gathered.shape[0], gathered.shape[1])
    parts = gathered.reshape(all_frames, few_patches, 3, H, HD)
    scores = (
        jnp.einsum(
            "fphd,gphd->phfg", parts[:, :, 0], parts[:, :, 1], preferred_element_type=jnp.float32
        )
        * 0.125
    )
    key_valid = jnp.arange(all_frames) < limit
    scores = jnp.where(key_valid[None, None, None, :], scores, -1e30)
    weights = jax.nn.softmax(scores, axis=-1).astype(jnp.bfloat16)
    temporal = jnp.einsum(
        "phfg,gphd->fphd", weights, parts[:, :, 2], preferred_element_type=jnp.float32
    )
    temporal = temporal.astype(jnp.bfloat16).reshape(all_frames, few_patches, H * HD)
    returned = lax.all_to_all(temporal, "tm", split_axis=0, concat_axis=1, tiled=True)
    branch2 = jnp.dot(
        returned.reshape(frames * patches, H * HD), out_time, preferred_element_type=jnp.float32
    )
    return (middle.astype(jnp.float32) + valid * branch2.reshape(frames, patches, width)).astype(
        jnp.bfloat16
    )


def solution(mesh):
    return jax.shard_map(
        per_device,
        mesh=mesh,
        in_specs=(P("tm", "space", None), P(), P(), P(), P(), P()),
        out_specs=P("tm", "space", None),
        check_vma=False,
    )
```

profile of v0, /device:TPU:0, one launch (start us, length us, event | category | flops | bytes accessed | tf_op | source)
XLA Modules:
  0.0 348.2 jit_solution(6353712201065361152)
XLA Ops:
  0.0 0.0 copy-start
  0.0 0.0 copy-start.1
  0.0 1.9 convert_reduce_fusion.1
  2.0 2.1 fusion.12
  4.1 0.0 copy-done.1
  4.1 0.5 fusion.13
  4.6 11.0 %convolution_convert_fusion.1 = bf16[576,3072]{1,0:T(8,128)(2,1)} fusion(bf16[576,1536]{1,0:T(8,128)(2,1)S(1)} %bitcast.93, bf16[1536,3072]{1,0:T(8,128)(2,1)} %param.8), kind=kOutput, calls=%fused_computation.18 | convolution fusion | flops 5437587456 | bytes 14745600 | tf_op jit(solution)/shard_map/dot_general | solution.py:42
  15.6 10.6 %reshape.75 = bf16[4,144,3,1024]{3,2,1,0:T(4,128)(2,1)} reshape(bf16[576,3072]{1,0:T(8,128)(2,1)} %convolution_convert_fusion.1) | data formatting | bytes 7077888 | tf_op jit(solution)/shard_map/reshape | solution.py:45
  26.2 13.6 %copy.50 = bf16[4,144,3,1024]{1,0,2,3:T(4,128)(2,1)} copy(bf16[4,144,3,1024]{3,2,1,0:T(4,128)(2,1)} %reshape.75) | data formatting | bytes 7077888 | tf_op jit(solution)/shard_map/reshape | solution.py:45
  39.8 78.5 %all_to_all.60 = bf16[4,144,3,1024]{1,0,2,3:T(4,128)(2,1)S(1)} all-to-all(bf16[4,144,3,1024]{1,0,2,3:T(4,128)(2,1)} %copy.50), channel_id=1, replica_groups=mesh['tm'=16,'space'=8] {'space'}, dimensions={3} | all-to-all | bytes 7077888 | tf_op jit(solution)/shard_map/all_to_all | solution.py:46
  118.4 6.3 %copy.96 = bf16[4,144,3,8,128]{1,3,4,2,0:T(8,128)(2,1)} copy(bf16[4,144,3,8,128]{1,0,2,4,3:T(4,128)(2,1)S(1)} %bitcast.88) | data formatting | bytes 7077888 | tf_op jit(solution)/shard_map/all_to_all | solution.py:46
  124.7 10.3 %reshape.76 = bf16[4,1152,3,2,64]{1,4,3,2,0:T(8,128)(2,1)} reshape(bf16[4,8,144,3,128]{2,1,4,3,0:T(8,128)(2,1)} %bitcast.89) | data formatting | bytes 7077888 | tf_op jit(solution)/shard_map/reshape | solution.py:21
  135.0 20.5 %fusion.37 = (f32[4,2,1152]{2,1,0:T(2,128)S(1)}, f32[4,2,1152,1152]{2,3,1,0:T(8,128)}) fusion(bf16[4,1152,3,2,64]{1,4,3,2,0:T(8,128)(2,1)} %reshape.76), kind=kOutput, calls=%fused_computation.60 | convolution fusion | flops 1390806144 | bytes 44863488 | tf_op jit(solution)/shard_map/sub | solution.py:28
  155.5 16.3 %fusion.18 = bf16[4,2,64,1152]{3,2,1,0:T(8,128)(2,1)} fusion(f32[4,2,1152,1152]{2,3,1,0:T(8,128)} %get-tuple-element.9, f32[4,2,1152]{2,1,0:T(2,128)S(1)} %get-tuple-element.8, bf16[4,1152,3,2,64]{1,4,3,2,0:T(8,128)(2,1)} %reshape.76), kind=kOutput, calls=%fused_computation.32 | convolution fusion | flops 1380777984 | bytes 44863488 | tf_op jit(solution)/shard_map/fhqk,fkhd->fqhd/dot_general | solution.py:29
  171.8 3.4 copy.57
  175.2 4.5 %all-to-all-start.1 = ((bf16[4,1152,128]{2,0,1:T(4,128)(2,1)}), bf16[4,1152,128]{2,0,1:T(4,128)(2,1)}, u32[]{:S(2)}, u32[]{:S(2)}) async-start(bf16[4,1152,128]{2,0,1:T(4,128)(2,1)} %copy.57), calls=%async_computation.1 | async-start | bytes 2359296 | tf_op jit(solution)/shard_map/all_to_all | solution.py:33
  180.3 16.5 %all-to-all-done.1 = bf16[4,1152,128]{2,0,1:T(4,128)(2,1)} async-done(((bf16[4,1152,128]{2,0,1:T(4,128)(2,1)}), bf16[4,1152,128]{2,0,1:T(4,128)(2,1)}, u32[]{:S(2)}, u32[]{:S(2)}) %all-to-all-start.1) | async-done | bytes 1179680 | tf_op jit(solution)/shard_map/all_to_all | solution.py:33
  196.8 1.4 copy.58
  198.2 0.0 slice-start
  198.3 0.0 copy-done
  198.3 0.0 slice-start.1
  198.3 0.0 slice-start.2
  198.3 3.8 %convert_reduce_fusion = (f32[4,144]{1,0:T(4,128)S(1)}, bf16[4,144,1536]{2,1,0:T(8,128)(2,1)S(1)}) fusion(bf16[1024,1536]{1,0:T(8,128)(2,1)S(1)} %copy-done, bf16[4,8,18,8,128]{4,3,2,1,0:T(8,128)(2,1)S(1)} %bitcast.97, f32[4]{0:T(128)S(1)} %compare_convert_fusion, bf16[4,144,1536]{2,1,0:T(8,128)(2,1)} %param.6), kind=kOutput, calls=%fused_computation.10 | convolution fusion | flops 1817247232 | bytes 7866640 | tf_op jit(solution)/shard_map/dot_general | solution.py:47
  202.1 0.0 copy-start.2
  202.1 0.6 fusion.10
  202.8 0.6 copy-done.2
  203.3 0.5 fusion.11
  203.8 0.0 slice-done
  203.8 0.0 slice-done.1
  203.8 0.0 slice-done.2
  203.9 5.9 %convolution_convert_fusion = bf16[576,3072]{1,0:T(8,128)(2,1)S(1)} fusion(bf16[576,1536]{1,0:T(8,128)(2,1)S(1)} %bitcast.94, bf16[1536,3072]{1,0:T(8,128)(2,1)S(1)} %bitcast.99), kind=kOutput, calls=%fused_computation.17 | convolution fusion | flops 5437587456 | bytes 14745600 | tf_op jit(solution)/shard_map/dot_general | solution.py:54
  209.7 4.5 %copy.60 = bf16[4,144,3072]{2,0,1:T(4,128)(2,1)} copy(bf16[4,144,3072]{2,1,0:T(8,128)(2,1)S(1)} %bitcast.91) | data formatting | bytes 7077888 | tf_op jit(solution)/shard_map/reshape | solution.py:57
  214.3 7.1 %all-to-all-start.2 = ((bf16[4,144,3072]{2,0,1:T(4,128)(2,1)}), bf16[4,144,3072]{2,0,1:T(4,128)(2,1)}, u32[]{:S(2)}, u32[]{:S(2)}) async-start(bf16[4,144,3072]{2,0,1:T(4,128)(2,1)} %copy.60), calls=%async_computation.2 | async-start | bytes 7077888 | tf_op jit(solution)/shard_map/all_to_all | solution.py:58
  221.4 47.0 %all-to-all-done.2 = bf16[4,144,3072]{2,0,1:T(4,128)(2,1)} async-done(((bf16[4,144,3072]{2,0,1:T(4,128)(2,1)}), bf16[4,144,3072]{2,0,1:T(4,128)(2,1)}, u32[]{:S(2)}, u32[]{:S(2)}) %all-to-all-start.2) | async-done | bytes 3538976 | tf_op jit(solution)/shard_map/all_to_all | solution.py:58
  268.3 5.3 %copy.61 = bf16[16,4,9,3072]{3,1,0,2:T(4,128)(2,1)} copy(bf16[16,4,9,3072]{3,1,2,0:T(4,128)(2,1)} %bitcast.16) | data formatting | bytes 7077888 | tf_op jit(solution)/shard_map/all_to_all | solution.py:58
  273.6 10.1 %reshape.80 = bf16[64,9,3,16,64]{4,3,2,0,1:T(8,128)(2,1)} reshape(bf16[16,4,9,3072]{3,1,0,2:T(4,128)(2,1)} %copy.61) | data formatting | bytes 7077888 | tf_op jit(solution)/shard_map/reshape | solution.py:60
  283.7 6.9 %fusion.36 = (bf16[64,9,1,16,64]{4,3,2,0,1:T(8,128)(2,1)}, bf16[64,9,1,16,64]{4,3,2,0,1:T(8,128)(2,1)}, bf16[64,9,1,16,64]{4,3,2,0,1:T(8,128)(2,1)}) fusion(bf16[64,9,3,16,64]{4,3,2,0,1:T(8,128)(2,1)} %reshape.80), kind=kLoop, calls=%fused_computation.59 | loop fusion | bytes 7077888 | tf_op jit(solution)/shard_map/slice | solution.py:71
  290.6 4.6 %copy.79 = bf16[64,9,1,16,64]{0,4,3,1,2:T(8,128)(2,1)} copy(bf16[64,9,1,16,64]{4,3,2,0,1:T(8,128)(2,1)} %get-tuple-element.5) | data formatting | bytes 2359296
  295.2 3.7 %fusion.20 = f32[9,16,64,64]{2,3,1,0:T(8,128)S(1)} fusion(bf16[64,9,1,16,64]{4,3,2,0,1:T(8,128)(2,1)} %get-tuple-element.6, bf16[64,9,1,16,64]{4,3,2,0,1:T(8,128)(2,1)} %get-tuple-element.7), kind=kOutput, calls=%fused_computation.35 | convolution fusion | flops 75497472 | bytes 4718592 | tf_op jit(solution)/shard_map/fphd,gphd->phfg/dot_general | solution.py:62
  299.0 1.8 fusion.38
  300.8 0.0 copy-done.4
  300.8 2.2 fusion.26
  303.0 5.3 %copy.66 = bf16[64,9,1024]{2,1,0:T(8,128)(2,1)} copy(bf16[64,9,1024]{0,2,1:T(8,128)(2,1)} %bitcast.92) | data formatting | bytes 2359296 | tf_op jit(solution)/shard_map/reshape | solution.py:73
  308.3 35.6 %all_to_all.61 = bf16[64,9,1024]{2,1,0:T(8,128)(2,1)S(1)} all-to-all(bf16[64,9,1024]{2,1,0:T(8,128)(2,1)} %copy.66), channel_id=1, replica_groups=mesh['tm'=16,'space'=8] {'tm'}, dimensions={0} | all-to-all | bytes 2359296 | tf_op jit(solution)/shard_map/all_to_all | solution.py:74
  343.9 1.1 copy.75
  345.0 0.0 copy-done.3
  345.0 0.0 copy-done.5
  345.0 3.2 fusion.15
  (10 shorter events, 0.0 us)
Async XLA Ops:
  0.0 198.3 %copy-start = (bf16[1024,1536]{1,0:T(8,128)(2,1)S(1)}, bf16[1024,1536]{1,0:T(8,128)(2,1)}, u32[]{:S(2)}) copy-start(bf16[1024,1536]{1,0:T(8,128)(2,1)} %param.9) | copy-start | bytes 9437188
  0.0 4.1 %copy-start.1 = (bf16[4,144,1536]{2,1,0:T(8,128)(2,1)S(1)}, bf16[4,144,1536]{2,1,0:T(8,128)(2,1)}, u32[]{:S(2)}) copy-start(bf16[4,144,1536]{2,1,0:T(8,128)(2,1)} %param.6) | copy-start | bytes 5308420
  175.2 21.6 %all-to-all-start.1 = ((bf16[4,1152,128]{2,0,1:T(4,128)(2,1)}), bf16[4,1152,128]{2,0,1:T(4,128)(2,1)}, u32[]{:S(2)}, u32[]{:S(2)}) async-start(bf16[4,1152,128]{2,0,1:T(4,128)(2,1)} %copy.57), calls=%async_computation.1 | async-start | bytes 2359296 | tf_op jit(solution)/shard_map/all_to_all | solution.py:33
  198.2 5.6 %slice-start = ((s8[9437184]{0:T(1024)(128)(4,1)}), s8[4194304]{0:T(1024)(128)(4,1)S(1)}, s32[]{:S(2)}) async-start(s8[9437184]{0:T(1024)(128)(4,1)} %bitcast.98), calls=%async_computation.4 | async-start | bytes 8388608
  198.3 5.6 %slice-start.1 = ((s8[9437184]{0:T(1024)(128)(4,1)}), s8[4194304]{0:T(1024)(128)(4,1)S(1)}, s32[]{:S(2)}) async-start(s8[9437184]{0:T(1024)(128)(4,1)} %bitcast.98), calls=%async_computation.5 | async-start | bytes 8388608
  198.3 5.6 %slice-start.2 = ((s8[9437184]{0:T(1024)(128)(4,1)}), s8[1048576]{0:T(1024)(128)(4,1)S(1)}, s32[]{:S(2)}) async-start(s8[9437184]{0:T(1024)(128)(4,1)} %bitcast.98), calls=%async_computation.6 | async-start | bytes 2097152
  202.1 1.2 copy-start.2
  214.3 54.1 %all-to-all-start.2 = ((bf16[4,144,3072]{2,0,1:T(4,128)(2,1)}), bf16[4,144,3072]{2,0,1:T(4,128)(2,1)}, u32[]{:S(2)}, u32[]{:S(2)}) async-start(bf16[4,144,3072]{2,0,1:T(4,128)(2,1)} %copy.60), calls=%async_computation.2 | async-start | bytes 7077888 | tf_op jit(solution)/shard_map/all_to_all | solution.py:58
  299.0 1.8 copy-start.4
  308.3 36.7 %copy-start.3 = (bf16[4,144,1536]{2,1,0:T(8,128)(2,1)S(1)}, bf16[4,144,1536]{2,1,0:T(8,128)(2,1)}, u32[]{:S(2)}) copy-start(bf16[4,144,1536]{2,1,0:T(8,128)(2,1)} %copy-done.2) | copy-start | bytes 5308420
  308.3 36.7 %copy-start.5 = (bf16[1024,1536]{1,0:T(8,128)(2,1)S(1)}, bf16[1024,1536]{1,0:T(8,128)(2,1)}, u32[]{:S(2)}) copy-start(bf16[1024,1536]{1,0:T(8,128)(2,1)} %param.11) | copy-start | bytes 9437188
where the time goes:
time: 350 us; the launch traced here: 348 us
  blocking collectives  114 us (33%)
  local copies, waits for them, and re-layouts  84 us (24%)
  matrix products  66.7 us (19%)
  waiting for transfers between devices  63.4 us (18%)
  starting transfers between devices  11.6 us (3%)
  other arithmetic  7.5 us (2%)
    all_to_all x1, blocking collectives, per_device(): lax.all_to_all(qkv1, 'space', split_axis=3, concat_axis=1, tiled=True)  78.5 us
    all_to_all x1, waiting for transfers between devices, per_device(): lax.all_to_all(qkv2, 'tm', split_axis=1, concat_axis=0, tiled=True)  47 us
    all_to_all x1, blocking collectives, per_device(): lax.all_to_all(temporal, 'tm', split_axis=0, concat_axis=1, tiled=True)  35.6 us
    reshape x2, local copies, waits for them, and re-layouts, per_device(): qkv1 = qkv1.astype(jnp.bfloat16).reshape(frames, patches, 3, H * HD)  24.2 us
    sub x1, matrix products, spatial_attend(): weights = jax.nn.softmax(scores, axis=-1).astype(jnp.bfloat16)  20.5 us
    all_to_all x1, waiting for transfers between devices, spatial_attend(): lax.all_to_all(result, 'space', split_axis=1, concat_axis=2, tiled=True)  16.5 us
    dot_general x1, matrix products, spatial_attend(): jnp.einsum('fhqk,fkhd->fqhd', weights, parts[:, :, 2], preferred_element_...  16.3 us
    dot_general x1, matrix products, per_device(): jnp.dot(norm1.reshape(frames * patches, width), qkv_space, preferred_elem...  11 us
  transfers between devices with their start and end apart: 2, of which 2 were waited for; matrix products, arithmetic and copies ran while one was open for 0% of the time, Pallas kernels for 0%

commit v1 on v0

v1 whole, which is shorter than its diff:
```python
import functools

import jax
import jax.numpy as jnp
from jax import lax
from jax.experimental import pallas as pl
from jax.experimental.pallas import tpu as pltpu
from jax.sharding import PartitionSpec as P

H = 16
HD = 64
WIDTH = 1536
HW = H * HD
TM = 16
QSCALE = 0.125 * 1.4426950408889634
CHUNKS = (9,)
OFFSETS = tuple(sum(CHUNKS[:j]) for j in range(len(CHUNKS)))
SWAP = [(i, i ^ 1) for i in range(8)]
Z_GROUPS = [[0, 2, 4, 6], [1, 3, 5, 7]]
BF = jnp.bfloat16
F32 = jnp.float32
VMEM = 56 * 1024 * 1024


def params(**more):
    return pltpu.CompilerParams(vmem_limit_bytes=VMEM, **more)


def normalise(wide):
    center = wide - jnp.mean(wide, axis=-1, keepdims=True)
    spread = jnp.mean(center * center, axis=-1, keepdims=True)
    return (center * lax.rsqrt(spread + 1e-06)).astype(BF)


def nt_dot(a, b):
    return lax.dot_general(a, b, (((1,), (1,)), ((), ())), preferred_element_type=F32)


def tn_dot(a, b):
    return lax.dot_general(a, b, (((0,), (0,)), ((), ())), preferred_element_type=F32)


def kv_kernel(x_ref, w_ref, kv_ref, norm_ref):
    @pl.when(pl.program_id(0) == 0)
    def _():
        def step(i, carry):
            rows = pl.ds(pl.multiple_of(i * 64, 64), 64)
            norm_ref[rows, :] = normalise(x_ref[rows, :].astype(F32))
            return carry

        lax.fori_loop(0, x_ref.shape[0] // 64, step, 0)

    kv_ref[...] = jnp.dot(norm_ref[...], w_ref[...], preferred_element_type=F32).astype(BF)


def keys_values(x, w):
    rows = x.shape[0]
    return pl.pallas_call(
        kv_kernel,
        grid=(4,),
        in_specs=[
            pl.BlockSpec((rows, WIDTH), lambda j: (0, 0)),
            pl.BlockSpec((WIDTH, 512), lambda j: (0, j + 2)),
        ],
        out_specs=[
            pl.BlockSpec((rows, 512), lambda j: (0, j)),
            pl.BlockSpec((rows, WIDTH), lambda j: (0, 0)),
        ],
        out_shape=[
            jax.ShapeDtypeStruct((rows, 2 * HW), BF),
            jax.ShapeDtypeStruct((rows, WIDTH), BF),
        ],
        compiler_params=params(),
        cost_estimate=pl.CostEstimate(
            flops=2 * rows * WIDTH * 2 * HW, bytes_accessed=12_000_000, transcendentals=0
        ),
        name="keys_values",
    )(x, w)


def q_kernel(norm_ref, w_ref, *q_refs):
    q = jnp.dot(norm_ref[...], w_ref[...], preferred_element_type=F32) * QSCALE
    q = q.astype(BF)
    for n, off, q_ref in zip(CHUNKS, OFFSETS, q_refs):
        for z in range(4):
            lo = z * 144 + off * 16
            q_ref[z] = q[lo : lo + n * 16]


def queries(norm, w):
    rows = norm.shape[0]
    return pl.pallas_call(
        q_kernel,
        grid=(2,),
        in_specs=[
            pl.BlockSpec((rows, WIDTH), lambda j: (0, 0)),
            pl.BlockSpec((WIDTH, 512), lambda j: (0, j)),
        ],
        out_specs=[pl.BlockSpec((4, 16 * n, 512), lambda j: (0, 0, j)) for n in CHUNKS],
        out_shape=[jax.ShapeDtypeStruct((4, 16 * n, HW), BF) for n in CHUNKS],
        compiler_params=params(),
        cost_estimate=pl.CostEstimate(
            flops=2 * rows * WIDTH * HW, bytes_accessed=6_000_000, transcendentals=0
        ),
        name="queries",
    )(norm, w)


def spatial_kernel(block, q_ref, ka_ref, kb_ref, va_ref, vb_ref, o_ref, kk, v0, v1):
    half = ka_ref.shape[0]
    low_v = lax.broadcasted_iota(jnp.int32, (half, 128), 1) < HD
    one = jnp.ones((half, 128), BF)
    for part, (k_ref, v_ref) in enumerate(((ka_ref, va_ref), (kb_ref, vb_ref))):
        rows = slice(part * half, (part + 1) * half)
        kk[rows, :] = k_ref[...]
        v = v_ref[...]
        v0[rows, :] = jnp.where(low_v, v, one)
        v1[rows, :] = jnp.where(low_v, one, v)
    low = lax.broadcasted_iota(jnp.int32, (block, 128), 1) < HD
    zero = jnp.zeros((block, 128), BF)

    def attend(q, v):
        s = nt_dot(q, kk[...])
        p = jnp.exp2(s - jnp.max(s, axis=-1, keepdims=True)).astype(BF)
        return jnp.dot(p, v[...], preferred_element_type=F32)

    def step(i, carry):
        rows = pl.ds(pl.multiple_of(i * block, block), block)
        q = q_ref[rows, :]
        o0 = attend(jnp.where(low, q, zero), v0)
        o1 = attend(jnp.where(low, zero, q), v1)
        top = jnp.where(low, o0, o1)
        total = pltpu.roll(jnp.where(low, o1, o0), HD, 1)
        o_ref[rows, :] = (top / total).astype(BF)
        return carry

    lax.fori_loop(0, q_ref.shape[0] // block, step, 0)


def spatial_attention(q, kv_a, kv_b, block):
    rows, half = q.shape[0], kv_a.shape[0]
    pairs = H // 2
    return pl.pallas_call(
        functools.partial(spatial_kernel, block),
        grid=(pairs,),
        in_specs=[
            pl.BlockSpec((rows, 128), lambda h: (0, h)),
            pl.BlockSpec((half, 128), lambda h: (0, h)),
            pl.BlockSpec((half, 128), lambda h: (0, h)),
            pl.BlockSpec((half, 128), lambda h: (0, h + pairs)),
            pl.BlockSpec((half, 128), lambda h: (0, h + pairs)),
        ],
        out_specs=pl.BlockSpec((rows, 128), lambda h: (0, h)),
        out_shape=jax.ShapeDtypeStruct((rows, HW), BF),
        scratch_shapes=[pltpu.VMEM((2 * half, 128), BF)] * 3,
        compiler_params=params(),
        cost_estimate=pl.CostEstimate(
            flops=16 * rows * half * HW, bytes_accessed=8_000_000, transcendentals=2 * rows * half * H
        ),
        name="spatial_attention",
    )(q, kv_a, kv_b, kv_a, kv_b)


def reorder(to_patch_major):
    row = lax.broadcasted_iota(jnp.int32, (64, 64), 0)
    col = lax.broadcasted_iota(jnp.int32, (64, 64), 1)
    if to_patch_major:
        return (col == (row % 4) * 16 + row // 4).astype(BF)
    return (col == (row % 16) * 4 + row // 16).astype(BF)


def middle_kernel(off, n, scalars, s_ref, x_ref, w_ref, middle_ref, send_ref, norm):
    span = 16 * n
    first, limit = scalars[0], scalars[1]
    for f in range(4):
        valid = (first + f < limit).astype(F32)
        branch = jnp.dot(s_ref[f], w_ref[...], preferred_element_type=F32)
        x = x_ref[f, off * 16 : off * 16 + span, :].astype(F32)
        middle = (x + valid * branch).astype(BF)
        middle_ref[f] = middle
        norm[f] = normalise(middle.astype(F32))
    move = reorder(True)
    for b in range(n):
        rows = slice(b * 16, b * 16 + 16)
        block = jnp.concatenate([norm[f, rows, :] for f in range(4)], axis=0)
        moved = jnp.dot(move, block, preferred_element_type=F32).astype(BF)
        send_ref[rows] = moved.reshape(16, 4, WIDTH)


def middle_rows(scalars, spatial, video, w, off, n):
    span = 16 * n
    return pl.pallas_call(
        functools.partial(middle_kernel, off, n),
        in_specs=[
            pl.BlockSpec(memory_space=pltpu.SMEM),
            pl.BlockSpec(memory_space=pltpu.VMEM),
            pl.BlockSpec(memory_space=pltpu.VMEM),
            pl.BlockSpec(memory_space=pltpu.VMEM),
        ],
        out_specs=[
            pl.BlockSpec(memory_space=pltpu.VMEM),
            pl.BlockSpec(memory_space=pltpu.VMEM),
        ],
        out_shape=[
            jax.ShapeDtypeStruct((4, span, WIDTH), BF),
            jax.ShapeDtypeStruct((span, 4, WIDTH), BF),
        ],
        scratch_shapes=[pltpu.VMEM((4, span, WIDTH), BF)],
        compiler_params=params(),
        cost_estimate=pl.CostEstimate(
            flops=8 * span * HW * WIDTH, bytes_accessed=8_000_000, transcendentals=0
        ),
        name="middle_rows",
    )(scalars, spatial, video, w)


def temporal_kernel(n, scalars, x_ref, wq_ref, wk_ref, wv_ref, o_ref, rows_ref):
    @pl.when(pl.program_id(0) == 0)
    def _():
        for i in range(n):
            rows_ref[64 * i : 64 * i + 64, :] = x_ref[:, i].reshape(64, WIDTH)

    limit = scalars[1]
    x = rows_ref[...]
    q = (jnp.dot(x, wq_ref[...], preferred_element_type=F32) * QSCALE).astype(BF)
    k = jnp.dot(x, wk_ref[...], preferred_element_type=F32).astype(BF)
    v = jnp.dot(x, wv_ref[...], preferred_element_type=F32).astype(BF)
    head_row = lax.broadcasted_iota(jnp.int32, (256, 256), 0) // HD
    head_col = lax.broadcasted_iota(jnp.int32, (256, 256), 1) // HD
    same = head_row == head_col
    zero = jnp.zeros((256, 256), BF)
    key_valid = lax.broadcasted_iota(jnp.int32, (4, 64, 64), 1) < limit
    for i in range(n):
        rows = slice(64 * i, 64 * i + 64)
        k4 = jnp.where(same, jnp.concatenate([k[rows]] * 4, axis=0), zero)
        v4 = jnp.where(same, jnp.concatenate([v[rows]] * 4, axis=0), zero)
        s = nt_dot(k4, q[rows]).reshape(4, 64, 64)
        s = jnp.where(key_valid, s, -1e30)
        p = jnp.exp2(s - jnp.max(s, axis=1, keepdims=True))
        p = (p / jnp.sum(p, axis=1, keepdims=True)).reshape(256, 64).astype(BF)
        o_ref[:, i] = tn_dot(p, v4).astype(BF).reshape(16, 4, 256)


def temporal_attention(scalars, x, w, n):
    rows = 64 * n
    return pl.pallas_call(
        functools.partial(temporal_kernel, n),
        grid=(4,),
        in_specs=[
            pl.BlockSpec(memory_space=pltpu.SMEM),
            pl.BlockSpec((TM, n, 4, WIDTH), lambda g: (0, 0, 0, 0)),
            pl.BlockSpec((WIDTH, 256), lambda g: (0, g)),
            pl.BlockSpec((WIDTH, 256), lambda g: (0, g + 4)),
            pl.BlockSpec((WIDTH, 256), lambda g: (0, g + 8)),
        ],
        out_specs=pl.BlockSpec((TM, n, 4, 256), lambda g: (0, 0, 0, g)),
        out_shape=jax.ShapeDtypeStruct((TM, n, 4, HW), BF),
        scratch_shapes=[pltpu.VMEM((rows, WIDTH), BF)],
        compiler_params=params(),
        cost_estimate=pl.CostEstimate(
            flops=2 * rows * WIDTH * 3 * HW, bytes_accessed=14_000_000, transcendentals=0
        ),
        name="temporal_attention",
    )(scalars, x, w, w, w)


def encoded_kernel(scalars, *refs):
    count = len(CHUNKS)
    t_refs, m_refs = refs[:count], refs[count : 2 * count]
    w_ref, o_ref, rows_ref = refs[2 * count :]

    @pl.when(pl.program_id(0) == 0)
    def _():
        move = reorder(False)
        for n, off, t_ref in zip(CHUNKS, OFFSETS, t_refs):
            for b in range(n):
                block = t_ref[b * 16 : b * 16 + 16].reshape(64, HW)
                moved = jnp.dot(move, block, preferred_element_type=F32).astype(BF)
                for f in range(4):
                    lo = (off + b) * 16
                    rows_ref[f, lo : lo + 16, :] = moved[f * 16 : f * 16 + 16]

    first, limit = scalars[0], scalars[1]
    for f in range(4):
        valid = (first + f < limit).astype(F32)
        branch = jnp.dot(rows_ref[f], w_ref[...], preferred_element_type=F32)
        for n, off, m_ref in zip(CHUNKS, OFFSETS, m_refs):
            rows = slice(off * 16, (off + n) * 16)
            o_ref[f, rows, :] = (m_ref[f].astype(F32) + valid * branch[rows]).astype(BF)


def encoded_rows(scalars, temporals, middles, w):
    columns = 512
    return pl.pallas_call(
        encoded_kernel,
        grid=(WIDTH // columns,),
        in_specs=[pl.BlockSpec(memory_space=pltpu.SMEM)]
        + [pl.BlockSpec((16 * n, 4, HW), lambda j: (0, 0, 0)) for n in CHUNKS]
        + [pl.BlockSpec((4, 16 * n, columns), lambda j: (0, 0, j)) for n in CHUNKS]
        + [pl.BlockSpec((HW, columns), lambda j: (0, j))],
        out_specs=pl.BlockSpec((4, 144, columns), lambda j: (0, 0, j)),
        out_shape=jax.ShapeDtypeStruct((4, 144, WIDTH), BF),
        scratch_shapes=[pltpu.VMEM((4, 144, HW), BF)],
        compiler_params=params(),
        cost_estimate=pl.CostEstimate(
            flops=8 * 144 * HW * WIDTH, bytes_accessed=8_000_000, transcendentals=0
        ),
        name="encoded_rows",
    )(scalars, *temporals, *middles, w)


def over_z(x):
    return lax.all_to_all(
        x, "space", split_axis=0, concat_axis=0, axis_index_groups=Z_GROUPS, tiled=True
    )


def over_tm(x):
    return lax.all_to_all(x, "tm", split_axis=0, concat_axis=0, tiled=True)


def per_device(video, frame_count, qkv_space, out_space, qkv_time, out_time):
    first = lax.axis_index("tm") * video.shape[0]
    scalars = jnp.stack([first, frame_count[0]]).astype(jnp.int32)
    frame = over_z(video).reshape(4 * 144, WIDTH)
    kv_own, norm1 = keys_values(frame, qkv_space)
    kv_other = lax.ppermute(kv_own, "space", SWAP)
    qs = queries(norm1, qkv_space)
    temporals, middles = [], []
    for n, off, q in zip(CHUNKS, OFFSETS, qs):
        spatial = spatial_attention(q.reshape(64 * n, HW), kv_own, kv_other, 192 if n % 3 == 0 else 64 * n)
        spatial = over_z(spatial.reshape(4, 16 * n, HW))
        middle, send = middle_rows(scalars, spatial, video, out_space, off, n)
        middles.append(middle)
        rows = over_tm(send.reshape(TM, n, 4, WIDTH))
        temporal = temporal_attention(scalars, rows, qkv_time, n)
        temporals.append(over_tm(temporal).reshape(16 * n, 4, HW))
    return encoded_rows(scalars, temporals, middles, out_time)


def solution(mesh):
    return jax.shard_map(
        per_device,
        mesh=mesh,
        in_specs=(P("tm", "space", None), P(), P(), P(), P(), P()),
        out_specs=P("tm", "space", None),
        check_vma=False,
    )
```

time: 350 us -> 186 us (0.53)
  local copies, waits for them, and re-layouts: 84 us -> 2.42 us
  Pallas kernels: 0 us -> 80.6 us
  matrix products: 66.7 us -> 0 us
  waiting for transfers between devices: 63.4 us -> 16.1 us
  blocking collectives: 114 us -> 81.4 us
  starting transfers between devices: 11.6 us -> 3.53 us
  other arithmetic: 7.5 us -> 0.67 us
    pallas_call x0 -> x6, Pallas kernels: none -> 80.6 us  [the longest x1 31.5 us: spatial_attention(): pl.pallas_call(functools.partial(spatial_kernel, block), grid=(pairs,), i...]
    reshape x7 -> x0, local copies, waits for them, and re-layouts: 57.8 us -> none  [the longest x2 24.2 us: per_device(): qkv1 = qkv1.astype(jnp.bfloat16).reshape(frames, patches, 3, H * HD)]
    all_to_all x2 -> x1, waiting for transfers between devices: 63.4 us -> 16.1 us  [over_z(): lax.all_to_all(x, 'space', split_axis=0, concat_axis=0, axis_index_groups...]
    dot_general x7 -> x0, matrix products: 46.2 us -> none  [the longest x1 16.3 us: spatial_attend(): jnp.einsum('fhqk,fkhd->fqhd', weights, parts[:, :, 2], preferred_element_...]
    all_to_all x2 -> x3, blocking collectives: 114 us -> 81.4 us  [the longest x2 53 us: over_tm(): return lax.all_to_all(x, 'tm', split_axis=0, concat_axis=0, tiled=True)]
    sub x1 -> x0, matrix products: 20.5 us -> none  [spatial_attend(): weights = jax.nn.softmax(scores, axis=-1).astype(jnp.bfloat16)]
    all_to_all x4 -> x0, local copies, waits for them, and re-layouts: 14.1 us -> none  [the longest x1 6.33 us: per_device(): lax.all_to_all(qkv1, 'space', split_axis=3, concat_axis=1, tiled=True)]
    all_to_all x2 -> x1, starting transfers between devices: 11.6 us -> 3.53 us  [over_z(): lax.all_to_all(x, 'space', split_axis=0, concat_axis=0, axis_index_groups...]
  transfers between devices with their start and end apart: 2 -> 2, of which waited for: 2 -> 1; matrix products, arithmetic and copies ran while one was open for 0% -> 0% of each run, Pallas kernels for 0% -> 3%
where the time goes in v1:
time: 186 us; the launch traced here: 185 us
  blocking collectives  81.4 us (44%)
  Pallas kernels  80.6 us (43%)
  waiting for transfers between devices  16.1 us (9%)
  starting transfers between devices  3.53 us (2%)
  local copies, waits for them, and re-layouts  2.42 us (1%)
    all_to_all x2, blocking collectives, over_tm(): return lax.all_to_all(x, 'tm', split_axis=0, concat_axis=0, tiled=True)  53 us
    pallas_call x1, Pallas kernels, spatial_attention(): pl.pallas_call(functools.partial(spatial_kernel, block), grid=(pairs,), i...  31.5 us
    all_to_all x1, blocking collectives, over_z(): lax.all_to_all(x, 'space', split_axis=0, concat_axis=0, axis_index_groups...  28.4 us
    pallas_call x1, Pallas kernels, temporal_attention(): pl.pallas_call(functools.partial(temporal_kernel, n), grid=(4,), in_specs...  20.4 us
    all_to_all x1, waiting for transfers between devices, over_z(): lax.all_to_all(x, 'space', split_axis=0, concat_axis=0, axis_index_groups...  16.1 us
    pallas_call x1, Pallas kernels, keys_values(): pl.pallas_call(kv_kernel, grid=(4,), in_specs=[pl.BlockSpec((rows, WIDTH)...  9.98 us
    pallas_call x1, Pallas kernels, middle_rows(): pl.pallas_call(functools.partial(middle_kernel, off, n), in_specs=[pl.Blo...  7.38 us
    pallas_call x1, Pallas kernels, encoded_rows(): pl.pallas_call(encoded_kernel, grid=(WIDTH // columns,), in_specs=[pl.Blo...  6.29 us
  transfers between devices with their start and end apart: 2, of which 1 were waited for; matrix products, arithmetic and copies ran while one was open for 0% of the time, Pallas kernels for 3%

profile of v1, /device:TPU:0, one launch (start us, length us, event | category | flops | bytes accessed | tf_op | source)
XLA Modules:
  0.0 185.4 jit_solution(12078418731861895139)
XLA Ops:
  0.0 28.4 %all_to_all.20 = bf16[4,144,1536]{2,1,0:T(8,128)(2,1)} all-to-all(bf16[4,144,1536]{2,1,0:T(8,128)(2,1)} %x_ref.1), channel_id=1, replica_groups={{0,2,4,6},{1,3,5,7},{8,10,12,14},{9,11,13,15},{16,18,20,22},{17,19,21,2..., dimensions={0} | all-to-all | bytes 3538944 | tf_op jit(solution)/shard_map/all_to_all | solution.py:313
  28.4 10.0 %keys_values.1 = (bf16[576,2048]{1,0:T(8,128)(2,1)}, bf16[576,1536]{1,0:T(8,128)(2,1)}) custom-call(bf16[576,1536]{1,0:T(8,128)(2,1)} %bitcast.8, bf16[1536,3072]{1,0:T(8,128)(2,1)} %w_ref.4), custom_call_target="tpu_custom_call" | custom-call | flops 3623878656 | bytes 12000000 | tf_op jit(solution)/shard_map/keys_values/pallas_call | solution.py:58
  38.4 0.0 collective-permute-start
  38.4 5.1 %queries.1 = bf16[4,144,1024]{2,1,0:T(8,128)(2,1)} custom-call(bf16[576,1536]{1,0:T(8,128)(2,1)} %get-tuple-element.9.norm_ref, bf16[1536,3072]{1,0:T(8,128)(2,1)} %w_ref.4), custom_call_target="tpu_custom_call" | custom-call | flops 1811939328 | bytes 6000000 | tf_op jit(solution)/shard_map/queries/pallas_call | solution.py:92
  43.4 0.0 collective-permute-done.kb_ref.vb_ref
  43.4 0.0 copy-start.1
  43.4 1.4 copy-done.1
  44.8 31.5 %spatial_attention.1 = bf16[576,1024]{1,0:T(8,128)(2,1)} custom-call(bf16[576,1024]{1,0:T(8,128)(2,1)} %bitcast.9, bf16[576,2048]{1,0:T(8,128)(2,1)} %get-tuple-element.10.ka_ref.va_ref, bf16[576,2048]{1,0:T(8,128)(2,1)} %copy-done.1, bf16[576,2048]{1,0:T(8,128)(2,1)} %get-tuple-element.10.ka_ref.va_ref, bf16[576,2048]{1,0:T(8,128)(2,1)} %copy-done.1), custom_call_target="tpu_custom_call" | custom-call | flops 5435817984 | bytes 8000000 | tf_op jit(solution)/shard_map/spatial_attention/pallas_call | solution.py:143
  76.3 3.5 %all-to-all-start.1 = ((bf16[4,144,1024]{2,1,0:T(8,128)(2,1)}), bf16[4,144,1024]{2,1,0:T(8,128)(2,1)S(1)}, u32[]{:S(2)}, u32[]{:S(2)}) async-start(bf16[4,144,1024]{2,1,0:T(8,128)(2,1)} %bitcast.10), calls=%async_computation.1 | async-start | bytes 2359296 | tf_op jit(solution)/shard_map/all_to_all | solution.py:313
  80.5 0.7 pad_add_fusion.scalars
  81.2 16.1 %all-to-all-done.1.s_ref = bf16[4,144,1024]{2,1,0:T(8,128)(2,1)S(1)} async-done(((bf16[4,144,1024]{2,1,0:T(8,128)(2,1)}), bf16[4,144,1024]{2,1,0:T(8,128)(2,1)S(1)}, u32[]{:S(2)}, u32[]{:S(2)}) %all-to-all-start.1) | async-done | bytes 1179680 | tf_op jit(solution)/shard_map/all_to_all | solution.py:313
  97.3 0.0 copy-start
  97.3 1.0 copy-done
  98.3 7.4 %middle_rows.1 = (bf16[4,144,1536]{2,1,0:T(8,128)(2,1)}, bf16[144,4,1536]{2,1,0:T(4,128)(2,1)}) custom-call(s32[2]{0:T(128)} %pad_add_fusion.scalars, bf16[4,144,1024]{2,1,0:T(8,128)(2,1)} %copy-done, bf16[4,144,1536]{2,1,0:T(8,128)(2,1)} %x_ref.1, bf16[1024,1536]{1,0:T(8,128)(2,1)} %w_ref.5), custom_call_target="tpu_custom_call" | custom-call | flops 1811939328 | bytes 8000000 | tf_op jit(solution)/shard_map/middle_rows/pallas_call | solution.py:192
  105.7 31.7 %all_to_all.21.x_ref = bf16[16,9,4,1536]{3,2,1,0:T(4,128)(2,1)} all-to-all(bf16[16,9,4,1536]{3,2,1,0:T(4,128)(2,1)} %bitcast.7), channel_id=1, replica_groups=mesh['tm'=16,'space'=8] {'tm'}, dimensions={0} | all-to-all | bytes 3538944 | tf_op jit(solution)/shard_map/all_to_all | solution.py:319
  137.3 20.4 %temporal_attention.1 = bf16[16,9,4,1024]{3,2,1,0:T(4,128)(2,1)} custom-call(s32[2]{0:T(128)} %pad_add_fusion.scalars, bf16[16,9,4,1536]{3,2,1,0:T(4,128)(2,1)} %all_to_all.21.x_ref, bf16[1536,3072]{1,0:T(8,128)(2,1)} %wv_ref.1, bf16[1536,3072]{1,0:T(8,128)(2,1)} %wv_ref.1, bf16[1536,3072]{1,0:T(8,128)(2,1)} %wv_ref.1), custom_call_target="tpu_custom_call" | custom-call | flops 5435817984 | bytes 14000000 | tf_op jit(solution)/shard_map/temporal_attention/pallas_call | solution.py:246
  157.8 21.4 %all_to_all.22 = bf16[16,9,4,1024]{3,2,1,0:T(4,128)(2,1)} all-to-all(bf16[16,9,4,1024]{3,2,1,0:T(4,128)(2,1)} %temporal_attention.1), channel_id=1, replica_groups=mesh['tm'=16,'space'=8] {'tm'}, dimensions={0} | all-to-all | bytes 2359296 | tf_op jit(solution)/shard_map/all_to_all | solution.py:319
  179.1 6.3 %encoded_rows.1 = bf16[4,144,1536]{2,1,0:T(8,128)(2,1)} custom-call(s32[2]{0:T(128)} %pad_add_fusion.scalars, bf16[144,4,1024]{2,1,0:T(4,128)(2,1)} %bitcast.6, bf16[4,144,1536]{2,1,0:T(8,128)(2,1)} %get-tuple-element.12.refs_1_, bf16[1024,1536]{1,0:T(8,128)(2,1)} %refs_2_.1), custom_call_target="tpu_custom_call" | custom-call | flops 1811939328 | bytes 8000000 | tf_op jit(solution)/shard_map/encoded_rows/pallas_call | solution.py:294
Async XLA Ops:
  38.4 5.1 %collective-permute-start = (bf16[576,2048]{1,0:T(8,128)(2,1)}, bf16[576,2048]{1,0:T(8,128)(2,1)S(1)}, u32[]{:S(2)}, u32[]{:S(2)}) collective-permute-start(bf16[576,2048]{1,0:T(8,128)(2,1)} %get-tuple-element.10.ka_ref.va_ref), channel_id=1, source_target_pairs={{0,1},{1,0},{2,3},{3,2},{4,5},{5,4},{6,7},{7,6},{8,9},{9,8},{10,11... | collective-permute-start | bytes 7077896 | tf_op jit(solution)/shard_map/ppermute | solution.py:327
  43.4 1.4 copy-start.1
  76.3 20.9 %all-to-all-start.1 = ((bf16[4,144,1024]{2,1,0:T(8,128)(2,1)}), bf16[4,144,1024]{2,1,0:T(8,128)(2,1)S(1)}, u32[]{:S(2)}, u32[]{:S(2)}) async-start(bf16[4,144,1024]{2,1,0:T(8,128)(2,1)} %bitcast.10), calls=%async_computation.1 | async-start | bytes 2359296 | tf_op jit(solution)/shard_map/all_to_all | solution.py:313
  97.3 1.0 copy-start

commit v2 on v1

--- a/solution.py
+++ b/solution.py
@@ -14,16 +14,16 @@
 TM = 16
 QSCALE = 0.125 * 1.4426950408889634
 CHUNKS = (9,)
+SUB = {9: 144, 5: 160, 4: 128, 3: 96}
 OFFSETS = tuple(sum(CHUNKS[:j]) for j in range(len(CHUNKS)))
 SWAP = [(i, i ^ 1) for i in range(8)]
 Z_GROUPS = [[0, 2, 4, 6], [1, 3, 5, 7]]
 BF = jnp.bfloat16
 F32 = jnp.float32
-VMEM = 56 * 1024 * 1024
-
-
-def params(**more):
-    return pltpu.CompilerParams(vmem_limit_bytes=VMEM, **more)
+
+
+def params(mebibytes):
+    return pltpu.CompilerParams(vmem_limit_bytes=mebibytes * 1024 * 1024)
 
 
 def normalise(wide):
@@ -40,7 +40,7 @@
     return lax.dot_general(a, b, (((0,), (0,)), ((), ())), preferred_element_type=F32)
 
 
-def kv_kernel(x_ref, w_ref, kv_ref, norm_ref):
+def kv_kernel(scalars, x_ref, w_ref, kv_ref, norm_ref):
     @pl.when(pl.program_id(0) == 0)
     def _():
         def step(i, carry):
@@ -53,12 +53,13 @@
     kv_ref[...] = jnp.dot(norm_ref[...], w_ref[...], preferred_element_type=F32).astype(BF)
 
 
-def keys_values(x, w):
+def keys_values(scalars, x, w):
     rows = x.shape[0]
     return pl.pallas_call(
         kv_kernel,
         grid=(4,),
         in_specs=[
+            pl.BlockSpec(memory_space=pltpu.SMEM),
             pl.BlockSpec((rows, WIDTH), lambda j: (0, 0)),
             pl.BlockSpec((WIDTH, 512), lambda j: (0, j + 2)),
         ],
@@ -70,12 +71,12 @@
             jax.ShapeDtypeStruct((rows, 2 * HW), BF),
             jax.ShapeDtypeStruct((rows, WIDTH), BF),
         ],
-        compiler_params=params(),
+        compiler_params=params(24),
         cost_estimate=pl.CostEstimate(
             flops=2 * rows * WIDTH * 2 * HW, bytes_accessed=12_000_000, transcendentals=0
         ),
         name="keys_values",
-    )(x, w)
+    )(scalars, x, w)
 
 
 def q_kernel(norm_ref, w_ref, *q_refs):
@@ -98,7 +99,7 @@
         ],
         out_specs=[pl.BlockSpec((4, 16 * n, 512), lambda j: (0, 0, j)) for n in CHUNKS],
         out_shape=[jax.ShapeDtypeStruct((4, 16 * n, HW), BF) for n in CHUNKS],
-        compiler_params=params(),
+        compiler_params=params(24),
         cost_estimate=pl.CostEstimate(
             flops=2 * rows * WIDTH * HW, bytes_accessed=6_000_000, transcendentals=0
         ),
@@ -106,56 +107,71 @@
     )(norm, w)
 
 
-def spatial_kernel(block, q_ref, ka_ref, kb_ref, va_ref, vb_ref, o_ref, kk, v0, v1):
-    half = ka_ref.shape[0]
-    low_v = lax.broadcasted_iota(jnp.int32, (half, 128), 1) < HD
-    one = jnp.ones((half, 128), BF)
-    for part, (k_ref, v_ref) in enumerate(((ka_ref, va_ref), (kb_ref, vb_ref))):
-        rows = slice(part * half, (part + 1) * half)
-        kk[rows, :] = k_ref[...]
-        v = v_ref[...]
-        v0[rows, :] = jnp.where(low_v, v, one)
-        v1[rows, :] = jnp.where(low_v, one, v)
-    low = lax.broadcasted_iota(jnp.int32, (block, 128), 1) < HD
-    zero = jnp.zeros((block, 128), BF)
-
-    def attend(q, v):
-        s = nt_dot(q, kk[...])
-        p = jnp.exp2(s - jnp.max(s, axis=-1, keepdims=True)).astype(BF)
-        return jnp.dot(p, v[...], preferred_element_type=F32)
-
-    def step(i, carry):
-        rows = pl.ds(pl.multiple_of(i * block, block), block)
-        q = q_ref[rows, :]
-        o0 = attend(jnp.where(low, q, zero), v0)
-        o1 = attend(jnp.where(low, zero, q), v1)
-        top = jnp.where(low, o0, o1)
-        total = pltpu.roll(jnp.where(low, o1, o0), HD, 1)
-        o_ref[rows, :] = (top / total).astype(BF)
+def spatial_kernel(sub, q_ref, ka_ref, kb_ref, va_ref, vb_ref, o_ref, keys, values, s_a, s_b, m_a, m_b):
+    rows, half = q_ref.shape[0], ka_ref.shape[0]
+    count, pairs = rows // sub, H // 2
+    low = lax.broadcasted_iota(jnp.int32, (sub, 128), 1) < HD
+    zero = jnp.zeros((sub, 128), BF)
+    values[:, 128:] = jnp.ones((2 * half, 128), BF)
+
+    def columns(pair):
+        return pl.ds(pl.multiple_of(pair * 128, 128), 128)
+
+    def load(pair, a_ref, b_ref, held):
+        held[:half, :128] = a_ref[:, columns(pair)]
+        held[half:, :128] = b_ref[:, columns(pair)]
+
+    def score(pair, head, i, s_ref, m_ref):
+        part = slice(i * sub, (i + 1) * sub)
+        q = q_ref[part, columns(pair)]
+        q = jnp.where(low, q, zero) if head == 0 else jnp.where(low, zero, q)
+        s = nt_dot(q, keys[...])
+        s_ref[part, :] = s
+        m_ref[part, :] = jnp.broadcast_to(jnp.max(s, axis=-1, keepdims=True), (sub, 128))
+
+    def weigh(i, s_ref, m_ref):
+        part = slice(i * sub, (i + 1) * sub)
+        p = jnp.exp2(s_ref[part, :] - m_ref[part, :1]).astype(BF)
+        o = jnp.dot(p, values[...], preferred_element_type=F32)
+        return o[:, :128] / o[:, 128:]
+
+    load(0, ka_ref, kb_ref, keys)
+    for i in range(count):
+        score(0, 0, i, s_a, m_a)
+
+    def step(pair, carry):
+        load(pair, va_ref, vb_ref, values)
+        first = []
+        for i in range(count):
+            score(pair, 1, i, s_b, m_b)
+            first.append(weigh(i, s_a, m_a))
+        later = jnp.minimum(pair + 1, pairs - 1)
+        load(later, ka_ref, kb_ref, keys)
+        for i in range(count):
+            score(later, 0, i, s_a, m_a)
+            second = weigh(i, s_b, m_b)
+            o_ref[i * sub : (i + 1) * sub, columns(pair)] = jnp.where(low, first[i], second).astype(BF)
         return carry
 
-    lax.fori_loop(0, q_ref.shape[0] // block, step, 0)
-
-
-def spatial_attention(q, kv_a, kv_b, block):
+    lax.fori_loop(0, pairs, step, 0)
+
+
+def spatial_attention(q, kv_a, kv_b, sub):
     rows, half = q.shape[0], kv_a.shape[0]
-    pairs = H // 2
-    return pl.pallas_call(
-        functools.partial(spatial_kernel, block),
-        grid=(pairs,),
-        in_specs=[
-            pl.BlockSpec((rows, 128), lambda h: (0, h)),
-            pl.BlockSpec((half, 128), lambda h: (0, h)),
-            pl.BlockSpec((half, 128), lambda h: (0, h)),
-            pl.BlockSpec((half, 128), lambda h: (0, h + pairs)),
-            pl.BlockSpec((half, 128), lambda h: (0, h + pairs)),
-        ],
-        out_specs=pl.BlockSpec((rows, 128), lambda h: (0, h)),
+    k_spec = pl.BlockSpec((half, HW), lambda i: (0, 0))
+    v_spec = pl.BlockSpec((half, HW), lambda i: (0, 1))
+    return pl.pallas_call(
+        functools.partial(spatial_kernel, sub),
+        grid=(1,),
+        in_specs=[pl.BlockSpec((rows, HW), lambda i: (0, 0)), k_spec, k_spec, v_spec, v_spec],
+        out_specs=pl.BlockSpec((rows, HW), lambda i: (0, 0)),
         out_shape=jax.ShapeDtypeStruct((rows, HW), BF),
-        scratch_shapes=[pltpu.VMEM((2 * half, 128), BF)] * 3,
-        compiler_params=params(),
-        cost_estimate=pl.CostEstimate(
-            flops=16 * rows * half * HW, bytes_accessed=8_000_000, transcendentals=2 * rows * half * H
+        scratch_shapes=[pltpu.VMEM((2 * half, 128), BF), pltpu.VMEM((2 * half, 256), BF)]
+        + [pltpu.VMEM((rows, 2 * half), F32)] * 2
+        + [pltpu.VMEM((rows, 128), F32)] * 2,
+        compiler_params=params(32),
+        cost_estimate=pl.CostEstimate(
+            flops=40 * rows * half * HW, bytes_accessed=8_000_000, transcendentals=2 * rows * half * H
         ),
         name="spatial_attention",
     )(q, kv_a, kv_b, kv_a, kv_b)
@@ -206,7 +222,7 @@
             jax.ShapeDtypeStruct((span, 4, WIDTH), BF),
         ],
         scratch_shapes=[pltpu.VMEM((4, span, WIDTH), BF)],
-        compiler_params=params(),
+        compiler_params=params(24),
         cost_estimate=pl.CostEstimate(
             flops=8 * span * HW * WIDTH, bytes_accessed=8_000_000, transcendentals=0
         ),
@@ -230,15 +246,20 @@
     same = head_row == head_col
     zero = jnp.zeros((256, 256), BF)
     key_valid = lax.broadcasted_iota(jnp.int32, (4, 64, 64), 1) < limit
+    scores, weights = [], []
     for i in range(n):
         rows = slice(64 * i, 64 * i + 64)
         k4 = jnp.where(same, jnp.concatenate([k[rows]] * 4, axis=0), zero)
+        scores.append(nt_dot(k4, q[rows]).reshape(4, 64, 64))
+    for i in range(n):
+        s = jnp.where(key_valid, scores[i], -1e30)
+        p = jnp.exp2(s - jnp.max(s, axis=1, keepdims=True))
+        p = p / jnp.sum(p, axis=1, keepdims=True)
+        weights.append(p.reshape(256, 64).astype(BF))
+    for i in range(n):
+        rows = slice(64 * i, 64 * i + 64)
         v4 = jnp.where(same, jnp.concatenate([v[rows]] * 4, axis=0), zero)
-        s = nt_dot(k4, q[rows]).reshape(4, 64, 64)
-        s = jnp.where(key_valid, s, -1e30)
-        p = jnp.exp2(s - jnp.max(s, axis=1, keepdims=True))
-        p = (p / jnp.sum(p, axis=1, keepdims=True)).reshape(256, 64).astype(BF)
-        o_ref[:, i] = tn_dot(p, v4).astype(BF).reshape(16, 4, 256)
+        o_ref[:, i] = tn_dot(weights[i], v4).astype(BF).reshape(16, 4, 256)
 
 
 def temporal_attention(scalars, x, w, n):
@@ -256,7 +277,7 @@
         out_specs=pl.BlockSpec((TM, n, 4, 256), lambda g: (0, 0, 0, g)),
         out_shape=jax.ShapeDtypeStruct((TM, n, 4, HW), BF),
         scratch_shapes=[pltpu.VMEM((rows, WIDTH), BF)],
-        compiler_params=params(),
+        compiler_params=params(24),
         cost_estimate=pl.CostEstimate(
             flops=2 * rows * WIDTH * 3 * HW, bytes_accessed=14_000_000, transcendentals=0
         ),
@@ -301,7 +322,7 @@
         out_specs=pl.BlockSpec((4, 144, columns), lambda j: (0, 0, j)),
         out_shape=jax.ShapeDtypeStruct((4, 144, WIDTH), BF),
         scratch_shapes=[pltpu.VMEM((4, 144, HW), BF)],
-        compiler_params=params(),
+        compiler_params=params(24),
         cost_estimate=pl.CostEstimate(
             flops=8 * 144 * HW * WIDTH, bytes_accessed=8_000_000, transcendentals=0
         ),
@@ -323,12 +344,12 @@
     first = lax.axis_index("tm") * video.shape[0]
     scalars = jnp.stack([first, frame_count[0]]).astype(jnp.int32)
     frame = over_z(video).reshape(4 * 144, WIDTH)
-    kv_own, norm1 = keys_values(frame, qkv_space)
+    kv_own, norm1 = keys_values(scalars, frame, qkv_space)
     kv_other = lax.ppermute(kv_own, "space", SWAP)
     qs = queries(norm1, qkv_space)
     temporals, middles = [], []
     for n, off, q in zip(CHUNKS, OFFSETS, qs):
-        spatial = spatial_attention(q.reshape(64 * n, HW), kv_own, kv_other, 192 if n % 3 == 0 else 64 * n)
+        spatial = spatial_attention(q.reshape(64 * n, HW), kv_own, kv_other, SUB[n])
         spatial = over_z(spatial.reshape(4, 16 * n, HW))
         middle, send = middle_rows(scalars, spatial, video, out_space, off, n)
         middles.append(middle)

time: 186 us -> 151 us (0.81)
  Pallas kernels: 80.6 us -> 45.6 us
  blocking collectives: 81.4 us -> 70.7 us
  waiting for transfers between devices: 16.1 us -> 24.1 us
  starting transfers between devices: 3.53 us -> 5.47 us
    pallas_call x2, Pallas kernels: 41.5 us -> 23.6 us  [the longest x1 16 us: spatial_attention(): pl.pallas_call(functools.partial(spatial_kernel, sub), grid=(1,), in_spec...]
    pallas_call x1, Pallas kernels: 20.4 us -> 11.2 us  [temporal_attention(): pl.pallas_call(functools.partial(temporal_kernel, n), grid=(4,), in_specs...]
    all_to_all x1, blocking collectives: 28.4 us -> 19.6 us  [over_z(): lax.all_to_all(x, 'space', split_axis=0, concat_axis=0, axis_index_groups...]
    all_to_all x1, waiting for transfers between devices: 16.1 us -> 22.1 us  [over_z(): lax.all_to_all(x, 'space', split_axis=0, concat_axis=0, axis_index_groups...]
    pallas_call x1, Pallas kernels: 7.38 us -> 3.93 us  [middle_rows(): pl.pallas_call(functools.partial(middle_kernel, off, n), in_specs=[pl.Blo...]
    pallas_call x1, Pallas kernels: 5.06 us -> 2.5 us  [queries(): pl.pallas_call(q_kernel, grid=(2,), in_specs=[pl.BlockSpec((rows, WIDTH),...]
    all_to_all x2, blocking collectives: 53 us -> 51 us  [over_tm(): return lax.all_to_all(x, 'tm', split_axis=0, concat_axis=0, tiled=True)]
    ppermute x1, waiting for transfers between devices: 0.01 us -> 1.99 us  [per_device(): kv_other = lax.ppermute(kv_own, 'space', SWAP)]
  transfers between devices with their start and end apart: 2 -> 2, of which waited for: 1 -> 2; matrix products, arithmetic and copies ran while one was open for 0% -> 0% of each run, Pallas kernels for 3% -> 2%
where the time goes in v2:
time: 151 us; the launch traced here: 150 us
  blocking collectives  70.7 us (47%)
  Pallas kernels  45.6 us (30%)
  waiting for transfers between devices  24.1 us (16%)
  starting transfers between devices  5.47 us (4%)
  local copies, waits for them, and re-layouts  3.71 us (2%)
    all_to_all x2, blocking collectives, over_tm(): return lax.all_to_all(x, 'tm', split_axis=0, concat_axis=0, tiled=True)  51 us
    all_to_all x1, waiting for transfers between devices, over_z(): lax.all_to_all(x, 'space', split_axis=0, concat_axis=0, axis_index_groups...  22.1 us
    all_to_all x1, blocking collectives, over_z(): lax.all_to_all(x, 'space', split_axis=0, concat_axis=0, axis_index_groups...  19.6 us
    pallas_call x1, Pallas kernels, spatial_attention(): pl.pallas_call(functools.partial(spatial_kernel, sub), grid=(1,), in_spec...  16 us
    pallas_call x1, Pallas kernels, temporal_attention(): pl.pallas_call(functools.partial(temporal_kernel, n), grid=(4,), in_specs...  11.2 us
    pallas_call x1, Pallas kernels, keys_values(): pl.pallas_call(kv_kernel, grid=(4,), in_specs=[pl.BlockSpec(memory_space=...  7.51 us
    all_to_all x1, starting transfers between devices, over_z(): lax.all_to_all(x, 'space', split_axis=0, concat_axis=0, axis_index_groups...  5.39 us
    pallas_call x1, Pallas kernels, encoded_rows(): pl.pallas_call(encoded_kernel, grid=(WIDTH // columns,), in_specs=[pl.Blo...  4.47 us
  transfers between devices with their start and end apart: 2, of which 2 were waited for; matrix products, arithmetic and copies ran while one was open for 0% of the time, Pallas kernels for 2%

profile of v2, /device:TPU:0, one launch (start us, length us, event | category | flops | bytes accessed | tf_op | source)
XLA Modules:
  0.0 150.4 jit_solution(5900610279032800270)
XLA Ops:
  0.0 5.4 %all-to-all-start = ((bf16[4,144,1536]{2,1,0:T(8,128)(2,1)}), bf16[4,144,1536]{2,1,0:T(8,128)(2,1)S(1)}, u32[]{:S(2)}, u32[]{:S(2)}) async-start(bf16[4,144,1536]{2,1,0:T(8,128)(2,1)} %x_ref.1), calls=%async_computation | async-start | bytes 3538944 | tf_op jit(solution)/shard_map/all_to_all | solution.py:334
  6.0 0.1 pad_add_fusion.scalars
  6.1 22.1 %all-to-all-done = bf16[4,144,1536]{2,1,0:T(8,128)(2,1)S(1)} async-done(((bf16[4,144,1536]{2,1,0:T(8,128)(2,1)}), bf16[4,144,1536]{2,1,0:T(8,128)(2,1)S(1)}, u32[]{:S(2)}, u32[]{:S(2)}) %all-to-all-start) | async-done | bytes 1769504 | tf_op jit(solution)/shard_map/all_to_all | solution.py:334
  28.2 0.0 copy-start
  28.2 3.7 %copy-done = bf16[1536,3072]{1,0:T(8,128)(2,1)S(1)} copy-done((bf16[1536,3072]{1,0:T(8,128)(2,1)S(1)}, bf16[1536,3072]{1,0:T(8,128)(2,1)}, u32[]{:S(2)}) %copy-start) | copy-done | bytes 9437208
  31.9 0.0 copy-start.1
  31.9 7.5 %keys_values.1 = (bf16[576,2048]{1,0:T(8,128)(2,1)S(1)}, bf16[576,1536]{1,0:T(8,128)(2,1)S(1)}) custom-call(s32[2]{0:T(128)S(1)} %pad_add_fusion.scalars, bf16[576,1536]{1,0:T(8,128)(2,1)S(1)} %bitcast.9, bf16[1536,3072]{1,0:T(8,128)(2,1)S(1)} %copy-done), custom_call_target="tpu_custom_call" | custom-call | flops 3623878656 | bytes 12000000 | tf_op jit(solution)/shard_map/keys_values/pallas_call | solution.py:58
  39.4 0.1 collective-permute-start
  39.5 0.0 copy-done.1
  39.5 0.0 slice-start
  39.5 2.5 %queries.1 = bf16[4,144,1024]{2,1,0:T(8,128)(2,1)S(1)} custom-call(bf16[576,1536]{1,0:T(8,128)(2,1)S(1)} %get-tuple-element.9.norm_ref, bf16[1536,3072]{1,0:T(8,128)(2,1)S(1)} %copy-done.1), custom_call_target="tpu_custom_call" | custom-call | flops 1811939328 | bytes 6000000 | tf_op jit(solution)/shard_map/queries/pallas_call | solution.py:93
  42.0 2.0 %collective-permute-done.kb_ref.vb_ref = bf16[576,2048]{1,0:T(8,128)(2,1)S(1)} collective-permute-done((bf16[576,2048]{1,0:T(8,128)(2,1)S(1)}, bf16[576,2048]{1,0:T(8,128)(2,1)S(1)}, u32[]{:S(2)}, u32[]{:S(2)}) %collective-permute-start) | collective-permute-done | bytes 2359328 | tf_op jit(solution)/shard_map/ppermute | solution.py:348
  44.0 0.0 copy-start.4
  44.0 0.0 slice-start.1
  44.0 0.0 slice-start.2
  44.0 16.0 %spatial_attention.1 = bf16[576,1024]{1,0:T(8,128)(2,1)S(1)} custom-call(bf16[576,1024]{1,0:T(8,128)(2,1)S(1)} %bitcast.11, bf16[576,2048]{1,0:T(8,128)(2,1)S(1)} %get-tuple-element.10.ka_ref.va_ref, bf16[576,2048]{1,0:T(8,128)(2,1)S(1)} %collective-permute-done.kb_ref.vb_ref, bf16[576,2048]{1,0:T(8,128)(2,1)S(1)} %get-tuple-element.10.ka_ref.va_ref, ...), custom_call_target="tpu_custom_call" | custom-call | flops 13589544960 | bytes 8000000 | tf_op jit(solution)/shard_map/spatial_attention/pallas_call | solution.py:163
  60.1 0.0 copy-start.3
  60.1 19.6 %all_to_all.20.s_ref = bf16[4,144,1024]{2,1,0:T(8,128)(2,1)S(1)} all-to-all(bf16[4,144,1024]{2,1,0:T(8,128)(2,1)S(1)} %bitcast.12), channel_id=1, replica_groups={{0,2,4,6},{1,3,5,7},{8,10,12,14},{9,11,13,15},{16,18,20,22},{17,19,21,2..., dimensions={0} | all-to-all | bytes 2359296 | tf_op jit(solution)/shard_map/all_to_all | solution.py:334
  79.7 0.0 copy-done.4
  79.7 0.0 copy-done.3
  79.7 3.9 %middle_rows.1 = (bf16[4,144,1536]{2,1,0:T(8,128)(2,1)S(1)}, bf16[144,4,1536]{2,1,0:T(4,128)(2,1)S(1)}) custom-call(s32[2]{0:T(128)S(1)} %pad_add_fusion.scalars, bf16[4,144,1024]{2,1,0:T(8,128)(2,1)S(1)} %all_to_all.20.s_ref, bf16[4,144,1536]{2,1,0:T(8,128)(2,1)S(1)} %copy-done.3, bf16[1024,1536]{1,0:T(8,128)(2,1)S(1)} %copy-done.4), custom_call_target="tpu_custom_call" | custom-call | flops 1811939328 | bytes 8000000 | tf_op jit(solution)/shard_map/middle_rows/pallas_call | solution.py:208
  83.7 31.0 %all_to_all.21.x_ref = bf16[16,9,4,1536]{3,2,1,0:T(4,128)(2,1)S(1)} all-to-all(bf16[16,9,4,1536]{3,2,1,0:T(4,128)(2,1)S(1)} %bitcast.10), channel_id=1, replica_groups=mesh['tm'=16,'space'=8] {'tm'}, dimensions={0} | all-to-all | bytes 3538944 | tf_op jit(solution)/shard_map/all_to_all | solution.py:340
  114.6 0.0 slice-done
  114.7 0.0 slice-done.1
  114.7 0.0 slice-done.2
  114.7 0.0 copy-start.2
  114.7 11.2 %temporal_attention.1 = bf16[16,9,4,1024]{3,2,1,0:T(4,128)(2,1)S(1)} custom-call(s32[2]{0:T(128)S(1)} %pad_add_fusion.scalars, bf16[16,9,4,1536]{3,2,1,0:T(4,128)(2,1)S(1)} %all_to_all.21.x_ref, bf16[1536,3072]{1,0:T(8,128)(2,1)S(1)} %bitcast.7, bf16[1536,3072]{1,0:T(8,128)(2,1)S(1)} %bitcast.7, bf16[1536,3072]{1,0:T(8,128)(2,1)S(1)} %bitcast.7), custom_call_target="tpu_custom_call" | custom-call | flops 5435817984 | bytes 14000000 | tf_op jit(solution)/shard_map/temporal_attention/pallas_call | solution.py:267
  125.9 20.0 %all_to_all.22 = bf16[16,9,4,1024]{3,2,1,0:T(4,128)(2,1)S(1)} all-to-all(bf16[16,9,4,1024]{3,2,1,0:T(4,128)(2,1)S(1)} %temporal_attention.1), channel_id=1, replica_groups=mesh['tm'=16,'space'=8] {'tm'}, dimensions={0} | all-to-all | bytes 2359296 | tf_op jit(solution)/shard_map/all_to_all | solution.py:340
  145.9 0.0 copy-done.2
  145.9 4.5 %encoded_rows.1 = bf16[4,144,1536]{2,1,0:T(8,128)(2,1)} custom-call(s32[2]{0:T(128)S(1)} %pad_add_fusion.scalars, bf16[144,4,1024]{2,1,0:T(4,128)(2,1)S(1)} %bitcast.8, bf16[4,144,1536]{2,1,0:T(8,128)(2,1)S(1)} %get-tuple-element.12.refs_1_, bf16[1024,1536]{1,0:T(8,128)(2,1)S(1)} %copy-done.2), custom_call_target="tpu_custom_call" | custom-call | flops 1811939328 | bytes 8000000 | tf_op jit(solution)/shard_map/encoded_rows/pallas_call | solution.py:315
  (1 shorter events, 0.0 us)
Async XLA Ops:
  0.0 28.2 %all-to-all-start = ((bf16[4,144,1536]{2,1,0:T(8,128)(2,1)}), bf16[4,144,1536]{2,1,0:T(8,128)(2,1)S(1)}, u32[]{:S(2)}, u32[]{:S(2)}) async-start(bf16[4,144,1536]{2,1,0:T(8,128)(2,1)} %x_ref.1), calls=%async_computation | async-start | bytes 3538944 | tf_op jit(solution)/shard_map/all_to_all | solution.py:334
  28.2 3.7 %copy-start = (bf16[1536,3072]{1,0:T(8,128)(2,1)S(1)}, bf16[1536,3072]{1,0:T(8,128)(2,1)}, u32[]{:S(2)}) copy-start(bf16[1536,3072]{1,0:T(8,128)(2,1)} %w_ref.4) | copy-start | bytes 28311556
  31.9 7.6 %copy-start.1 = (bf16[1536,3072]{1,0:T(8,128)(2,1)S(1)}, bf16[1536,3072]{1,0:T(8,128)(2,1)}, u32[]{:S(2)}) copy-start(bf16[1536,3072]{1,0:T(8,128)(2,1)} %w_ref.4) | copy-start | bytes 28311556
  39.4 4.6 %collective-permute-start = (bf16[576,2048]{1,0:T(8,128)(2,1)S(1)}, bf16[576,2048]{1,0:T(8,128)(2,1)S(1)}, u32[]{:S(2)}, u32[]{:S(2)}) collective-permute-start(bf16[576,2048]{1,0:T(8,128)(2,1)S(1)} %get-tuple-element.10.ka_ref.va_ref), channel_id=1, source_target_pairs={{0,1},{1,0},{2,3},{3,2},{4,5},{5,4},{6,7},{7,6},{8,9},{9,8},{10,11... | collective-permute-start | bytes 7077896 | tf_op jit(solution)/shard_map/ppermute | solution.py:348
  39.5 75.1 %slice-start = ((s8[9437184]{0:T(1024)(128)(4,1)}), s8[4194304]{0:T(1024)(128)(4,1)S(1)}, s32[]{:S(2)}) async-start(s8[9437184]{0:T(1024)(128)(4,1)} %bitcast.6), calls=%async_computation.4 | async-start | bytes 8388608
  44.0 35.7 %copy-start.4 = (bf16[1024,1536]{1,0:T(8,128)(2,1)S(1)}, bf16[1024,1536]{1,0:T(8,128)(2,1)}, u32[]{:S(2)}) copy-start(bf16[1024,1536]{1,0:T(8,128)(2,1)} %w_ref.5) | copy-start | bytes 9437188
  44.0 70.6 %slice-start.1 = ((s8[9437184]{0:T(1024)(128)(4,1)}), s8[4194304]{0:T(1024)(128)(4,1)S(1)}, s32[]{:S(2)}) async-start(s8[9437184]{0:T(1024)(128)(4,1)} %bitcast.6), calls=%async_computation.5 | async-start | bytes 8388608
  44.0 70.6 %slice-start.2 = ((s8[9437184]{0:T(1024)(128)(4,1)}), s8[1048576]{0:T(1024)(128)(4,1)S(1)}, s32[]{:S(2)}) async-start(s8[9437184]{0:T(1024)(128)(4,1)} %bitcast.6), calls=%async_computation.6 | async-start | bytes 2097152
  60.1 19.7 %copy-start.3 = (bf16[4,144,1536]{2,1,0:T(8,128)(2,1)S(1)}, bf16[4,144,1536]{2,1,0:T(8,128)(2,1)}, u32[]{:S(2)}) copy-start(bf16[4,144,1536]{2,1,0:T(8,128)(2,1)} %x_ref.1) | copy-start | bytes 5308420
  114.7 31.3 %copy-start.2 = (bf16[1024,1536]{1,0:T(8,128)(2,1)S(1)}, bf16[1024,1536]{1,0:T(8,128)(2,1)}, u32[]{:S(2)}) copy-start(bf16[1024,1536]{1,0:T(8,128)(2,1)} %refs_2_.1) | copy-start | bytes 9437188

commit v3 on v2

--- a/solution.py
+++ b/solution.py
@@ -14,7 +14,6 @@
 TM = 16
 QSCALE = 0.125 * 1.4426950408889634
 CHUNKS = (9,)
-SUB = {9: 144, 5: 160, 4: 128, 3: 96}
 OFFSETS = tuple(sum(CHUNKS[:j]) for j in range(len(CHUNKS)))
 SWAP = [(i, i ^ 1) for i in range(8)]
 Z_GROUPS = [[0, 2, 4, 6], [1, 3, 5, 7]]
@@ -76,16 +75,12 @@
             flops=2 * rows * WIDTH * 2 * HW, bytes_accessed=12_000_000, transcendentals=0
         ),
         name="keys_values",
-    )(scalars, x, w)
-
-
-def q_kernel(norm_ref, w_ref, *q_refs):
+    )(scalars, x, pltpu.with_memory_space_constraint(w, pltpu.HBM))
+
+
+def q_kernel(norm_ref, w_ref, q_ref):
     q = jnp.dot(norm_ref[...], w_ref[...], preferred_element_type=F32) * QSCALE
-    q = q.astype(BF)
-    for n, off, q_ref in zip(CHUNKS, OFFSETS, q_refs):
-        for z in range(4):
-            lo = z * 144 + off * 16
-            q_ref[z] = q[lo : lo + n * 16]
+    q_ref[...] = q.astype(BF)
 
 
 def queries(norm, w):
@@ -97,8 +92,8 @@
             pl.BlockSpec((rows, WIDTH), lambda j: (0, 0)),
             pl.BlockSpec((WIDTH, 512), lambda j: (0, j)),
         ],
-        out_specs=[pl.BlockSpec((4, 16 * n, 512), lambda j: (0, 0, j)) for n in CHUNKS],
-        out_shape=[jax.ShapeDtypeStruct((4, 16 * n, HW), BF) for n in CHUNKS],
+        out_specs=pl.BlockSpec((rows, 512), lambda j: (0, j)),
+        out_shape=jax.ShapeDtypeStruct((rows, HW), BF),
         compiler_params=params(24),
         cost_estimate=pl.CostEstimate(
             flops=2 * rows * WIDTH * HW, bytes_accessed=6_000_000, transcendentals=0
@@ -107,74 +102,75 @@
     )(norm, w)
 
 
-def spatial_kernel(sub, q_ref, ka_ref, kb_ref, va_ref, vb_ref, o_ref, keys, values, s_a, s_b, m_a, m_b):
-    rows, half = q_ref.shape[0], ka_ref.shape[0]
-    count, pairs = rows // sub, H // 2
-    low = lax.broadcasted_iota(jnp.int32, (sub, 128), 1) < HD
-    zero = jnp.zeros((sub, 128), BF)
-    values[:, 128:] = jnp.ones((2 * half, 128), BF)
+def spatial_kernel(distance, scalars, q_ref, a_ref, b_ref, o_ref, keys, values, s_a, s_b, m_a, m_b):
+    half, pairs = a_ref.shape[0], H // 2
+    rows = o_ref.shape[0]
+    own = lax.rem(scalars[2] + distance, 4)
+    low = lax.broadcasted_iota(jnp.int32, (rows, 128), 1) < HD
+    zero = jnp.zeros((rows, 128), BF)
+    for e in range(2):
+        values[e, :, 128:] = jnp.ones((2 * half, 128), BF)
 
     def columns(pair):
         return pl.ds(pl.multiple_of(pair * 128, 128), 128)
 
-    def load(pair, a_ref, b_ref, held):
-        held[:half, :128] = a_ref[:, columns(pair)]
-        held[half:, :128] = b_ref[:, columns(pair)]
-
-    def score(pair, head, i, s_ref, m_ref):
-        part = slice(i * sub, (i + 1) * sub)
-        q = q_ref[part, columns(pair)]
+    def load(pair, held, e):
+        held[e, :half, :128] = a_ref[:, columns(pair)]
+        held[e, half:, :128] = b_ref[:, columns(pair)]
+
+    def score(group, e, head, s_ref, m_ref):
+        q = q_ref[own, :, columns(2 * group + e)]
         q = jnp.where(low, q, zero) if head == 0 else jnp.where(low, zero, q)
-        s = nt_dot(q, keys[...])
-        s_ref[part, :] = s
-        m_ref[part, :] = jnp.broadcast_to(jnp.max(s, axis=-1, keepdims=True), (sub, 128))
-
-    def weigh(i, s_ref, m_ref):
-        part = slice(i * sub, (i + 1) * sub)
-        p = jnp.exp2(s_ref[part, :] - m_ref[part, :1]).astype(BF)
-        o = jnp.dot(p, values[...], preferred_element_type=F32)
+        s = nt_dot(q, keys[e])
+        s_ref[2 * e + head] = s
+        m_ref[2 * e + head] = jnp.broadcast_to(jnp.max(s, axis=-1, keepdims=True), (rows, 128))
+
+    def weigh(e, head, s_ref, m_ref):
+        p = jnp.exp2(s_ref[2 * e + head] - m_ref[2 * e + head, :, :1]).astype(BF)
+        o = jnp.dot(p, values[e], preferred_element_type=F32)
         return o[:, :128] / o[:, 128:]
 
-    load(0, ka_ref, kb_ref, keys)
-    for i in range(count):
-        score(0, 0, i, s_a, m_a)
-
-    def step(pair, carry):
-        load(pair, va_ref, vb_ref, values)
-        first = []
-        for i in range(count):
-            score(pair, 1, i, s_b, m_b)
-            first.append(weigh(i, s_a, m_a))
-        later = jnp.minimum(pair + 1, pairs - 1)
-        load(later, ka_ref, kb_ref, keys)
-        for i in range(count):
-            score(later, 0, i, s_a, m_a)
-            second = weigh(i, s_b, m_b)
-            o_ref[i * sub : (i + 1) * sub, columns(pair)] = jnp.where(low, first[i], second).astype(BF)
+    def phase(group, later, s_now, m_now, s_next, m_next):
+        for e in range(2):
+            load(2 * group + e + pairs, values, e)
+            load(2 * later + e, keys, e)
+        for e in range(2):
+            out = []
+            for head in range(2):
+                score(later, e, head, s_next, m_next)
+                out.append(weigh(e, head, s_now, m_now))
+            o_ref[:, columns(2 * group + e)] = jnp.where(low, out[0], out[1]).astype(BF)
+
+    for e in range(2):
+        load(e, keys, e)
+        for head in range(2):
+            score(0, e, head, s_a, m_a)
+
+    def step(i, carry):
+        phase(2 * i, 2 * i + 1, s_a, m_a, s_b, m_b)
+        phase(2 * i + 1, jnp.minimum(2 * i + 2, pairs // 2 - 1), s_b, m_b, s_a, m_a)
         return carry
 
-    lax.fori_loop(0, pairs, step, 0)
-
-
-def spatial_attention(q, kv_a, kv_b, sub):
-    rows, half = q.shape[0], kv_a.shape[0]
-    k_spec = pl.BlockSpec((half, HW), lambda i: (0, 0))
-    v_spec = pl.BlockSpec((half, HW), lambda i: (0, 1))
-    return pl.pallas_call(
-        functools.partial(spatial_kernel, sub),
-        grid=(1,),
-        in_specs=[pl.BlockSpec((rows, HW), lambda i: (0, 0)), k_spec, k_spec, v_spec, v_spec],
-        out_specs=pl.BlockSpec((rows, HW), lambda i: (0, 0)),
+    lax.fori_loop(0, pairs // 4, step, 0)
+
+
+def spatial_attention(scalars, q, kv_a, kv_b, distance):
+    rows, total = q.shape[1], 2 * kv_a.shape[0]
+    whole = pl.BlockSpec(memory_space=pltpu.VMEM)
+    return pl.pallas_call(
+        functools.partial(spatial_kernel, distance),
+        in_specs=[pl.BlockSpec(memory_space=pltpu.SMEM), whole, whole, whole],
+        out_specs=whole,
         out_shape=jax.ShapeDtypeStruct((rows, HW), BF),
-        scratch_shapes=[pltpu.VMEM((2 * half, 128), BF), pltpu.VMEM((2 * half, 256), BF)]
-        + [pltpu.VMEM((rows, 2 * half), F32)] * 2
-        + [pltpu.VMEM((rows, 128), F32)] * 2,
-        compiler_params=params(32),
-        cost_estimate=pl.CostEstimate(
-            flops=40 * rows * half * HW, bytes_accessed=8_000_000, transcendentals=2 * rows * half * H
+        scratch_shapes=[pltpu.VMEM((2, total, 128), BF), pltpu.VMEM((2, total, 256), BF)]
+        + [pltpu.VMEM((4, rows, total), F32)] * 2
+        + [pltpu.VMEM((4, rows, 128), F32)] * 2,
+        compiler_params=params(24),
+        cost_estimate=pl.CostEstimate(
+            flops=20 * rows * total * HW, bytes_accessed=6_000_000, transcendentals=rows * total * H
         ),
         name="spatial_attention",
-    )(q, kv_a, kv_b, kv_a, kv_b)
+    )(scalars, q, kv_a, kv_b)
 
 
 def reorder(to_patch_major):
@@ -185,49 +181,41 @@
     return (col == (row % 16) * 4 + row // 16).astype(BF)
 
 
-def middle_kernel(off, n, scalars, s_ref, x_ref, w_ref, middle_ref, send_ref, norm):
-    span = 16 * n
-    first, limit = scalars[0], scalars[1]
-    for f in range(4):
+def middle_kernel(scalars, *refs):
+    s_refs, (x_ref, w_ref, middle_ref, send_ref, norm) = refs[:4], refs[4:]
+    first, limit, z = scalars[0], scalars[1], scalars[2]
+    for d in range(4):
+        f = lax.rem(z + 4 - d, 4)
         valid = (first + f < limit).astype(F32)
-        branch = jnp.dot(s_ref[f], w_ref[...], preferred_element_type=F32)
-        x = x_ref[f, off * 16 : off * 16 + span, :].astype(F32)
-        middle = (x + valid * branch).astype(BF)
+        branch = jnp.dot(s_refs[d][...], w_ref[...], preferred_element_type=F32)
+        middle = (x_ref[f].astype(F32) + valid * branch).astype(BF)
         middle_ref[f] = middle
         norm[f] = normalise(middle.astype(F32))
     move = reorder(True)
-    for b in range(n):
+    for b in range(9):
         rows = slice(b * 16, b * 16 + 16)
         block = jnp.concatenate([norm[f, rows, :] for f in range(4)], axis=0)
         moved = jnp.dot(move, block, preferred_element_type=F32).astype(BF)
         send_ref[rows] = moved.reshape(16, 4, WIDTH)
 
 
-def middle_rows(scalars, spatial, video, w, off, n):
-    span = 16 * n
-    return pl.pallas_call(
-        functools.partial(middle_kernel, off, n),
-        in_specs=[
-            pl.BlockSpec(memory_space=pltpu.SMEM),
-            pl.BlockSpec(memory_space=pltpu.VMEM),
-            pl.BlockSpec(memory_space=pltpu.VMEM),
-            pl.BlockSpec(memory_space=pltpu.VMEM),
-        ],
-        out_specs=[
-            pl.BlockSpec(memory_space=pltpu.VMEM),
-            pl.BlockSpec(memory_space=pltpu.VMEM),
-        ],
+def middle_rows(scalars, blocks, video, w):
+    whole = pl.BlockSpec(memory_space=pltpu.VMEM)
+    return pl.pallas_call(
+        middle_kernel,
+        in_specs=[pl.BlockSpec(memory_space=pltpu.SMEM)] + [whole] * 6,
+        out_specs=[whole, whole],
         out_shape=[
-            jax.ShapeDtypeStruct((4, span, WIDTH), BF),
-            jax.ShapeDtypeStruct((span, 4, WIDTH), BF),
-        ],
-        scratch_shapes=[pltpu.VMEM((4, span, WIDTH), BF)],
-        compiler_params=params(24),
-        cost_estimate=pl.CostEstimate(
-            flops=8 * span * HW * WIDTH, bytes_accessed=8_000_000, transcendentals=0
+            jax.ShapeDtypeStruct((4, 144, WIDTH), BF),
+            jax.ShapeDtypeStruct((144, 4, WIDTH), BF),
+        ],
+        scratch_shapes=[pltpu.VMEM((4, 144, WIDTH), BF)],
+        compiler_params=params(24),
+        cost_estimate=pl.CostEstimate(
+            flops=8 * 144 * HW * WIDTH, bytes_accessed=8_000_000, transcendentals=0
         ),
         name="middle_rows",
-    )(scalars, spatial, video, w)
+    )(scalars, *blocks, video, w)
 
 
 def temporal_kernel(n, scalars, x_ref, wq_ref, wk_ref, wv_ref, o_ref, rows_ref):
@@ -330,10 +318,9 @@
     )(scalars, *temporals, *middles, w)
 
 
-def over_z(x):
-    return lax.all_to_all(
-        x, "space", split_axis=0, concat_axis=0, axis_index_groups=Z_GROUPS, tiled=True
-    )
+def along_z(x, distance):
+    pairs = [(i, (i + 2 * distance) % 8) for i in range(8)]
+    return lax.ppermute(x, "space", pairs)
 
 
 def over_tm(x):
@@ -342,21 +329,24 @@
 
 def per_device(video, frame_count, qkv_space, out_space, qkv_time, out_time):
     first = lax.axis_index("tm") * video.shape[0]
-    scalars = jnp.stack([first, frame_count[0]]).astype(jnp.int32)
-    frame = over_z(video).reshape(4 * 144, WIDTH)
-    kv_own, norm1 = keys_values(scalars, frame, qkv_space)
+    z = lax.axis_index("space") // 2
+    scalars = jnp.stack([first, frame_count[0], z]).astype(jnp.int32)
+
+    frame = lax.all_to_all(
+        video, "space", split_axis=0, concat_axis=0, axis_index_groups=Z_GROUPS, tiled=True
+    )
+    kv_own, norm1 = keys_values(scalars, frame.reshape(4 * 144, WIDTH), qkv_space)
     kv_other = lax.ppermute(kv_own, "space", SWAP)
-    qs = queries(norm1, qkv_space)
-    temporals, middles = [], []
-    for n, off, q in zip(CHUNKS, OFFSETS, qs):
-        spatial = spatial_attention(q.reshape(64 * n, HW), kv_own, kv_other, SUB[n])
-        spatial = over_z(spatial.reshape(4, 16 * n, HW))
-        middle, send = middle_rows(scalars, spatial, video, out_space, off, n)
-        middles.append(middle)
-        rows = over_tm(send.reshape(TM, n, 4, WIDTH))
-        temporal = temporal_attention(scalars, rows, qkv_time, n)
-        temporals.append(over_tm(temporal).reshape(16 * n, 4, HW))
-    return encoded_rows(scalars, temporals, middles, out_time)
+    q = queries(norm1, qkv_space).reshape(4, 144, HW)
+    back = {}
+    for d in (2, 1, 3, 0):
+        o = spatial_attention(scalars, q, kv_own, kv_other, d)
+        back[d] = along_z(o, d) if d else o
+    middle, send = middle_rows(scalars, [back[d] for d in range(4)], video, out_space)
+    rows = over_tm(send.reshape(TM, 9, 4, WIDTH))
+    temporal = temporal_attention(scalars, rows, qkv_time, 9)
+    temporal = over_tm(temporal).reshape(144, 4, HW)
+    return encoded_rows(scalars, [temporal], [middle], out_time)
 
 
 def solution(mesh):

time: 151 us -> 141 us (0.934)
  blocking collectives: 70.7 us -> 50 us
  Pallas kernels: 45.6 us -> 53.7 us
  local copies, waits for them, and re-layouts: 3.71 us -> 0.04 us
  starting transfers between devices: 5.47 us -> 9.12 us
  waiting for transfers between devices: 24.1 us -> 26.3 us
    all_to_all x1 -> x0, blocking collectives: 19.6 us -> none  [over_z(): lax.all_to_all(x, 'space', split_axis=0, concat_axis=0, axis_index_groups...]
    pallas_call x2 -> x5, Pallas kernels: 20 us -> 27 us  [the longest x4 22.7 us: spatial_attention(): pl.pallas_call(functools.partial(spatial_kernel, distance), in_specs=[pl....]
    unnamed x16 -> x14, local copies, waits for them, and re-layouts: 3.71 us -> 0.04 us
    ppermute x0 -> x3, starting transfers between devices: none -> 3.65 us  [along_z(): return lax.ppermute(x, 'space', pairs)]
    ppermute x0 -> x3, waiting for transfers between devices: none -> 2.25 us  [along_z(): return lax.ppermute(x, 'space', pairs)]
  transfers between devices with their start and end apart: 2 -> 5, of which waited for: 2 -> 3; matrix products, arithmetic and copies ran while one was open for 0% -> 0% of each run, Pallas kernels for 2% -> 14%
where the time goes in v3:
time: 141 us; the launch traced here: 140 us
  Pallas kernels  53.7 us (38%)
  blocking collectives  50 us (35%)
  waiting for transfers between devices  26.3 us (19%)
  starting transfers between devices  9.12 us (6%)
    all_to_all x2, blocking collectives, over_tm(): return lax.all_to_all(x, 'tm', split_axis=0, concat_axis=0, tiled=True)  50 us
    pallas_call x4, Pallas kernels, spatial_attention(): pl.pallas_call(functools.partial(spatial_kernel, distance), in_specs=[pl....  22.7 us
    all_to_all x1, waiting for transfers between devices, per_device(): lax.all_to_all(video, 'space', split_axis=0, concat_axis=0, axis_index_gr...  22.1 us
    pallas_call x1, Pallas kernels, temporal_attention(): pl.pallas_call(functools.partial(temporal_kernel, n), grid=(4,), in_specs...  11.2 us
    pallas_call x1, Pallas kernels, keys_values(): pl.pallas_call(kv_kernel, grid=(4,), in_specs=[pl.BlockSpec(memory_space=...  8.57 us
    all_to_all x1, starting transfers between devices, per_device(): lax.all_to_all(video, 'space', split_axis=0, concat_axis=0, axis_index_gr...  5.39 us
    pallas_call x1, Pallas kernels, encoded_rows(): pl.pallas_call(encoded_kernel, grid=(WIDTH // columns,), in_specs=[pl.Blo...  4.47 us
    pallas_call x1, Pallas kernels, middle_rows(): pl.pallas_call(middle_kernel, in_specs=[pl.BlockSpec(memory_space=pltpu.S...  4.32 us
  transfers between devices with their start and end apart: 5, of which 3 were waited for; matrix products, arithmetic and copies ran while one was open for 0% of the time, Pallas kernels for 14%

profile of v3, /device:TPU:0, one launch (start us, length us, event | category | flops | bytes accessed | tf_op | source)
XLA Modules:
  0.0 140.1 jit_solution(16885654232794641376)
XLA Ops:
  0.0 5.4 %all-to-all-start = ((bf16[4,144,1536]{2,1,0:T(8,128)(2,1)}), bf16[4,144,1536]{2,1,0:T(8,128)(2,1)S(1)}, u32[]{:S(2)}, u32[]{:S(2)}) async-start(bf16[4,144,1536]{2,1,0:T(8,128)(2,1)} %refs_4_.1), calls=%async_computation | async-start | bytes 3538944 | tf_op jit(solution)/shard_map/all_to_all | solution.py:335
  6.0 0.1 pad_add_fusion.scalars
  6.1 22.1 %all-to-all-done = bf16[4,144,1536]{2,1,0:T(8,128)(2,1)S(1)} async-done(((bf16[4,144,1536]{2,1,0:T(8,128)(2,1)}), bf16[4,144,1536]{2,1,0:T(8,128)(2,1)S(1)}, u32[]{:S(2)}, u32[]{:S(2)}) %all-to-all-start) | async-done | bytes 1769504 | tf_op jit(solution)/shard_map/all_to_all | solution.py:335
  28.2 0.0 copy-start
  28.2 8.6 %keys_values.1 = (bf16[576,2048]{1,0:T(8,128)(2,1)S(1)}, bf16[576,1536]{1,0:T(8,128)(2,1)S(1)}) custom-call(s32[3]{0:T(128)S(1)} %pad_add_fusion.scalars, bf16[576,1536]{1,0:T(8,128)(2,1)S(1)} %bitcast.9, bf16[1536,3072]{1,0:T(8,128)(2,1)} %w_ref.3), custom_call_target="tpu_custom_call" | custom-call | flops 3623878656 | bytes 12000000 | tf_op jit(solution)/shard_map/keys_values/pallas_call | solution.py:57
  36.8 0.1 collective-permute-start
  36.9 0.0 copy-done
  36.9 2.5 %queries.1 = bf16[576,1024]{1,0:T(8,128)(2,1)S(1)} custom-call(bf16[576,1536]{1,0:T(8,128)(2,1)S(1)} %get-tuple-element.9.norm_ref, bf16[1536,3072]{1,0:T(8,128)(2,1)S(1)} %copy-done), custom_call_target="tpu_custom_call" | custom-call | flops 1811939328 | bytes 6000000 | tf_op jit(solution)/shard_map/queries/pallas_call | solution.py:88
  39.4 2.0 %collective-permute-done.b_ref = bf16[576,2048]{1,0:T(8,128)(2,1)S(1)} collective-permute-done((bf16[576,2048]{1,0:T(8,128)(2,1)S(1)}, bf16[576,2048]{1,0:T(8,128)(2,1)S(1)}, u32[]{:S(2)}, u32[]{:S(2)}) %collective-permute-start) | collective-permute-done | bytes 2359328 | tf_op jit(solution)/shard_map/ppermute | solution.py:339
  41.4 5.7 %spatial_attention.5 = bf16[144,1024]{1,0:T(8,128)(2,1)S(1)} custom-call(s32[3]{0:T(128)S(1)} %pad_add_fusion.scalars, bf16[4,144,1024]{2,1,0:T(8,128)(2,1)S(1)} %bitcast.11, bf16[576,2048]{1,0:T(8,128)(2,1)S(1)} %get-tuple-element.10.a_ref, bf16[576,2048]{1,0:T(8,128)(2,1)S(1)} %collective-permute-done.b_ref), custom_call_target="tpu_custom_call" | custom-call | flops 3397386240 | bytes 6000000 | tf_op jit(solution)/shard_map/spatial_attention/pallas_call | solution.py:160
  47.1 0.6 collective-permute-start.1
  47.7 5.7 %spatial_attention.6 = bf16[144,1024]{1,0:T(8,128)(2,1)S(1)} custom-call(s32[3]{0:T(128)S(1)} %pad_add_fusion.scalars, bf16[4,144,1024]{2,1,0:T(8,128)(2,1)S(1)} %bitcast.12, bf16[576,2048]{1,0:T(8,128)(2,1)S(1)} %get-tuple-element.10.a_ref, bf16[576,2048]{1,0:T(8,128)(2,1)S(1)} %collective-permute-done.b_ref), custom_call_target="tpu_custom_call" | custom-call | flops 3397386240 | bytes 6000000 | tf_op jit(solution)/shard_map/spatial_attention/pallas_call | solution.py:160
  53.4 2.1 %collective-permute-start.2 = (bf16[144,1024]{1,0:T(8,128)(2,1)S(1)}, bf16[144,1024]{1,0:T(8,128)(2,1)S(1)}, u32[]{:S(2)}, u32[]{:S(2)}) collective-permute-start(bf16[144,1024]{1,0:T(8,128)(2,1)S(1)} %spatial_attention.6), channel_id=1, source_target_pairs={{0,4},{1,5},{2,6},{3,7},{4,0},{5,1},{6,2},{7,3},{8,12},{9,13},{10,... | collective-permute-start | bytes 884744 | tf_op jit(solution)/shard_map/ppermute | solution.py:323
  55.5 5.7 %spatial_attention.7 = bf16[144,1024]{1,0:T(8,128)(2,1)S(1)} custom-call(s32[3]{0:T(128)S(1)} %pad_add_fusion.scalars, bf16[4,144,1024]{2,1,0:T(8,128)(2,1)S(1)} %bitcast.13, bf16[576,2048]{1,0:T(8,128)(2,1)S(1)} %get-tuple-element.10.a_ref, bf16[576,2048]{1,0:T(8,128)(2,1)S(1)} %collective-permute-done.b_ref), custom_call_target="tpu_custom_call" | custom-call | flops 3397386240 | bytes 6000000 | tf_op jit(solution)/shard_map/spatial_attention/pallas_call | solution.py:160
  61.2 0.0 copy-start.2
  61.2 0.0 copy-start.3
  61.2 0.9 collective-permute-start.3
  62.1 0.0 slice-start
  62.1 0.0 slice-start.1
  62.1 5.7 %spatial_attention.4.refs_0_ = bf16[144,1024]{1,0:T(8,128)(2,1)S(1)} custom-call(s32[3]{0:T(128)S(1)} %pad_add_fusion.scalars, bf16[4,144,1024]{2,1,0:T(8,128)(2,1)S(1)} %bitcast.14, bf16[576,2048]{1,0:T(8,128)(2,1)S(1)} %get-tuple-element.10.a_ref, bf16[576,2048]{1,0:T(8,128)(2,1)S(1)} %collective-permute-done.b_ref), custom_call_target="tpu_custom_call" | custom-call | flops 3397386240 | bytes 6000000 | tf_op jit(solution)/shard_map/spatial_attention/pallas_call | solution.py:160
  67.8 0.0 slice-start.2
  67.8 0.0 collective-permute-done.1.refs_1_
  67.8 0.0 collective-permute-done.2.refs_2_
  67.8 2.2 %collective-permute-done.3.refs_3_ = bf16[144,1024]{1,0:T(8,128)(2,1)S(1)} collective-permute-done((bf16[144,1024]{1,0:T(8,128)(2,1)S(1)}, bf16[144,1024]{1,0:T(8,128)(2,1)S(1)}, u32[]{:S(2)}, u32[]{:S(2)}) %collective-permute-start.3) | collective-permute-done | bytes 294944 | tf_op jit(solution)/shard_map/ppermute | solution.py:323
  70.0 0.0 copy-done.2
  70.1 0.0 copy-done.3
  70.1 4.3 %middle_rows.1 = (bf16[4,144,1536]{2,1,0:T(8,128)(2,1)S(1)}, bf16[144,4,1536]{2,1,0:T(4,128)(2,1)S(1)}) custom-call(s32[3]{0:T(128)S(1)} %pad_add_fusion.scalars, bf16[144,1024]{1,0:T(8,128)(2,1)S(1)} %spatial_attention.4.refs_0_, bf16[144,1024]{1,0:T(8,128)(2,1)S(1)} %collective-permute-done.1.refs_1_, ...), custom_call_target="tpu_custom_call" | custom-call | flops 1811939328 | bytes 8000000 | tf_op jit(solution)/shard_map/middle_rows/pallas_call | solution.py:204
  74.4 30.4 %all_to_all.15.x_ref = bf16[16,9,4,1536]{3,2,1,0:T(4,128)(2,1)S(1)} all-to-all(bf16[16,9,4,1536]{3,2,1,0:T(4,128)(2,1)S(1)} %bitcast.10), channel_id=1, replica_groups=mesh['tm'=16,'space'=8] {'tm'}, dimensions={0} | all-to-all | bytes 3538944 | tf_op jit(solution)/shard_map/all_to_all | solution.py:327
  104.8 0.0 slice-done
  104.8 0.0 slice-done.1
  104.8 0.0 slice-done.2
  104.8 0.0 copy-start.1
  104.8 11.2 %temporal_attention.1 = bf16[16,9,4,1024]{3,2,1,0:T(4,128)(2,1)S(1)} custom-call(s32[3]{0:T(128)S(1)} %pad_add_fusion.scalars, bf16[16,9,4,1536]{3,2,1,0:T(4,128)(2,1)S(1)} %all_to_all.15.x_ref, bf16[1536,3072]{1,0:T(8,128)(2,1)S(1)} %bitcast.7, bf16[1536,3072]{1,0:T(8,128)(2,1)S(1)} %bitcast.7, bf16[1536,3072]{1,0:T(8,128)(2,1)S(1)} %bitcast.7), custom_call_target="tpu_custom_call" | custom-call | flops 5435817984 | bytes 14000000 | tf_op jit(solution)/shard_map/temporal_attention/pallas_call | solution.py:255
  116.0 19.6 %all_to_all.16 = bf16[16,9,4,1024]{3,2,1,0:T(4,128)(2,1)S(1)} all-to-all(bf16[16,9,4,1024]{3,2,1,0:T(4,128)(2,1)S(1)} %temporal_attention.1), channel_id=1, replica_groups=mesh['tm'=16,'space'=8] {'tm'}, dimensions={0} | all-to-all | bytes 2359296 | tf_op jit(solution)/shard_map/all_to_all | solution.py:327
  135.6 0.0 copy-done.1
  135.6 4.5 %encoded_rows.1 = bf16[4,144,1536]{2,1,0:T(8,128)(2,1)} custom-call(s32[3]{0:T(128)S(1)} %pad_add_fusion.scalars, bf16[144,4,1024]{2,1,0:T(4,128)(2,1)S(1)} %bitcast.8, bf16[4,144,1536]{2,1,0:T(8,128)(2,1)S(1)} %get-tuple-element.12.refs_1_, bf16[1024,1536]{1,0:T(8,128)(2,1)S(1)} %copy-done.1), custom_call_target="tpu_custom_call" | custom-call | flops 1811939328 | bytes 8000000 | tf_op jit(solution)/shard_map/encoded_rows/pallas_call | solution.py:303
  (1 shorter events, 0.0 us)
Async XLA Ops:
  0.0 28.2 %all-to-all-start = ((bf16[4,144,1536]{2,1,0:T(8,128)(2,1)}), bf16[4,144,1536]{2,1,0:T(8,128)(2,1)S(1)}, u32[]{:S(2)}, u32[]{:S(2)}) async-start(bf16[4,144,1536]{2,1,0:T(8,128)(2,1)} %refs_4_.1), calls=%async_computation | async-start | bytes 3538944 | tf_op jit(solution)/shard_map/all_to_all | solution.py:335
  28.2 8.7 %copy-start = (bf16[1536,3072]{1,0:T(8,128)(2,1)S(1)}, bf16[1536,3072]{1,0:T(8,128)(2,1)}, u32[]{:S(2)}) copy-start(bf16[1536,3072]{1,0:T(8,128)(2,1)} %w_ref.3) | copy-start | bytes 28311556
  36.8 4.6 %collective-permute-start = (bf16[576,2048]{1,0:T(8,128)(2,1)S(1)}, bf16[576,2048]{1,0:T(8,128)(2,1)S(1)}, u32[]{:S(2)}, u32[]{:S(2)}) collective-permute-start(bf16[576,2048]{1,0:T(8,128)(2,1)S(1)} %get-tuple-element.10.a_ref), channel_id=1, source_target_pairs={{0,1},{1,0},{2,3},{3,2},{4,5},{5,4},{6,7},{7,6},{8,9},{9,8},{10,11... | collective-permute-start | bytes 7077896 | tf_op jit(solution)/shard_map/ppermute | solution.py:339
  47.1 20.7 %collective-permute-start.1 = (bf16[144,1024]{1,0:T(8,128)(2,1)S(1)}, bf16[144,1024]{1,0:T(8,128)(2,1)S(1)}, u32[]{:S(2)}, u32[]{:S(2)}) collective-permute-start(bf16[144,1024]{1,0:T(8,128)(2,1)S(1)} %spatial_attention.5), channel_id=1, source_target_pairs={{0,2},{1,3},{2,4},{3,5},{4,6},{5,7},{6,0},{7,1},{8,10},{9,11},{10,... | collective-permute-start | bytes 884744 | tf_op jit(solution)/shard_map/ppermute | solution.py:323
  53.4 14.4 %collective-permute-start.2 = (bf16[144,1024]{1,0:T(8,128)(2,1)S(1)}, bf16[144,1024]{1,0:T(8,128)(2,1)S(1)}, u32[]{:S(2)}, u32[]{:S(2)}) collective-permute-start(bf16[144,1024]{1,0:T(8,128)(2,1)S(1)} %spatial_attention.6), channel_id=1, source_target_pairs={{0,4},{1,5},{2,6},{3,7},{4,0},{5,1},{6,2},{7,3},{8,12},{9,13},{10,... | collective-permute-start | bytes 884744 | tf_op jit(solution)/shard_map/ppermute | solution.py:323
  61.2 8.9 %copy-start.2 = (bf16[4,144,1536]{2,1,0:T(8,128)(2,1)S(1)}, bf16[4,144,1536]{2,1,0:T(8,128)(2,1)}, u32[]{:S(2)}) copy-start(bf16[4,144,1536]{2,1,0:T(8,128)(2,1)} %refs_4_.1) | copy-start | bytes 5308420
  61.2 8.9 %copy-start.3 = (bf16[1024,1536]{1,0:T(8,128)(2,1)S(1)}, bf16[1024,1536]{1,0:T(8,128)(2,1)}, u32[]{:S(2)}) copy-start(bf16[1024,1536]{1,0:T(8,128)(2,1)} %refs_5_.1) | copy-start | bytes 9437188
  61.2 8.8 %collective-permute-start.3 = (bf16[144,1024]{1,0:T(8,128)(2,1)S(1)}, bf16[144,1024]{1,0:T(8,128)(2,1)S(1)}, u32[]{:S(2)}, u32[]{:S(2)}) collective-permute-start(bf16[144,1024]{1,0:T(8,128)(2,1)S(1)} %spatial_attention.7), channel_id=1, source_target_pairs={{0,6},{1,7},{2,0},{3,1},{4,2},{5,3},{6,4},{7,5},{8,14},{9,15},{10,... | collective-permute-start | bytes 884744 | tf_op jit(solution)/shard_map/ppermute | solution.py:323
  62.1 42.7 %slice-start = ((s8[9437184]{0:T(1024)(128)(4,1)}), s8[4194304]{0:T(1024)(128)(4,1)S(1)}, s32[]{:S(2)}) async-start(s8[9437184]{0:T(1024)(128)(4,1)} %bitcast.6), calls=%async_computation.3 | async-start | bytes 8388608
  62.1 42.7 %slice-start.1 = ((s8[9437184]{0:T(1024)(128)(4,1)}), s8[4194304]{0:T(1024)(128)(4,1)S(1)}, s32[]{:S(2)}) async-start(s8[9437184]{0:T(1024)(128)(4,1)} %bitcast.6), calls=%async_computation.4 | async-start | bytes 8388608
  67.8 37.0 %slice-start.2 = ((s8[9437184]{0:T(1024)(128)(4,1)}), s8[1048576]{0:T(1024)(128)(4,1)S(1)}, s32[]{:S(2)}) async-start(s8[9437184]{0:T(1024)(128)(4,1)} %bitcast.6), calls=%async_computation.5 | async-start | bytes 2097152
  104.8 30.8 %copy-start.1 = (bf16[1024,1536]{1,0:T(8,128)(2,1)S(1)}, bf16[1024,1536]{1,0:T(8,128)(2,1)}, u32[]{:S(2)}) copy-start(bf16[1024,1536]{1,0:T(8,128)(2,1)} %refs_2_.1) | copy-start | bytes 9437188

commit v4 on v3

v4 whole, which is shorter than its diff:
```python
import functools

import jax
import jax.numpy as jnp
from jax import lax
from jax.experimental import pallas as pl
from jax.experimental.pallas import tpu as pltpu
from jax.sharding import PartitionSpec as P

H = 16
HD = 64
WIDTH = 1536
HW = H * HD
TM = 16
QSCALE = 0.125 * 1.4426950408889634
CALLS = ((2,), (1, 3), (0,))
SWAP = [(i, i ^ 1) for i in range(8)]
Z_GROUPS = [[0, 2, 4, 6], [1, 3, 5, 7]]
BF = jnp.bfloat16
F32 = jnp.float32


def params(mebibytes):
    return pltpu.CompilerParams(vmem_limit_bytes=mebibytes * 1024 * 1024)


def normalise(wide):
    center = wide - jnp.mean(wide, axis=-1, keepdims=True)
    spread = jnp.mean(center * center, axis=-1, keepdims=True)
    return (center * lax.rsqrt(spread + 1e-06)).astype(BF)


def nt_dot(a, b):
    return lax.dot_general(a, b, (((1,), (1,)), ((), ())), preferred_element_type=F32)


def tn_dot(a, b):
    return lax.dot_general(a, b, (((0,), (0,)), ((), ())), preferred_element_type=F32)


def kv_kernel(scalars, x_ref, w_ref, kv_ref, norm_ref, wq_ref, wkv, sem):
    def fetch(j):
        cols = pl.ds(pl.multiple_of(j * 512, 128), 512)
        source = pl.ds(pl.multiple_of(j * 512 + HW, 128), 512)
        return pltpu.make_async_copy(w_ref.at[:, source], wkv.at[:, cols], sem.at[j])

    for j in range(4):
        fetch(j).start()
    for_queries = pltpu.make_async_copy(w_ref.at[:, :HW], wq_ref, sem.at[4])
    for_queries.start()

    def norm(i, carry):
        rows = pl.ds(pl.multiple_of(i * 96, 96), 96)
        norm_ref[rows, :] = normalise(x_ref[rows, :].astype(F32))
        return carry

    lax.fori_loop(0, x_ref.shape[0] // 96, norm, 0)

    def step(j, carry):
        fetch(j).wait()
        cols = pl.ds(pl.multiple_of(j * 512, 128), 512)
        y = jnp.dot(norm_ref[...], wkv[:, cols], preferred_element_type=F32)
        kv_ref[:, cols] = y.astype(BF)
        return carry

    lax.fori_loop(0, 4, step, 0)
    for_queries.wait()


def keys_values(scalars, x, w):
    rows = x.shape[0]
    whole = pl.BlockSpec(memory_space=pltpu.VMEM)
    return pl.pallas_call(
        kv_kernel,
        in_specs=[
            pl.BlockSpec(memory_space=pltpu.SMEM),
            whole,
            pl.BlockSpec(memory_space=pltpu.HBM),
        ],
        out_specs=[whole, whole, whole],
        out_shape=[
            jax.ShapeDtypeStruct((rows, 2 * HW), BF),
            jax.ShapeDtypeStruct((rows, WIDTH), BF),
            jax.ShapeDtypeStruct((WIDTH, HW), BF),
        ],
        scratch_shapes=[pltpu.VMEM((WIDTH, 2 * HW), BF), pltpu.SemaphoreType.DMA((5,))],
        compiler_params=params(24),
        cost_estimate=pl.CostEstimate(
            flops=2 * rows * WIDTH * 2 * HW, bytes_accessed=12_000_000, transcendentals=0
        ),
        name="keys_values",
    )(scalars, x, pltpu.with_memory_space_constraint(w, pltpu.HBM))


def q_kernel(norm_ref, w_ref, q_ref):
    def step(j, carry):
        cols = pl.ds(pl.multiple_of(j * 512, 128), 512)
        y = jnp.dot(norm_ref[...], w_ref[:, cols], preferred_element_type=F32)
        q_ref[:, cols] = (y * QSCALE).astype(BF)
        return carry

    lax.fori_loop(0, 2, step, 0)


def queries(norm, w):
    rows = norm.shape[0]
    whole = pl.BlockSpec(memory_space=pltpu.VMEM)
    return pl.pallas_call(
        q_kernel,
        in_specs=[whole, whole],
        out_specs=whole,
        out_shape=jax.ShapeDtypeStruct((rows, HW), BF),
        compiler_params=params(16),
        cost_estimate=pl.CostEstimate(
            flops=2 * rows * WIDTH * HW, bytes_accessed=6_000_000, transcendentals=0
        ),
        name="queries",
    )(norm, w)


def spatial_kernel(distances, scalars, q_ref, a_ref, b_ref, *refs):
    count = len(distances)
    o_refs, (keys, values, s_a, s_b, m_a, m_b) = refs[:count], refs[count:]
    half, pairs, rows = a_ref.shape[0], H // 2, o_refs[0].shape[0]
    width = keys.shape[0]
    groups = pairs // width
    owners = [lax.rem(scalars[2] + d, 4) for d in distances]
    low = lax.broadcasted_iota(jnp.int32, (rows, 128), 1) < HD
    zero = jnp.zeros((rows, 128), BF)
    for e in range(width):
        values[e, :, 128:] = jnp.ones((2 * half, 128), BF)

    def columns(pair):
        if isinstance(pair, int):
            return slice(pair * 128, pair * 128 + 128)
        return pl.ds(pl.multiple_of(pair * 128, 128), 128)

    def load(pair, held, e):
        held[e, :half, :128] = a_ref[:, columns(pair)]
        held[e, half:, :128] = b_ref[:, columns(pair)]

    def score(group, e, c, head, s_ref, m_ref):
        slot = (e * count + c) * 2 + head
        q = q_ref[owners[c], :, columns(width * group + e)]
        q = jnp.where(low, q, zero) if head == 0 else jnp.where(low, zero, q)
        s = nt_dot(q, keys[e])
        s_ref[slot] = s
        m_ref[slot] = jnp.broadcast_to(jnp.max(s, axis=-1, keepdims=True), (rows, 128))

    def weigh(e, c, head, s_ref, m_ref):
        slot = (e * count + c) * 2 + head
        p = jnp.exp2(s_ref[slot] - m_ref[slot, :, :1]).astype(BF)
        o = jnp.dot(p, values[e], preferred_element_type=F32)
        return o[:, :128] / o[:, 128:]

    def phase(group, later, now, after):
        for e in range(width):
            load(width * group + e + pairs, values, e)
            if later is not None:
                load(width * later + e, keys, e)
        for e in range(width):
            for c in range(count):
                out = []
                for head in range(2):
                    if later is not None:
                        score(later, e, c, head, *after)
                    out.append(weigh(e, c, head, *now))
                o_refs[c][:, columns(width * group + e)] = jnp.where(low, out[0], out[1]).astype(BF)

    first, second = (s_a, m_a), (s_b, m_b)
    for e in range(width):
        load(e, keys, e)
        for c in range(count):
            for head in range(2):
                score(0, e, c, head, *first)

    def step(i, carry):
        phase(2 * i, 2 * i + 1, first, second)
        phase(2 * i + 1, 2 * i + 2, second, first)
        return carry

    lax.fori_loop(0, groups // 2 - 1, step, 0)
    phase(groups - 2, groups - 1, first, second)
    phase(groups - 1, None, second, first)


def spatial_attention(scalars, q, kv_a, kv_b, distances):
    rows, total, count = q.shape[1], 2 * kv_a.shape[0], len(distances)
    width = 4 // count
    heads = 2 * width * count
    whole = pl.BlockSpec(memory_space=pltpu.VMEM)
    return pl.pallas_call(
        functools.partial(spatial_kernel, distances),
        in_specs=[pl.BlockSpec(memory_space=pltpu.SMEM), whole, whole, whole],
        out_specs=[whole] * count,
        out_shape=[jax.ShapeDtypeStruct((rows, HW), BF)] * count,
        scratch_shapes=[pltpu.VMEM((width, total, 128), BF), pltpu.VMEM((width, total, 256), BF)]
        + [pltpu.VMEM((heads, rows, total), F32)] * 2
        + [pltpu.VMEM((heads, rows, 128), F32)] * 2,
        compiler_params=params(24),
        cost_estimate=pl.CostEstimate(
            flops=20 * count * rows * total * HW,
            bytes_accessed=6_000_000,
            transcendentals=count * rows * total * H,
        ),
        name="spatial_attention",
    )(scalars, q, kv_a, kv_b)


def reorder(to_patch_major):
    row = lax.broadcasted_iota(jnp.int32, (64, 64), 0)
    col = lax.broadcasted_iota(jnp.int32, (64, 64), 1)
    if to_patch_major:
        return (col == (row % 4) * 16 + row // 4).astype(BF)
    return (col == (row % 16) * 4 + row // 16).astype(BF)


def middle_kernel(scalars, *refs):
    s_refs, (x_ref, w_ref, middle_ref, send_ref, norm) = refs[:4], refs[4:]
    first, limit, z = scalars[0], scalars[1], scalars[2]
    for d in range(4):
        f = lax.rem(z + 4 - d, 4)
        valid = (first + f < limit).astype(F32)
        branch = jnp.dot(s_refs[d][...], w_ref[...], preferred_element_type=F32)
        middle = (x_ref[f].astype(F32) + valid * branch).astype(BF)
        middle_ref[f] = middle
        norm[f] = normalise(middle.astype(F32))
    move = reorder(True)
    for b in range(9):
        rows = slice(b * 16, b * 16 + 16)
        block = jnp.concatenate([norm[f, rows, :] for f in range(4)], axis=0)
        moved = jnp.dot(move, block, preferred_element_type=F32).astype(BF)
        send_ref[rows] = moved.reshape(16, 4, WIDTH)


def middle_rows(scalars, blocks, video, w):
    whole = pl.BlockSpec(memory_space=pltpu.VMEM)
    return pl.pallas_call(
        middle_kernel,
        in_specs=[pl.BlockSpec(memory_space=pltpu.SMEM)] + [whole] * 6,
        out_specs=[whole, whole],
        out_shape=[
            jax.ShapeDtypeStruct((4, 144, WIDTH), BF),
            jax.ShapeDtypeStruct((144, 4, WIDTH), BF),
        ],
        scratch_shapes=[pltpu.VMEM((4, 144, WIDTH), BF)],
        compiler_params=params(24),
        cost_estimate=pl.CostEstimate(
            flops=8 * 144 * HW * WIDTH, bytes_accessed=8_000_000, transcendentals=0
        ),
        name="middle_rows",
    )(scalars, *blocks, video, w)


def temporal_kernel(n, scalars, x_ref, w_ref, o_ref, rows_ref):
    for i in range(n):
        rows_ref[64 * i : 64 * i + 64, :] = x_ref[:, i].reshape(64, WIDTH)
    limit = scalars[1]
    head_row = lax.broadcasted_iota(jnp.int32, (256, 256), 0) // HD
    head_col = lax.broadcasted_iota(jnp.int32, (256, 256), 1) // HD
    same = head_row == head_col
    zero = jnp.zeros((256, 256), BF)
    key_valid = lax.broadcasted_iota(jnp.int32, (4, 64, 64), 1) < limit

    def step(g, carry):
        def project(part):
            cols = pl.ds(pl.multiple_of(part * HW + g * 256, 128), 256)
            return jnp.dot(rows_ref[...], w_ref[:, cols], preferred_element_type=F32)

        q = (project(0) * QSCALE).astype(BF)
        k = project(1).astype(BF)
        v = project(2).astype(BF)
        scores, weights = [], []
        for i in range(n):
            rows = slice(64 * i, 64 * i + 64)
            k4 = jnp.where(same, jnp.concatenate([k[rows]] * 4, axis=0), zero)
            scores.append(nt_dot(k4, q[rows]).reshape(4, 64, 64))
        for i in range(n):
            s = jnp.where(key_valid, scores[i], -1e30)
            p = jnp.exp2(s - jnp.max(s, axis=1, keepdims=True))
            p = p / jnp.sum(p, axis=1, keepdims=True)
            weights.append(p.reshape(256, 64).astype(BF))
        cols = pl.ds(pl.multiple_of(g * 256, 128), 256)
        for i in range(n):
            rows = slice(64 * i, 64 * i + 64)
            v4 = jnp.where(same, jnp.concatenate([v[rows]] * 4, axis=0), zero)
            o_ref[:, i, :, cols] = tn_dot(weights[i], v4).astype(BF).reshape(16, 4, 256)
        return carry

    lax.fori_loop(0, 4, step, 0)


def temporal_attention(scalars, x, w, n):
    rows = 64 * n
    whole = pl.BlockSpec(memory_space=pltpu.VMEM)
    return pl.pallas_call(
        functools.partial(temporal_kernel, n),
        in_specs=[pl.BlockSpec(memory_space=pltpu.SMEM), whole, whole],
        out_specs=whole,
        out_shape=jax.ShapeDtypeStruct((TM, n, 4, HW), BF),
        scratch_shapes=[pltpu.VMEM((rows, WIDTH), BF)],
        compiler_params=params(24),
        cost_estimate=pl.CostEstimate(
            flops=2 * rows * WIDTH * 3 * HW, bytes_accessed=14_000_000, transcendentals=0
        ),
        name="temporal_attention",
    )(scalars, x, w)


def encoded_kernel(scalars, t_ref, m_ref, w_ref, o_ref, rows_ref, held, sem):
    move = reorder(False)
    for b in range(9):
        block = t_ref[b * 16 : b * 16 + 16].reshape(64, HW)
        moved = jnp.dot(move, block, preferred_element_type=F32).astype(BF)
        for f in range(4):
            lo = f * 144 + b * 16
            rows_ref[lo : lo + 16, :] = moved[f * 16 : f * 16 + 16]
    first, limit = scalars[0], scalars[1]

    def leave(j):
        cols = pl.ds(pl.multiple_of(j * 512, 128), 512)
        return pltpu.make_async_copy(held.at[:, :, cols], o_ref.at[:, :, cols], sem.at[j])

    def project(j, carry):
        cols = pl.ds(pl.multiple_of(j * 512, 128), 512)
        branch = jnp.dot(rows_ref[...], w_ref[:, cols], preferred_element_type=F32)
        for f in range(4):
            valid = (first + f < limit).astype(F32)
            own = branch[f * 144 : (f + 1) * 144]
            held[f, :, cols] = (m_ref[f, :, cols].astype(F32) + valid * own).astype(BF)
        leave(j).start()
        return carry

    lax.fori_loop(0, 3, project, 0)
    for j in range(3):
        leave(j).wait()


def encoded_rows(scalars, temporal, middle, w):
    whole = pl.BlockSpec(memory_space=pltpu.VMEM)
    return pl.pallas_call(
        encoded_kernel,
        in_specs=[pl.BlockSpec(memory_space=pltpu.SMEM), whole, whole, whole],
        out_specs=pl.BlockSpec(memory_space=pltpu.HBM),
        out_shape=jax.ShapeDtypeStruct((4, 144, WIDTH), BF),
        scratch_shapes=[
            pltpu.VMEM((4 * 144, HW), BF),
            pltpu.VMEM((4, 144, WIDTH), BF),
            pltpu.SemaphoreType.DMA((3,)),
        ],
        compiler_params=params(24),
        cost_estimate=pl.CostEstimate(
            flops=8 * 144 * HW * WIDTH, bytes_accessed=8_000_000, transcendentals=0
        ),
        name="encoded_rows",
    )(scalars, temporal, middle, w)


def along_z(x, distance):
    pairs = [(i, (i + 2 * distance) % 8) for i in range(8)]
    return lax.ppermute(x, "space", pairs)


def over_tm(x):
    return lax.all_to_all(x, "tm", split_axis=0, concat_axis=0, tiled=True)


def per_device(video, frame_count, qkv_space, out_space, qkv_time, out_time):
    first = lax.axis_index("tm") * video.shape[0]
    z = lax.axis_index("space") // 2
    scalars = jnp.stack([first, frame_count[0], z]).astype(jnp.int32)

    frame = lax.all_to_all(
        video, "space", split_axis=0, concat_axis=0, axis_index_groups=Z_GROUPS, tiled=True
    )
    kv_own, norm1, w_q = keys_values(scalars, frame.reshape(4 * 144, WIDTH), qkv_space)
    kv_other = lax.ppermute(kv_own, "space", SWAP)
    q = queries(norm1, w_q).reshape(4, 144, HW)
    back = {}
    for distances in CALLS:
        results = spatial_attention(scalars, q, kv_own, kv_other, distances)
        for d, o in zip(distances, results):
            back[d] = along_z(o, d) if d else o
    middle, send = middle_rows(scalars, [back[d] for d in range(4)], video, out_space)
    rows = over_tm(send.reshape(TM, 9, 4, WIDTH))
    temporal = temporal_attention(scalars, rows, qkv_time, 9)
    temporal = over_tm(temporal).reshape(144, 4, HW)
    return encoded_rows(scalars, temporal, middle, out_time)


def solution(mesh):
    return jax.shard_map(
        per_device,
        mesh=mesh,
        in_specs=(P("tm", "space", None), P(), P(), P(), P(), P()),
        out_specs=P("tm", "space", None),
        check_vma=False,
    )
```

time: 141 us -> 134 us (0.950)
  Pallas kernels: 53.7 us -> 44.5 us
  waiting for transfers between devices: 26.3 us -> 29.7 us
    pallas_call x8 -> x7, Pallas kernels: 49.4 us -> 40.3 us  [the longest x3 17.4 us: spatial_attention(): pl.pallas_call(functools.partial(spatial_kernel, distances), in_specs=[pl...]
    ppermute x3, waiting for transfers between devices: 2.25 us -> 5.22 us  [along_z(): return lax.ppermute(x, 'space', pairs)]
  transfers between devices with their start and end apart: 5 -> 5, of which waited for: 3 -> 4; matrix products, arithmetic and copies ran while one was open for 0% -> 0% of each run, Pallas kernels for 14% -> 9%
where the time goes in v4:
time: 134 us
  blocking collectives  49.9 us (37%)
  Pallas kernels  44.5 us (33%)
  waiting for transfers between devices  29.7 us (22%)
  starting transfers between devices  8.87 us (7%)
    all_to_all x2, blocking collectives, over_tm(): return lax.all_to_all(x, 'tm', split_axis=0, concat_axis=0, tiled=True)  49.9 us
    all_to_all x1, waiting for transfers between devices, per_device(): lax.all_to_all(video, 'space', split_axis=0, concat_axis=0, axis_index_gr...  22.1 us
    pallas_call x3, Pallas kernels, spatial_attention(): pl.pallas_call(functools.partial(spatial_kernel, distances), in_specs=[pl...  17.4 us
    pallas_call x1, Pallas kernels, temporal_attention(): pl.pallas_call(functools.partial(temporal_kernel, n), in_specs=[pl.BlockS...  10.1 us
    pallas_call x1, Pallas kernels, keys_values(): pl.pallas_call(kv_kernel, in_specs=[pl.BlockSpec(memory_space=pltpu.SMEM)...  6.53 us
    all_to_all x1, starting transfers between devices, per_device(): lax.all_to_all(video, 'space', split_axis=0, concat_axis=0, axis_index_gr...  5.39 us
    ppermute x3, waiting for transfers between devices, along_z(): return lax.ppermute(x, 'space', pairs)  5.22 us
    pallas_call x1, Pallas kernels, encoded_rows(): pl.pallas_call(encoded_kernel, in_specs=[pl.BlockSpec(memory_space=pltpu....  4.18 us
  transfers between devices with their start and end apart: 5, of which 4 were waited for; matrix products, arithmetic and copies ran while one was open for 0% of the time, Pallas kernels for 9%

profile of v4, /device:TPU:0, one launch (start us, length us, event | category | flops | bytes accessed | tf_op | source)
XLA Modules:
  0.0 134.0 jit_solution(16115368799268535113)
XLA Ops:
  0.0 5.4 %all-to-all-start = ((bf16[4,144,1536]{2,1,0:T(8,128)(2,1)}), bf16[4,144,1536]{2,1,0:T(8,128)(2,1)S(1)}, u32[]{:S(2)}, u32[]{:S(2)}) async-start(bf16[4,144,1536]{2,1,0:T(8,128)(2,1)} %refs_4_.1), calls=%async_computation | async-start | bytes 3538944 | tf_op jit(solution)/shard_map/all_to_all | solution.py:373
  6.0 0.1 pad_add_fusion.scalars
  6.1 22.1 %all-to-all-done = bf16[4,144,1536]{2,1,0:T(8,128)(2,1)S(1)} async-done(((bf16[4,144,1536]{2,1,0:T(8,128)(2,1)}), bf16[4,144,1536]{2,1,0:T(8,128)(2,1)S(1)}, u32[]{:S(2)}, u32[]{:S(2)}) %all-to-all-start) | async-done | bytes 1769504 | tf_op jit(solution)/shard_map/all_to_all | solution.py:373
  28.2 6.5 %keys_values.1 = (bf16[576,2048]{1,0:T(8,128)(2,1)S(1)}, bf16[576,1536]{1,0:T(8,128)(2,1)S(1)}, bf16[1536,1024]{1,0:T(8,128)(2,1)S(1)}) custom-call(s32[3]{0:T(128)S(1)} %pad_add_fusion.scalars, bf16[576,1536]{1,0:T(8,128)(2,1)S(1)} %bitcast.7, bf16[1536,3072]{1,0:T(8,128)(2,1)} %w_ref.3), custom_call_target="tpu_custom_call" | custom-call | flops 3623878656 | bytes 12000000 | tf_op jit(solution)/shard_map/keys_values/pallas_call | solution.py:73
  34.7 0.1 collective-permute-start
  34.8 2.2 %queries.1 = bf16[576,1024]{1,0:T(8,128)(2,1)S(1)} custom-call(bf16[576,1536]{1,0:T(8,128)(2,1)S(1)} %get-tuple-element.12.norm_ref, bf16[1536,1024]{1,0:T(8,128)(2,1)S(1)} %get-tuple-element.13.w_ref), custom_call_target="tpu_custom_call" | custom-call | flops 1811939328 | bytes 6000000 | tf_op jit(solution)/shard_map/queries/pallas_call | solution.py:108
  37.0 2.3 %collective-permute-done.b_ref = bf16[576,2048]{1,0:T(8,128)(2,1)S(1)} collective-permute-done((bf16[576,2048]{1,0:T(8,128)(2,1)S(1)}, bf16[576,2048]{1,0:T(8,128)(2,1)S(1)}, u32[]{:S(2)}, u32[]{:S(2)}) %collective-permute-start) | collective-permute-done | bytes 2359328 | tf_op jit(solution)/shard_map/ppermute | solution.py:377
  39.4 8.0 %spatial_attention.4 = (bf16[144,1024]{1,0:T(8,128)(2,1)S(1)}, bf16[144,1024]{1,0:T(8,128)(2,1)S(1)}) custom-call(s32[3]{0:T(128)S(1)} %pad_add_fusion.scalars, bf16[4,144,1024]{2,1,0:T(8,128)(2,1)S(1)} %bitcast.11, bf16[576,2048]{1,0:T(8,128)(2,1)S(1)} %get-tuple-element.14.a_ref, bf16[576,2048]{1,0:T(8,128)(2,1)S(1)} %collective-permute-done.b_ref), custom_call_target="tpu_custom_call" | custom-call | flops 6794772480 | bytes 6000000 | tf_op jit(solution)/shard_map/spatial_attention/pallas_call | solution.py:192
  47.4 0.6 collective-permute-start.1
  48.0 2.7 %collective-permute-start.3 = (bf16[144,1024]{1,0:T(8,128)(2,1)S(1)}, bf16[144,1024]{1,0:T(8,128)(2,1)S(1)}, u32[]{:S(2)}, u32[]{:S(2)}) collective-permute-start(bf16[144,1024]{1,0:T(8,128)(2,1)S(1)} %get-tuple-element.16), channel_id=1, source_target_pairs={{0,6},{1,7},{2,0},{3,1},{4,2},{5,3},{6,4},{7,5},{8,14},{9,15},{10,... | collective-permute-start | bytes 884744 | tf_op jit(solution)/shard_map/ppermute | solution.py:361
  50.7 4.7 %spatial_attention.5 = bf16[144,1024]{1,0:T(8,128)(2,1)S(1)} custom-call(s32[3]{0:T(128)S(1)} %pad_add_fusion.scalars, bf16[4,144,1024]{2,1,0:T(8,128)(2,1)S(1)} %bitcast.12, bf16[576,2048]{1,0:T(8,128)(2,1)S(1)} %get-tuple-element.14.a_ref, bf16[576,2048]{1,0:T(8,128)(2,1)S(1)} %collective-permute-done.b_ref), custom_call_target="tpu_custom_call" | custom-call | flops 3397386240 | bytes 6000000 | tf_op jit(solution)/shard_map/spatial_attention/pallas_call | solution.py:192
  55.4 0.0 copy-start.1
  55.4 0.0 copy-start.2
  55.4 0.1 collective-permute-start.2
  55.5 0.0 slice-start
  55.5 0.0 slice-start.1
  55.5 4.7 %spatial_attention.3.refs_0_ = bf16[144,1024]{1,0:T(8,128)(2,1)S(1)} custom-call(s32[3]{0:T(128)S(1)} %pad_add_fusion.scalars, bf16[4,144,1024]{2,1,0:T(8,128)(2,1)S(1)} %bitcast.13, bf16[576,2048]{1,0:T(8,128)(2,1)S(1)} %get-tuple-element.14.a_ref, bf16[576,2048]{1,0:T(8,128)(2,1)S(1)} %collective-permute-done.b_ref), custom_call_target="tpu_custom_call" | custom-call | flops 3397386240 | bytes 6000000 | tf_op jit(solution)/shard_map/spatial_attention/pallas_call | solution.py:192
  60.2 0.0 slice-start.2
  60.2 0.0 collective-permute-done.1.refs_1_
  60.3 3.1 %collective-permute-done.3.refs_3_ = bf16[144,1024]{1,0:T(8,128)(2,1)S(1)} collective-permute-done((bf16[144,1024]{1,0:T(8,128)(2,1)S(1)}, bf16[144,1024]{1,0:T(8,128)(2,1)S(1)}, u32[]{:S(2)}, u32[]{:S(2)}) %collective-permute-start.3) | collective-permute-done | bytes 294944 | tf_op jit(solution)/shard_map/ppermute | solution.py:361
  63.3 2.1 %collective-permute-done.2.refs_2_ = bf16[144,1024]{1,0:T(8,128)(2,1)S(1)} collective-permute-done((bf16[144,1024]{1,0:T(8,128)(2,1)S(1)}, bf16[144,1024]{1,0:T(8,128)(2,1)S(1)}, u32[]{:S(2)}, u32[]{:S(2)}) %collective-permute-start.2) | collective-permute-done | bytes 294944 | tf_op jit(solution)/shard_map/ppermute | solution.py:361
  65.5 0.0 copy-done.1
  65.5 0.0 copy-done.2
  65.5 4.2 %middle_rows.1 = (bf16[4,144,1536]{2,1,0:T(8,128)(2,1)S(1)}, bf16[144,4,1536]{2,1,0:T(4,128)(2,1)S(1)}) custom-call(s32[3]{0:T(128)S(1)} %pad_add_fusion.scalars, bf16[144,1024]{1,0:T(8,128)(2,1)S(1)} %spatial_attention.3.refs_0_, bf16[144,1024]{1,0:T(8,128)(2,1)S(1)} %collective-permute-done.1.refs_1_, ...), custom_call_target="tpu_custom_call" | custom-call | flops 1811939328 | bytes 8000000 | tf_op jit(solution)/shard_map/middle_rows/pallas_call | solution.py:238
  69.7 30.4 %all_to_all.15.x_ref = bf16[16,9,4,1536]{3,2,1,0:T(4,128)(2,1)S(1)} all-to-all(bf16[16,9,4,1536]{3,2,1,0:T(4,128)(2,1)S(1)} %bitcast.8), channel_id=1, replica_groups=mesh['tm'=16,'space'=8] {'tm'}, dimensions={0} | all-to-all | bytes 3538944 | tf_op jit(solution)/shard_map/all_to_all | solution.py:365
  100.0 0.0 slice-done
  100.0 0.0 slice-done.1
  100.0 0.0 slice-done.2
  100.0 0.0 copy-start
  100.1 10.1 %temporal_attention.1 = bf16[16,9,4,1024]{3,2,1,0:T(4,128)(2,1)S(1)} custom-call(s32[3]{0:T(128)S(1)} %pad_add_fusion.scalars, bf16[16,9,4,1536]{3,2,1,0:T(4,128)(2,1)S(1)} %all_to_all.15.x_ref, bf16[1536,3072]{1,0:T(8,128)(2,1)S(1)} %bitcast.10), custom_call_target="tpu_custom_call" | custom-call | flops 5435817984 | bytes 14000000 | tf_op jit(solution)/shard_map/temporal_attention/pallas_call | solution.py:296
  110.1 19.5 %all_to_all.16 = bf16[16,9,4,1024]{3,2,1,0:T(4,128)(2,1)S(1)} all-to-all(bf16[16,9,4,1024]{3,2,1,0:T(4,128)(2,1)S(1)} %temporal_attention.1), channel_id=1, replica_groups=mesh['tm'=16,'space'=8] {'tm'}, dimensions={0} | all-to-all | bytes 2359296 | tf_op jit(solution)/shard_map/all_to_all | solution.py:365
  129.7 0.0 copy-done
  129.7 4.2 %encoded_rows.1 = bf16[4,144,1536]{2,1,0:T(8,128)(2,1)} custom-call(s32[3]{0:T(128)S(1)} %pad_add_fusion.scalars, bf16[144,4,1024]{2,1,0:T(4,128)(2,1)S(1)} %bitcast.6, bf16[4,144,1536]{2,1,0:T(8,128)(2,1)S(1)} %get-tuple-element.18.m_ref, bf16[1024,1536]{1,0:T(8,128)(2,1)S(1)} %copy-done), custom_call_target="tpu_custom_call" | custom-call | flops 1811939328 | bytes 8000000 | tf_op jit(solution)/shard_map/encoded_rows/pallas_call | solution.py:341
  (1 shorter events, 0.0 us)
Async XLA Ops:
  0.0 28.2 %all-to-all-start = ((bf16[4,144,1536]{2,1,0:T(8,128)(2,1)}), bf16[4,144,1536]{2,1,0:T(8,128)(2,1)S(1)}, u32[]{:S(2)}, u32[]{:S(2)}) async-start(bf16[4,144,1536]{2,1,0:T(8,128)(2,1)} %refs_4_.1), calls=%async_computation | async-start | bytes 3538944 | tf_op jit(solution)/shard_map/all_to_all | solution.py:373
  34.7 4.6 %collective-permute-start = (bf16[576,2048]{1,0:T(8,128)(2,1)S(1)}, bf16[576,2048]{1,0:T(8,128)(2,1)S(1)}, u32[]{:S(2)}, u32[]{:S(2)}) collective-permute-start(bf16[576,2048]{1,0:T(8,128)(2,1)S(1)} %get-tuple-element.14.a_ref), channel_id=1, source_target_pairs={{0,1},{1,0},{2,3},{3,2},{4,5},{5,4},{6,7},{7,6},{8,9},{9,8},{10,11... | collective-permute-start | bytes 7077896 | tf_op jit(solution)/shard_map/ppermute | solution.py:377
  47.4 12.9 %collective-permute-start.1 = (bf16[144,1024]{1,0:T(8,128)(2,1)S(1)}, bf16[144,1024]{1,0:T(8,128)(2,1)S(1)}, u32[]{:S(2)}, u32[]{:S(2)}) collective-permute-start(bf16[144,1024]{1,0:T(8,128)(2,1)S(1)} %get-tuple-element.15), channel_id=1, source_target_pairs={{0,2},{1,3},{2,4},{3,5},{4,6},{5,7},{6,0},{7,1},{8,10},{9,11},{10,... | collective-permute-start | bytes 884744 | tf_op jit(solution)/shard_map/ppermute | solution.py:361
  48.0 15.3 %collective-permute-start.3 = (bf16[144,1024]{1,0:T(8,128)(2,1)S(1)}, bf16[144,1024]{1,0:T(8,128)(2,1)S(1)}, u32[]{:S(2)}, u32[]{:S(2)}) collective-permute-start(bf16[144,1024]{1,0:T(8,128)(2,1)S(1)} %get-tuple-element.16), channel_id=1, source_target_pairs={{0,6},{1,7},{2,0},{3,1},{4,2},{5,3},{6,4},{7,5},{8,14},{9,15},{10,... | collective-permute-start | bytes 884744 | tf_op jit(solution)/shard_map/ppermute | solution.py:361
  55.4 10.1 %copy-start.1 = (bf16[4,144,1536]{2,1,0:T(8,128)(2,1)S(1)}, bf16[4,144,1536]{2,1,0:T(8,128)(2,1)}, u32[]{:S(2)}) copy-start(bf16[4,144,1536]{2,1,0:T(8,128)(2,1)} %refs_4_.1) | copy-start | bytes 5308420
  55.4 10.1 %copy-start.2 = (bf16[1024,1536]{1,0:T(8,128)(2,1)S(1)}, bf16[1024,1536]{1,0:T(8,128)(2,1)}, u32[]{:S(2)}) copy-start(bf16[1024,1536]{1,0:T(8,128)(2,1)} %refs_5_.1) | copy-start | bytes 9437188
  55.4 10.1 %collective-permute-start.2 = (bf16[144,1024]{1,0:T(8,128)(2,1)S(1)}, bf16[144,1024]{1,0:T(8,128)(2,1)S(1)}, u32[]{:S(2)}, u32[]{:S(2)}) collective-permute-start(bf16[144,1024]{1,0:T(8,128)(2,1)S(1)} %spatial_attention.5), channel_id=1, source_target_pairs={{0,4},{1,5},{2,6},{3,7},{4,0},{5,1},{6,2},{7,3},{8,12},{9,13},{10,... | collective-permute-start | bytes 884744 | tf_op jit(solution)/shard_map/ppermute | solution.py:361
  55.5 44.5 %slice-start = ((s8[9437184]{0:T(1024)(128)(4,1)}), s8[4194304]{0:T(1024)(128)(4,1)S(1)}, s32[]{:S(2)}) async-start(s8[9437184]{0:T(1024)(128)(4,1)} %bitcast.9), calls=%async_computation.3 | async-start | bytes 8388608
  55.5 44.5 %slice-start.1 = ((s8[9437184]{0:T(1024)(128)(4,1)}), s8[4194304]{0:T(1024)(128)(4,1)S(1)}, s32[]{:S(2)}) async-start(s8[9437184]{0:T(1024)(128)(4,1)} %bitcast.9), calls=%async_computation.4 | async-start | bytes 8388608
  60.2 39.8 %slice-start.2 = ((s8[9437184]{0:T(1024)(128)(4,1)}), s8[1048576]{0:T(1024)(128)(4,1)S(1)}, s32[]{:S(2)}) async-start(s8[9437184]{0:T(1024)(128)(4,1)} %bitcast.9), calls=%async_computation.5 | async-start | bytes 2097152
  100.0 29.6 %copy-start = (bf16[1024,1536]{1,0:T(8,128)(2,1)S(1)}, bf16[1024,1536]{1,0:T(8,128)(2,1)}, u32[]{:S(2)}) copy-start(bf16[1024,1536]{1,0:T(8,128)(2,1)} %w_ref.5) | copy-start | bytes 9437188

commit v5 on v4

--- a/solution.py
+++ b/solution.py
@@ -13,7 +13,8 @@
 HW = H * HD
 TM = 16
 QSCALE = 0.125 * 1.4426950408889634
-CALLS = ((2,), (1, 3), (0,))
+CALLS = ((1, 3), (2,))
+LATE = 2
 SWAP = [(i, i ^ 1) for i in range(8)]
 Z_GROUPS = [[0, 2, 4, 6], [1, 3, 5, 7]]
 BF = jnp.bfloat16
@@ -38,29 +39,98 @@
     return lax.dot_general(a, b, (((0,), (0,)), ((), ())), preferred_element_type=F32)
 
 
+def block(j):
+    return pl.ds(pl.multiple_of(j * 512, 128), 512)
+
+
+def own_kernel(scalars, video_ref, w_ref, kv_ref, q_ref, x_ref, norm_ref, held, sem):
+    mine = pltpu.make_async_copy(video_ref.at[scalars[2]], x_ref, sem.at[6])
+    mine.start()
+
+    def fetch(j):
+        return pltpu.make_async_copy(w_ref.at[:, block(j)], held.at[:, block(j)], sem.at[j])
+
+    for j in (2, 3, 4, 5, 0, 1):
+        fetch(j).start()
+    mine.wait()
+
+    def norm(i, carry):
+        rows = pl.ds(pl.multiple_of(i * 48, 48), 48)
+        norm_ref[rows, :] = normalise(x_ref[rows, :].astype(F32))
+        return carry
+
+    lax.fori_loop(0, 3, norm, 0)
+
+    def key_value(j, carry):
+        fetch(j).wait()
+        y = jnp.dot(norm_ref[...], held[:, block(j)], preferred_element_type=F32)
+        kv_ref[:, block(j - 2)] = y.astype(BF)
+        return carry
+
+    def query(j, carry):
+        fetch(j).wait()
+        y = jnp.dot(norm_ref[...], held[:, block(j)], preferred_element_type=F32)
+        q_ref[0, :, block(j)] = (y * QSCALE).astype(BF)
+        return carry
+
+    lax.fori_loop(2, 6, key_value, 0)
+    lax.fori_loop(0, 2, query, 0)
+
+
+def own_block(scalars, video, w):
+    rows = video.shape[1]
+    whole = pl.BlockSpec(memory_space=pltpu.VMEM)
+    far = pl.BlockSpec(memory_space=pltpu.HBM)
+    return pl.pallas_call(
+        own_kernel,
+        in_specs=[pl.BlockSpec(memory_space=pltpu.SMEM), far, far],
+        out_specs=[whole, whole],
+        out_shape=[
+            jax.ShapeDtypeStruct((rows, 2 * HW), BF),
+            jax.ShapeDtypeStruct((1, rows, HW), BF),
+        ],
+        scratch_shapes=[
+            pltpu.VMEM((rows, WIDTH), BF),
+            pltpu.VMEM((rows, WIDTH), BF),
+            pltpu.VMEM((WIDTH, 3 * HW), BF),
+            pltpu.SemaphoreType.DMA((7,)),
+        ],
+        compiler_params=params(24),
+        cost_estimate=pl.CostEstimate(
+            flops=2 * rows * WIDTH * 3 * HW, bytes_accessed=12_000_000, transcendentals=0
+        ),
+        name="own_block",
+    )(
+        scalars,
+        pltpu.with_memory_space_constraint(video, pltpu.HBM),
+        pltpu.with_memory_space_constraint(w, pltpu.HBM),
+    )
+
+
 def kv_kernel(scalars, x_ref, w_ref, kv_ref, norm_ref, wq_ref, wkv, sem):
     def fetch(j):
-        cols = pl.ds(pl.multiple_of(j * 512, 128), 512)
         source = pl.ds(pl.multiple_of(j * 512 + HW, 128), 512)
-        return pltpu.make_async_copy(w_ref.at[:, source], wkv.at[:, cols], sem.at[j])
+        return pltpu.make_async_copy(w_ref.at[:, source], wkv.at[:, block(j)], sem.at[j])
 
     for j in range(4):
         fetch(j).start()
     for_queries = pltpu.make_async_copy(w_ref.at[:, :HW], wq_ref, sem.at[4])
     for_queries.start()
-
-    def norm(i, carry):
-        rows = pl.ds(pl.multiple_of(i * 96, 96), 96)
-        norm_ref[rows, :] = normalise(x_ref[rows, :].astype(F32))
-        return carry
-
-    lax.fori_loop(0, x_ref.shape[0] // 96, norm, 0)
+    for d in range(1, 4):
+        other = lax.rem(scalars[2] + d, 4)
+
+        def norm(i, carry):
+            lo = pl.multiple_of(i * 48, 48)
+            wide = x_ref[other, pl.ds(lo, 48), :].astype(F32)
+            norm_ref[pl.ds((d - 1) * 144 + lo, 48), :] = normalise(wide)
+            return carry
+
+        lax.fori_loop(0, 3, norm, 0, unroll=True)
 
     def step(j, carry):
         fetch(j).wait()
-        cols = pl.ds(pl.multiple_of(j * 512, 128), 512)
-        y = jnp.dot(norm_ref[...], wkv[:, cols], preferred_element_type=F32)
-        kv_ref[:, cols] = y.astype(BF)
+        y = jnp.dot(norm_ref[...], wkv[:, block(j)], preferred_element_type=F32)
+        kv_ref[:, block(j)] = y.astype(BF)
         return carry
 
     lax.fori_loop(0, 4, step, 0)
@@ -68,7 +138,7 @@
 
 
 def keys_values(scalars, x, w):
-    rows = x.shape[0]
+    rows = 3 * x.shape[1]
     whole = pl.BlockSpec(memory_space=pltpu.VMEM)
     return pl.pallas_call(
         kv_kernel,
@@ -94,9 +164,10 @@
 
 def q_kernel(norm_ref, w_ref, q_ref):
     def step(j, carry):
-        cols = pl.ds(pl.multiple_of(j * 512, 128), 512)
-        y = jnp.dot(norm_ref[...], w_ref[:, cols], preferred_element_type=F32)
-        q_ref[:, cols] = (y * QSCALE).astype(BF)
+        y = jnp.dot(norm_ref[...], w_ref[:, block(j)], preferred_element_type=F32)
+        q = (y * QSCALE).astype(BF)
+        for d in range(3):
+            q_ref[d, :, block(j)] = q[d * 144 : (d + 1) * 144]
         return carry
 
     lax.fori_loop(0, 2, step, 0)
@@ -109,7 +180,7 @@
         q_kernel,
         in_specs=[whole, whole],
         out_specs=whole,
-        out_shape=jax.ShapeDtypeStruct((rows, HW), BF),
+        out_shape=jax.ShapeDtypeStruct((3, 144, HW), BF),
         compiler_params=params(16),
         cost_estimate=pl.CostEstimate(
             flops=2 * rows * WIDTH * HW, bytes_accessed=6_000_000, transcendentals=0
@@ -118,17 +189,17 @@
     )(norm, w)
 
 
-def spatial_kernel(distances, scalars, q_ref, a_ref, b_ref, *refs):
-    count = len(distances)
-    o_refs, (keys, values, s_a, s_b, m_a, m_b) = refs[:count], refs[count:]
-    half, pairs, rows = a_ref.shape[0], H // 2, o_refs[0].shape[0]
+def spatial_kernel(which, q_ref, *refs):
+    count = len(which)
+    kv_refs, o_refs = refs[: -count - 6], refs[-count - 6 : -6]
+    keys, values, s_a, s_b, m_a, m_b = refs[-6:]
+    pairs, rows = H // 2, o_refs[0].shape[0]
     width = keys.shape[0]
     groups = pairs // width
-    owners = [lax.rem(scalars[2] + d, 4) for d in distances]
     low = lax.broadcasted_iota(jnp.int32, (rows, 128), 1) < HD
     zero = jnp.zeros((rows, 128), BF)
     for e in range(width):
-        values[e, :, 128:] = jnp.ones((2 * half, 128), BF)
+        values[e, :, 128:] = jnp.ones((values.shape[1], 128), BF)
 
     def columns(pair):
         if isinstance(pair, int):
@@ -136,12 +207,14 @@
         return pl.ds(pl.multiple_of(pair * 128, 128), 128)
 
     def load(pair, held, e):
-        held[e, :half, :128] = a_ref[:, columns(pair)]
-        held[e, half:, :128] = b_ref[:, columns(pair)]
+        lo = 0
+        for ref in kv_refs:
+            held[e, lo : lo + ref.shape[0], :128] = ref[:, columns(pair)]
+            lo += ref.shape[0]
 
     def score(group, e, c, head, s_ref, m_ref):
         slot = (e * count + c) * 2 + head
-        q = q_ref[owners[c], :, columns(width * group + e)]
+        q = q_ref[which[c], :, columns(width * group + e)]
         q = jnp.where(low, q, zero) if head == 0 else jnp.where(low, zero, q)
         s = nt_dot(q, keys[e])
         s_ref[slot] = s
@@ -184,14 +257,14 @@
     phase(groups - 1, None, second, first)
 
 
-def spatial_attention(scalars, q, kv_a, kv_b, distances):
-    rows, total, count = q.shape[1], 2 * kv_a.shape[0], len(distances)
+def spatial_attention(q, kvs, which):
+    rows, total, count = q.shape[1], sum(kv.shape[0] for kv in kvs), len(which)
     width = 4 // count
     heads = 2 * width * count
     whole = pl.BlockSpec(memory_space=pltpu.VMEM)
     return pl.pallas_call(
-        functools.partial(spatial_kernel, distances),
-        in_specs=[pl.BlockSpec(memory_space=pltpu.SMEM), whole, whole, whole],
+        functools.partial(spatial_kernel, which),
+        in_specs=[whole] * (1 + len(kvs)),
         out_specs=[whole] * count,
         out_shape=[jax.ShapeDtypeStruct((rows, HW), BF)] * count,
         scratch_shapes=[pltpu.VMEM((width, total, 128), BF), pltpu.VMEM((width, total, 256), BF)]
@@ -199,12 +272,12 @@
         + [pltpu.VMEM((heads, rows, 128), F32)] * 2,
         compiler_params=params(24),
         cost_estimate=pl.CostEstimate(
-            flops=20 * count * rows * total * HW,
-            bytes_accessed=6_000_000,
-            transcendentals=count * rows * total * H,
+            flops=count * rows * total * HW,
+            bytes_accessed=1_000_000,
+            transcendentals=0,
         ),
         name="spatial_attention",
-    )(scalars, q, kv_a, kv_b)
+    )(q, *kvs)
 
 
 def reorder(to_patch_major):
@@ -215,41 +288,70 @@
     return (col == (row % 16) * 4 + row // 16).astype(BF)
 
 
-def middle_kernel(scalars, *refs):
-    s_refs, (x_ref, w_ref, middle_ref, send_ref, norm) = refs[:4], refs[4:]
-    first, limit, z = scalars[0], scalars[1], scalars[2]
-    for d in range(4):
-        f = lax.rem(z + 4 - d, 4)
-        valid = (first + f < limit).astype(F32)
-        branch = jnp.dot(s_refs[d][...], w_ref[...], preferred_element_type=F32)
-        middle = (x_ref[f].astype(F32) + valid * branch).astype(BF)
+def home(scalars, d):
+    return lax.rem(scalars[2] + 4 - d, 4)
+
+
+def middle_of(scalars, f, s_ref, x_ref, w_ref):
+    valid = (scalars[0] + f < scalars[1]).astype(F32)
+    branch = jnp.dot(s_ref[...], w_ref[...], preferred_element_type=F32)
+    return (x_ref[f].astype(F32) + valid * branch).astype(BF)
+
+
+def early_kernel(distances, scalars, *refs):
+    s_refs, (x_ref, w_ref, middle_ref, norm_ref) = refs[:-4], refs[-4:]
+    for d, s_ref in zip(distances, s_refs):
+        f = home(scalars, d)
+        middle = middle_of(scalars, f, s_ref, x_ref, w_ref)
         middle_ref[f] = middle
-        norm[f] = normalise(middle.astype(F32))
+        norm_ref[f] = normalise(middle.astype(F32))
+
+
+def early_rows(scalars, blocks, distances, video, w):
+    whole = pl.BlockSpec(memory_space=pltpu.VMEM)
+    return pl.pallas_call(
+        functools.partial(early_kernel, distances),
+        in_specs=[pl.BlockSpec(memory_space=pltpu.SMEM)] + [whole] * (2 + len(blocks)),
+        out_specs=[whole, whole],
+        out_shape=[jax.ShapeDtypeStruct((4, 144, WIDTH), BF)] * 2,
+        compiler_params=params(16),
+        cost_estimate=pl.CostEstimate(
+            flops=2 * len(blocks) * 144 * HW * WIDTH, bytes_accessed=8_000_000, transcendentals=0
+        ),
+        name="early_rows",
+    )(scalars, *blocks, video, w)
+
+
+def late_kernel(distance, scalars, s_ref, norm_ref, x_ref, w_ref, middle_ref, send_ref, late):
+    last = home(scalars, distance)
+    middle = middle_of(scalars, last, s_ref, x_ref, w_ref)
+    middle_ref[...] = middle
+    late[...] = normalise(middle.astype(F32))
     move = reorder(True)
     for b in range(9):
         rows = slice(b * 16, b * 16 + 16)
-        block = jnp.concatenate([norm[f, rows, :] for f in range(4)], axis=0)
-        moved = jnp.dot(move, block, preferred_element_type=F32).astype(BF)
-        send_ref[rows] = moved.reshape(16, 4, WIDTH)
-
-
-def middle_rows(scalars, blocks, video, w):
-    whole = pl.BlockSpec(memory_space=pltpu.VMEM)
-    return pl.pallas_call(
-        middle_kernel,
-        in_specs=[pl.BlockSpec(memory_space=pltpu.SMEM)] + [whole] * 6,
+        parts = [jnp.where(last == f, late[rows, :], norm_ref[f, rows, :]) for f in range(4)]
+        moved = jnp.dot(move, jnp.concatenate(parts, axis=0), preferred_element_type=F32)
+        send_ref[rows] = moved.astype(BF).reshape(16, 4, WIDTH)
+
+
+def late_rows(scalars, spatial, norm, distance, video, w):
+    whole = pl.BlockSpec(memory_space=pltpu.VMEM)
+    return pl.pallas_call(
+        functools.partial(late_kernel, distance),
+        in_specs=[pl.BlockSpec(memory_space=pltpu.SMEM)] + [whole] * 4,
         out_specs=[whole, whole],
         out_shape=[
-            jax.ShapeDtypeStruct((4, 144, WIDTH), BF),
+            jax.ShapeDtypeStruct((144, WIDTH), BF),
             jax.ShapeDtypeStruct((144, 4, WIDTH), BF),
         ],
-        scratch_shapes=[pltpu.VMEM((4, 144, WIDTH), BF)],
-        compiler_params=params(24),
-        cost_estimate=pl.CostEstimate(
-            flops=8 * 144 * HW * WIDTH, bytes_accessed=8_000_000, transcendentals=0
-        ),
-        name="middle_rows",
-    )(scalars, *blocks, video, w)
+        scratch_shapes=[pltpu.VMEM((144, WIDTH), BF)],
+        compiler_params=params(16),
+        cost_estimate=pl.CostEstimate(
+            flops=2 * 144 * HW * WIDTH, bytes_accessed=8_000_000, transcendentals=0
+        ),
+        name="late_rows",
+    )(scalars, spatial, norm, video, w)
 
 
 def temporal_kernel(n, scalars, x_ref, w_ref, o_ref, rows_ref):
@@ -307,7 +409,8 @@
     )(scalars, x, w)
 
 
-def encoded_kernel(scalars, t_ref, m_ref, w_ref, o_ref, rows_ref, held, sem):
+def encoded_kernel(distance, scalars, t_ref, m_ref, late_ref, w_ref, o_ref, rows_ref, held, sem):
+    last = home(scalars, distance)
     move = reorder(False)
     for b in range(9):
         block = t_ref[b * 16 : b * 16 + 16].reshape(64, HW)
@@ -327,7 +430,8 @@
         for f in range(4):
             valid = (first + f < limit).astype(F32)
             own = branch[f * 144 : (f + 1) * 144]
-            held[f, :, cols] = (m_ref[f, :, cols].astype(F32) + valid * own).astype(BF)
+            middle = jnp.where(last == f, late_ref[:, cols], m_ref[f, :, cols])
+            held[f, :, cols] = (middle.astype(F32) + valid * own).astype(BF)
         leave(j).start()
         return carry
 
@@ -336,11 +440,11 @@
         leave(j).wait()
 
 
-def encoded_rows(scalars, temporal, middle, w):
-    whole = pl.BlockSpec(memory_space=pltpu.VMEM)
-    return pl.pallas_call(
-        encoded_kernel,
-        in_specs=[pl.BlockSpec(memory_space=pltpu.SMEM), whole, whole, whole],
+def encoded_rows(scalars, temporal, middle, late, distance, w):
+    whole = pl.BlockSpec(memory_space=pltpu.VMEM)
+    return pl.pallas_call(
+        functools.partial(encoded_kernel, distance),
+        in_specs=[pl.BlockSpec(memory_space=pltpu.SMEM)] + [whole] * 4,
         out_specs=pl.BlockSpec(memory_space=pltpu.HBM),
         out_shape=jax.ShapeDtypeStruct((4, 144, WIDTH), BF),
         scratch_shapes=[
@@ -353,7 +457,7 @@
             flops=8 * 144 * HW * WIDTH, bytes_accessed=8_000_000, transcendentals=0
         ),
         name="encoded_rows",
-    )(scalars, temporal, middle, w)
+    )(scalars, temporal, middle, late, w)
 
 
 def along_z(x, distance):
@@ -373,19 +477,27 @@
     frame = lax.all_to_all(
         video, "space", split_axis=0, concat_axis=0, axis_index_groups=Z_GROUPS, tiled=True
     )
-    kv_own, norm1, w_q = keys_values(scalars, frame.reshape(4 * 144, WIDTH), qkv_space)
-    kv_other = lax.ppermute(kv_own, "space", SWAP)
-    q = queries(norm1, w_q).reshape(4, 144, HW)
+    kv_own, q_own = own_block(scalars, video, qkv_space)
+    kv_own_other = lax.ppermute(kv_own, "space", SWAP)
+    frame, kv_own, kv_own_other = lax.optimization_barrier((frame, kv_own, kv_own_other))
+    kv_rest, norm1, w_q = keys_values(scalars, frame, qkv_space)
+    kv_rest_other = lax.ppermute(kv_rest, "space", SWAP)
+    q_rest = queries(norm1, w_q)
+    kvs = (kv_rest, kv_own, kv_rest_other, kv_own_other)
     back = {}
     for distances in CALLS:
-        results = spatial_attention(scalars, q, kv_own, kv_other, distances)
+        results = spatial_attention(q_rest, kvs, [d - 1 for d in distances])
+        q_rest, q_own, *results = lax.optimization_barrier((q_rest, q_own, *results))
         for d, o in zip(distances, results):
-            back[d] = along_z(o, d) if d else o
-    middle, send = middle_rows(scalars, [back[d] for d in range(4)], video, out_space)
+            back[d] = along_z(o, d)
+    (back[0],) = spatial_attention(q_own, kvs, [0])
+    early = tuple(d for d in (0, 1, 2, 3) if d != LATE)
+    middle, norm2 = early_rows(scalars, [back[d] for d in early], early, video, out_space)
+    late, send = late_rows(scalars, back[LATE], norm2, LATE, video, out_space)
     rows = over_tm(send.reshape(TM, 9, 4, WIDTH))
     temporal = temporal_attention(scalars, rows, qkv_time, 9)
     temporal = over_tm(temporal).reshape(144, 4, HW)
-    return encoded_rows(scalars, temporal, middle, out_time)
+    return encoded_rows(scalars, temporal, middle, late, LATE, out_time)
 
 
 def solution(mesh):

time: 134 us -> 129 us (0.963)
  waiting for transfers between devices: 29.7 us -> 22.9 us
  Pallas kernels: 44.5 us -> 47.8 us
  blocking collectives: 49.9 us -> 47.7 us
    all_to_all x1, waiting for transfers between devices: 22.1 us -> 15 us  [per_device(): lax.all_to_all(video, 'space', split_axis=0, concat_axis=0, axis_index_gr...]
    pallas_call x5 -> x7, Pallas kernels: 25.8 us -> 30.1 us  [the longest x3 16.2 us: spatial_attention(): pl.pallas_call(functools.partial(spatial_kernel, which), in_specs=[whole]...]
    all_to_all x2, blocking collectives: 49.9 us -> 47.7 us  [over_tm(): return lax.all_to_all(x, 'tm', split_axis=0, concat_axis=0, tiled=True)]
    ppermute x1 -> x2, waiting for transfers between devices: 2.35 us -> 3.94 us  [the longest x1 1.99 us: per_device(): kv_own_other = lax.ppermute(kv_own, 'space', SWAP)]
  transfers between devices with their start and end apart: 5 -> 6, of which waited for: 4 -> 4; matrix products, arithmetic and copies ran while one was open for 0% -> 0% of each run, Pallas kernels for 9% -> 14%
where the time goes in v5:
time: 129 us; the launch traced here: 128 us
  Pallas kernels  47.8 us (37%)
  blocking collectives  47.7 us (37%)
  waiting for transfers between devices  22.9 us (18%)
  starting transfers between devices  8.95 us (7%)
    all_to_all x2, blocking collectives, over_tm(): return lax.all_to_all(x, 'tm', split_axis=0, concat_axis=0, tiled=True)  47.7 us
    pallas_call x3, Pallas kernels, spatial_attention(): pl.pallas_call(functools.partial(spatial_kernel, which), in_specs=[whole]...  16.2 us
    all_to_all x1, waiting for transfers between devices, per_device(): lax.all_to_all(video, 'space', split_axis=0, concat_axis=0, axis_index_gr...  15 us
    pallas_call x1, Pallas kernels, temporal_attention(): pl.pallas_call(functools.partial(temporal_kernel, n), in_specs=[pl.BlockS...  10.1 us
    pallas_call x1, Pallas kernels, keys_values(): pl.pallas_call(kv_kernel, in_specs=[pl.BlockSpec(memory_space=pltpu.SMEM)...  5.88 us
    all_to_all x1, starting transfers between devices, per_device(): lax.all_to_all(video, 'space', split_axis=0, concat_axis=0, axis_index_gr...  5.39 us
    pallas_call x1, Pallas kernels, own_block(): pl.pallas_call(own_kernel, in_specs=[pl.BlockSpec(memory_space=pltpu.SMEM...  4.95 us
    pallas_call x1, Pallas kernels, encoded_rows(): pl.pallas_call(functools.partial(encoded_kernel, distance), in_specs=[pl....  4.2 us
  transfers between devices with their start and end apart: 6, of which 4 were waited for; matrix products, arithmetic and copies ran while one was open for 0% of the time, Pallas kernels for 14%

profile of v5, /device:TPU:0, one launch (start us, length us, event | category | flops | bytes accessed | tf_op | source)
XLA Modules:
  0.0 128.4 jit_solution(15709190775056788345)
XLA Ops:
  0.0 5.4 %all-to-all-start = ((bf16[4,144,1536]{2,1,0:T(8,128)(2,1)}), bf16[4,144,1536]{2,1,0:T(8,128)(2,1)S(1)}, u32[]{:S(2)}, u32[]{:S(2)}) async-start(bf16[4,144,1536]{2,1,0:T(8,128)(2,1)} %x_ref.1), calls=%async_computation | async-start | bytes 3538944 | tf_op jit(solution)/shard_map/all_to_all | solution.py:477
  6.0 0.1 pad_add_fusion.scalars
  6.1 5.0 %own_block.1 = (bf16[144,2048]{1,0:T(8,128)(2,1)S(1)}, bf16[1,144,1024]{2,1,0:T(8,128)(2,1)S(1)}) custom-call(s32[3]{0:T(128)S(1)} %pad_add_fusion.scalars, bf16[4,144,1536]{2,1,0:T(8,128)(2,1)} %x_ref.1, bf16[1536,3072]{1,0:T(8,128)(2,1)} %w_ref.6), custom_call_target="tpu_custom_call" | custom-call | flops 1358954496 | bytes 12000000 | tf_op jit(solution)/shard_map/own_block/pallas_call | solution.py:84
  11.1 0.1 collective-permute-start
  11.2 2.0 %collective-permute-done.refs_3_ = bf16[144,2048]{1,0:T(8,128)(2,1)S(1)} collective-permute-done((bf16[144,2048]{1,0:T(8,128)(2,1)S(1)}, bf16[144,2048]{1,0:T(8,128)(2,1)S(1)}, u32[]{:S(2)}, u32[]{:S(2)}) %collective-permute-start) | collective-permute-done | bytes 589856 | tf_op jit(solution)/shard_map/ppermute | solution.py:481
  13.2 15.0 %all-to-all-done.x_ref = bf16[4,144,1536]{2,1,0:T(8,128)(2,1)S(1)} async-done(((bf16[4,144,1536]{2,1,0:T(8,128)(2,1)}), bf16[4,144,1536]{2,1,0:T(8,128)(2,1)S(1)}, u32[]{:S(2)}, u32[]{:S(2)}) %all-to-all-start) | async-done | bytes 1769504 | tf_op jit(solution)/shard_map/all_to_all | solution.py:477
  28.2 0.0 slice-start
  28.2 5.9 %keys_values.1 = (bf16[432,2048]{1,0:T(8,128)(2,1)S(1)}, bf16[432,1536]{1,0:T(8,128)(2,1)S(1)}, bf16[1536,1024]{1,0:T(8,128)(2,1)S(1)}) custom-call(s32[3]{0:T(128)S(1)} %pad_add_fusion.scalars, bf16[4,144,1536]{2,1,0:T(8,128)(2,1)S(1)} %all-to-all-done.x_ref, bf16[1536,3072]{1,0:T(8,128)(2,1)} %w_ref.6), custom_call_target="tpu_custom_call" | custom-call | flops 2717908992 | bytes 12000000 | tf_op jit(solution)/shard_map/keys_values/pallas_call | solution.py:143
  34.1 0.1 collective-permute-start.1
  34.2 1.7 %queries.1.q_ref = bf16[3,144,1024]{2,1,0:T(8,128)(2,1)S(1)} custom-call(bf16[432,1536]{1,0:T(8,128)(2,1)S(1)} %get-tuple-element.27.norm_ref, bf16[1536,1024]{1,0:T(8,128)(2,1)S(1)} %get-tuple-element.28.w_ref), custom_call_target="tpu_custom_call" | custom-call | flops 1358954496 | bytes 6000000 | tf_op jit(solution)/shard_map/queries/pallas_call | solution.py:179
  35.9 0.0 slice-start.1
  35.9 2.0 %collective-permute-done.1.refs_2_ = bf16[432,2048]{1,0:T(8,128)(2,1)S(1)} collective-permute-done((bf16[432,2048]{1,0:T(8,128)(2,1)S(1)}, bf16[432,2048]{1,0:T(8,128)(2,1)S(1)}, u32[]{:S(2)}, u32[]{:S(2)}) %collective-permute-start.1) | collective-permute-done | bytes 1769504 | tf_op jit(solution)/shard_map/ppermute | solution.py:484
  37.9 7.7 %spatial_attention.3 = (bf16[144,1024]{1,0:T(8,128)(2,1)S(1)}, bf16[144,1024]{1,0:T(8,128)(2,1)S(1)}) custom-call(bf16[3,144,1024]{2,1,0:T(8,128)(2,1)S(1)} %queries.1.q_ref, bf16[432,2048]{1,0:T(8,128)(2,1)S(1)} %get-tuple-element.30.refs_0_, bf16[144,2048]{1,0:T(8,128)(2,1)S(1)} %get-tuple-element.31.refs_1_, ...), custom_call_target="tpu_custom_call" | custom-call | flops 339738624 | bytes 1000000 | tf_op jit(solution)/shard_map/spatial_attention/pallas_call | solution.py:265
  45.5 0.6 collective-permute-start.3
  46.2 2.7 %collective-permute-start.4 = (bf16[144,1024]{1,0:T(8,128)(2,1)S(1)}, bf16[144,1024]{1,0:T(8,128)(2,1)S(1)}, u32[]{:S(2)}, u32[]{:S(2)}) collective-permute-start(bf16[144,1024]{1,0:T(8,128)(2,1)S(1)} %get-tuple-element.40), channel_id=1, source_target_pairs={{0,6},{1,7},{2,0},{3,1},{4,2},{5,3},{6,4},{7,5},{8,14},{9,15},{10,... | collective-permute-start | bytes 884744 | tf_op jit(solution)/shard_map/ppermute | solution.py:465
  48.8 4.3 %spatial_attention.4 = bf16[144,1024]{1,0:T(8,128)(2,1)S(1)} custom-call(bf16[3,144,1024]{2,1,0:T(8,128)(2,1)S(1)} %queries.1.q_ref, bf16[432,2048]{1,0:T(8,128)(2,1)S(1)} %get-tuple-element.30.refs_0_, bf16[144,2048]{1,0:T(8,128)(2,1)S(1)} %get-tuple-element.31.refs_1_, bf16[432,2048]{1,0:T(8,128)(2,1)S(1)} %collective-permute-done.1.refs_2_, ...), custom_call_target="tpu_custom_call" | custom-call | flops 169869312 | bytes 1000000 | tf_op jit(solution)/shard_map/spatial_attention/pallas_call | solution.py:265
  53.1 0.0 copy-start
  53.1 0.0 copy-start.1
  53.2 0.0 slice-start.2
  53.2 0.1 collective-permute-start.2
  53.3 4.3 %spatial_attention.5.refs_0_ = bf16[144,1024]{1,0:T(8,128)(2,1)S(1)} custom-call(bf16[1,144,1024]{2,1,0:T(8,128)(2,1)S(1)} %get-tuple-element.38.q_ref, bf16[432,2048]{1,0:T(8,128)(2,1)S(1)} %get-tuple-element.30.refs_0_, bf16[144,2048]{1,0:T(8,128)(2,1)S(1)} %get-tuple-element.31.refs_1_, bf16[432,2048]{1,0:T(8,128)(2,1)S(1)} %collective-permute-done.1.refs_2_, ...), custom_call_target="tpu_custom_call" | custom-call | flops 169869312 | bytes 1000000 | tf_op jit(solution)/shard_map/spatial_attention/pallas_call | solution.py:265
  57.6 0.0 collective-permute-done.3.refs_1_
  57.6 3.9 %collective-permute-done.4.refs_2_ = bf16[144,1024]{1,0:T(8,128)(2,1)S(1)} collective-permute-done((bf16[144,1024]{1,0:T(8,128)(2,1)S(1)}, bf16[144,1024]{1,0:T(8,128)(2,1)S(1)}, u32[]{:S(2)}, u32[]{:S(2)}) %collective-permute-start.4) | collective-permute-done | bytes 294944 | tf_op jit(solution)/shard_map/ppermute | solution.py:465
  61.5 0.0 copy-done
  61.5 0.0 copy-done.1
  61.5 2.7 %early_rows.1 = (bf16[4,144,1536]{2,1,0:T(8,128)(2,1)S(1)}, bf16[4,144,1536]{2,1,0:T(8,128)(2,1)S(1)}) custom-call(s32[3]{0:T(128)S(1)} %pad_add_fusion.scalars, bf16[144,1024]{1,0:T(8,128)(2,1)S(1)} %spatial_attention.5.refs_0_, bf16[144,1024]{1,0:T(8,128)(2,1)S(1)} %collective-permute-done.3.refs_1_, bf16[144,1024]{1,0:T(8,128)(2,1)S(1)} %collective-permute-done.4.refs_2_, ...), custom_call_target="tpu_custom_call" | custom-call | flops 1358954496 | bytes 8000000 | tf_op jit(solution)/shard_map/early_rows/pallas_call | solution.py:312
  64.2 0.0 collective-permute-done.2.s_ref
  64.2 2.0 %late_rows.1 = (bf16[144,1536]{1,0:T(8,128)(2,1)S(1)}, bf16[144,4,1536]{2,1,0:T(4,128)(2,1)S(1)}) custom-call(s32[3]{0:T(128)S(1)} %pad_add_fusion.scalars, bf16[144,1024]{1,0:T(8,128)(2,1)S(1)} %collective-permute-done.2.s_ref, bf16[4,144,1536]{2,1,0:T(8,128)(2,1)S(1)} %get-tuple-element.41.norm_ref, bf16[4,144,1536]{2,1,0:T(8,128)(2,1)S(1)} %copy-done, ...), custom_call_target="tpu_custom_call" | custom-call | flops 452984832 | bytes 8000000 | tf_op jit(solution)/shard_map/late_rows/pallas_call | solution.py:340
  66.2 29.3 %all_to_all.15.x_ref = bf16[16,9,4,1536]{3,2,1,0:T(4,128)(2,1)S(1)} all-to-all(bf16[16,9,4,1536]{3,2,1,0:T(4,128)(2,1)S(1)} %bitcast.5), channel_id=1, replica_groups=mesh['tm'=16,'space'=8] {'tm'}, dimensions={0} | all-to-all | bytes 3538944 | tf_op jit(solution)/shard_map/all_to_all | solution.py:469
  95.6 0.0 slice-done
  95.6 0.0 slice-done.1
  95.6 0.0 slice-done.2
  95.6 0.0 copy-start.2
  95.6 10.1 %temporal_attention.1 = bf16[16,9,4,1024]{3,2,1,0:T(4,128)(2,1)S(1)} custom-call(s32[3]{0:T(128)S(1)} %pad_add_fusion.scalars, bf16[16,9,4,1536]{3,2,1,0:T(4,128)(2,1)S(1)} %all_to_all.15.x_ref, bf16[1536,3072]{1,0:T(8,128)(2,1)S(1)} %bitcast.7), custom_call_target="tpu_custom_call" | custom-call | flops 5435817984 | bytes 14000000 | tf_op jit(solution)/shard_map/temporal_attention/pallas_call | solution.py:398
  105.7 18.4 %all_to_all.16 = bf16[16,9,4,1024]{3,2,1,0:T(4,128)(2,1)S(1)} all-to-all(bf16[16,9,4,1024]{3,2,1,0:T(4,128)(2,1)S(1)} %temporal_attention.1), channel_id=1, replica_groups=mesh['tm'=16,'space'=8] {'tm'}, dimensions={0} | all-to-all | bytes 2359296 | tf_op jit(solution)/shard_map/all_to_all | solution.py:469
  124.1 0.0 copy-done.2
  124.1 4.2 %encoded_rows.1 = bf16[4,144,1536]{2,1,0:T(8,128)(2,1)} custom-call(s32[3]{0:T(128)S(1)} %pad_add_fusion.scalars, bf16[144,4,1024]{2,1,0:T(4,128)(2,1)S(1)} %bitcast.4, bf16[4,144,1536]{2,1,0:T(8,128)(2,1)S(1)} %get-tuple-element.43.m_ref, bf16[144,1536]{1,0:T(8,128)(2,1)S(1)} %get-tuple-element.44.late_ref, bf16[1024,1536]{1,0:T(8,128)(2,1)S(1)} %copy-done.2), custom_call_target="tpu_custom_call" | custom-call | flops 1811939328 | bytes 8000000 | tf_op jit(solution)/shard_map/encoded_rows/pallas_call | solution.py:445
  (1 shorter events, 0.0 us)
Async XLA Ops:
  0.0 28.2 %all-to-all-start = ((bf16[4,144,1536]{2,1,0:T(8,128)(2,1)}), bf16[4,144,1536]{2,1,0:T(8,128)(2,1)S(1)}, u32[]{:S(2)}, u32[]{:S(2)}) async-start(bf16[4,144,1536]{2,1,0:T(8,128)(2,1)} %x_ref.1), calls=%async_computation | async-start | bytes 3538944 | tf_op jit(solution)/shard_map/all_to_all | solution.py:477
  11.1 2.1 %collective-permute-start = (bf16[144,2048]{1,0:T(8,128)(2,1)S(1)}, bf16[144,2048]{1,0:T(8,128)(2,1)S(1)}, u32[]{:S(2)}, u32[]{:S(2)}) collective-permute-start(bf16[144,2048]{1,0:T(8,128)(2,1)S(1)} %get-tuple-element.31.refs_1_), channel_id=1, source_target_pairs={{0,1},{1,0},{2,3},{3,2},{4,5},{5,4},{6,7},{7,6},{8,9},{9,8},{10,11... | collective-permute-start | bytes 1769480 | tf_op jit(solution)/shard_map/ppermute | solution.py:481
  28.2 67.4 %slice-start = ((s8[9437184]{0:T(1024)(128)(4,1)}), s8[4194304]{0:T(1024)(128)(4,1)S(1)}, s32[]{:S(2)}) async-start(s8[9437184]{0:T(1024)(128)(4,1)} %bitcast.6), calls=%async_computation.3 | async-start | bytes 8388608
  34.1 3.8 %collective-permute-start.1 = (bf16[432,2048]{1,0:T(8,128)(2,1)S(1)}, bf16[432,2048]{1,0:T(8,128)(2,1)S(1)}, u32[]{:S(2)}, u32[]{:S(2)}) collective-permute-start(bf16[432,2048]{1,0:T(8,128)(2,1)S(1)} %get-tuple-element.30.refs_0_), channel_id=1, source_target_pairs={{0,1},{1,0},{2,3},{3,2},{4,5},{5,4},{6,7},{7,6},{8,9},{9,8},{10,11... | collective-permute-start | bytes 5308424 | tf_op jit(solution)/shard_map/ppermute | solution.py:484
  35.9 59.7 %slice-start.1 = ((s8[9437184]{0:T(1024)(128)(4,1)}), s8[4194304]{0:T(1024)(128)(4,1)S(1)}, s32[]{:S(2)}) async-start(s8[9437184]{0:T(1024)(128)(4,1)} %bitcast.6), calls=%async_computation.4 | async-start | bytes 8388608
  45.5 12.0 %collective-permute-start.3 = (bf16[144,1024]{1,0:T(8,128)(2,1)S(1)}, bf16[144,1024]{1,0:T(8,128)(2,1)S(1)}, u32[]{:S(2)}, u32[]{:S(2)}) collective-permute-start(bf16[144,1024]{1,0:T(8,128)(2,1)S(1)} %get-tuple-element.39), channel_id=1, source_target_pairs={{0,2},{1,3},{2,4},{3,5},{4,6},{5,7},{6,0},{7,1},{8,10},{9,11},{10,... | collective-permute-start | bytes 884744 | tf_op jit(solution)/shard_map/ppermute | solution.py:465
  46.2 15.3 %collective-permute-start.4 = (bf16[144,1024]{1,0:T(8,128)(2,1)S(1)}, bf16[144,1024]{1,0:T(8,128)(2,1)S(1)}, u32[]{:S(2)}, u32[]{:S(2)}) collective-permute-start(bf16[144,1024]{1,0:T(8,128)(2,1)S(1)} %get-tuple-element.40), channel_id=1, source_target_pairs={{0,6},{1,7},{2,0},{3,1},{4,2},{5,3},{6,4},{7,5},{8,14},{9,15},{10,... | collective-permute-start | bytes 884744 | tf_op jit(solution)/shard_map/ppermute | solution.py:465
  53.1 8.3 %copy-start = (bf16[4,144,1536]{2,1,0:T(8,128)(2,1)S(1)}, bf16[4,144,1536]{2,1,0:T(8,128)(2,1)}, u32[]{:S(2)}) copy-start(bf16[4,144,1536]{2,1,0:T(8,128)(2,1)} %x_ref.1) | copy-start | bytes 5308420
  53.1 8.3 %copy-start.1 = (bf16[1024,1536]{1,0:T(8,128)(2,1)S(1)}, bf16[1024,1536]{1,0:T(8,128)(2,1)}, u32[]{:S(2)}) copy-start(bf16[1024,1536]{1,0:T(8,128)(2,1)} %w_ref.7) | copy-start | bytes 9437188
  53.2 42.4 %slice-start.2 = ((s8[9437184]{0:T(1024)(128)(4,1)}), s8[1048576]{0:T(1024)(128)(4,1)S(1)}, s32[]{:S(2)}) async-start(s8[9437184]{0:T(1024)(128)(4,1)} %bitcast.6), calls=%async_computation.5 | async-start | bytes 2097152
  53.2 11.0 %collective-permute-start.2 = (bf16[144,1024]{1,0:T(8,128)(2,1)S(1)}, bf16[144,1024]{1,0:T(8,128)(2,1)S(1)}, u32[]{:S(2)}, u32[]{:S(2)}) collective-permute-start(bf16[144,1024]{1,0:T(8,128)(2,1)S(1)} %spatial_attention.4), channel_id=1, source_target_pairs={{0,4},{1,5},{2,6},{3,7},{4,0},{5,1},{6,2},{7,3},{8,12},{9,13},{10,... | collective-permute-start | bytes 884744 | tf_op jit(solution)/shard_map/ppermute | solution.py:465
  95.6 28.5 %copy-start.2 = (bf16[1024,1536]{1,0:T(8,128)(2,1)S(1)}, bf16[1024,1536]{1,0:T(8,128)(2,1)}, u32[]{:S(2)}) copy-start(bf16[1024,1536]{1,0:T(8,128)(2,1)} %w_ref.9) | copy-start | bytes 9437188

commit v6 on v5

--- a/solution.py
+++ b/solution.py
@@ -13,12 +13,14 @@
 HW = H * HD
 TM = 16
 QSCALE = 0.125 * 1.4426950408889634
-CALLS = ((1, 3), (2,))
 LATE = 2
 SWAP = [(i, i ^ 1) for i in range(8)]
-Z_GROUPS = [[0, 2, 4, 6], [1, 3, 5, 7]]
 BF = jnp.bfloat16
 F32 = jnp.float32
+
+
+HEAVY = pl.CostEstimate(flops=20_000_000_000, bytes_accessed=1_000_000, transcendentals=0)
+LIGHT = pl.CostEstimate(flops=100_000_000, bytes_accessed=1_000_000, transcendentals=0)
 
 
 def params(mebibytes):
@@ -96,9 +98,7 @@
             pltpu.SemaphoreType.DMA((7,)),
         ],
         compiler_params=params(24),
-        cost_estimate=pl.CostEstimate(
-            flops=2 * rows * WIDTH * 3 * HW, bytes_accessed=12_000_000, transcendentals=0
-        ),
+        cost_estimate=LIGHT,
         name="own_block",
     )(
         scalars,
@@ -107,7 +107,68 @@
     )
 
 
-def kv_kernel(scalars, x_ref, w_ref, kv_ref, norm_ref, wq_ref, wkv, sem):
+def near_kernel(count, *refs):
+    x_refs, (w_ref, kv_ref, q_ref, norm_ref, held, sem) = refs[:count], refs[count:]
+
+    def fetch(j):
+        return pltpu.make_async_copy(w_ref.at[:, block(j)], held.at[:, block(j)], sem.at[j])
+
+    for j in (2, 3, 4, 5, 0, 1):
+        fetch(j).start()
+    normalise_blocks(x_refs, norm_ref)
+
+    def key_value(j, carry):
+        fetch(j).wait()
+        y = jnp.dot(norm_ref[...], held[:, block(j)], preferred_element_type=F32)
+        kv_ref[:, block(j - 2)] = y.astype(BF)
+        return carry
+
+    def query(j, carry):
+        fetch(j).wait()
+        y = jnp.dot(norm_ref[...], held[:, block(j)], preferred_element_type=F32)
+        q = (y * QSCALE).astype(BF)
+        for b in range(count):
+            q_ref[b, :, block(j)] = q[b * 144 : (b + 1) * 144]
+        return carry
+
+    lax.fori_loop(2, 6, key_value, 0)
+    lax.fori_loop(0, 2, query, 0)
+
+
+def normalise_blocks(x_refs, norm_ref):
+    for b, x_ref in enumerate(x_refs):
+
+        def norm(i, carry):
+            lo = pl.multiple_of(i * 48, 48)
+            norm_ref[pl.ds(b * 144 + lo, 48), :] = normalise(x_ref[pl.ds(lo, 48), :].astype(F32))
+            return carry
+
+        lax.fori_loop(0, 3, norm, 0, unroll=True)
+
+
+def near_blocks(blocks, w):
+    count, rows = len(blocks), 144 * len(blocks)
+    whole = pl.BlockSpec(memory_space=pltpu.VMEM)
+    return pl.pallas_call(
+        functools.partial(near_kernel, count),
+        in_specs=[whole] * count + [pl.BlockSpec(memory_space=pltpu.HBM)],
+        out_specs=[whole, whole],
+        out_shape=[
+            jax.ShapeDtypeStruct((rows, 2 * HW), BF),
+            jax.ShapeDtypeStruct((count, 144, HW), BF),
+        ],
+        scratch_shapes=[
+            pltpu.VMEM((rows, WIDTH), BF),
+            pltpu.VMEM((WIDTH, 3 * HW), BF),
+            pltpu.SemaphoreType.DMA((6,)),
+        ],
+        compiler_params=params(24),
+        cost_estimate=LIGHT,
+        name="near_blocks",
+    )(*blocks, pltpu.with_memory_space_constraint(w, pltpu.HBM))
+
+
+def kv_kernel(x_ref, w_ref, kv_ref, norm_ref, wq_ref, wkv, sem):
     def fetch(j):
         source = pl.ds(pl.multiple_of(j * 512 + HW, 128), 512)
         return pltpu.make_async_copy(w_ref.at[:, source], wkv.at[:, block(j)], sem.at[j])
@@ -116,16 +177,7 @@
         fetch(j).start()
     for_queries = pltpu.make_async_copy(w_ref.at[:, :HW], wq_ref, sem.at[4])
     for_queries.start()
-    for d in range(1, 4):
-        other = lax.rem(scalars[2] + d, 4)
-
-        def norm(i, carry):
-            lo = pl.multiple_of(i * 48, 48)
-            wide = x_ref[other, pl.ds(lo, 48), :].astype(F32)
-            norm_ref[pl.ds((d - 1) * 144 + lo, 48), :] = normalise(wide)
-            return carry
-
-        lax.fori_loop(0, 3, norm, 0, unroll=True)
+    normalise_blocks([x_ref], norm_ref)
 
     def step(j, carry):
         fetch(j).wait()
@@ -133,20 +185,16 @@
         kv_ref[:, block(j)] = y.astype(BF)
         return carry
 
-    lax.fori_loop(0, 4, step, 0)
+    lax.fori_loop(0, 4, step, 0, unroll=4)
     for_queries.wait()
 
 
-def keys_values(scalars, x, w):
-    rows = 3 * x.shape[1]
+def keys_values(x, w):
+    rows = x.shape[0]
     whole = pl.BlockSpec(memory_space=pltpu.VMEM)
     return pl.pallas_call(
         kv_kernel,
-        in_specs=[
-            pl.BlockSpec(memory_space=pltpu.SMEM),
-            whole,
-            pl.BlockSpec(memory_space=pltpu.HBM),
-        ],
+        in_specs=[whole, pl.BlockSpec(memory_space=pltpu.HBM)],
         out_specs=[whole, whole, whole],
         out_shape=[
             jax.ShapeDtypeStruct((rows, 2 * HW), BF),
@@ -155,36 +203,29 @@
         ],
         scratch_shapes=[pltpu.VMEM((WIDTH, 2 * HW), BF), pltpu.SemaphoreType.DMA((5,))],
         compiler_params=params(24),
-        cost_estimate=pl.CostEstimate(
-            flops=2 * rows * WIDTH * 2 * HW, bytes_accessed=12_000_000, transcendentals=0
-        ),
+        cost_estimate=HEAVY,
         name="keys_values",
-    )(scalars, x, pltpu.with_memory_space_constraint(w, pltpu.HBM))
+    )(x, pltpu.with_memory_space_constraint(w, pltpu.HBM))
 
 
 def q_kernel(norm_ref, w_ref, q_ref):
     def step(j, carry):
         y = jnp.dot(norm_ref[...], w_ref[:, block(j)], preferred_element_type=F32)
-        q = (y * QSCALE).astype(BF)
-        for d in range(3):
-            q_ref[d, :, block(j)] = q[d * 144 : (d + 1) * 144]
-        return carry
-
-    lax.fori_loop(0, 2, step, 0)
+        q_ref[0, :, block(j)] = (y * QSCALE).astype(BF)
+        return carry
+
+    lax.fori_loop(0, 2, step, 0, unroll=2)
 
 
 def queries(norm, w):
-    rows = norm.shape[0]
     whole = pl.BlockSpec(memory_space=pltpu.VMEM)
     return pl.pallas_call(
         q_kernel,
         in_specs=[whole, whole],
         out_specs=whole,
-        out_shape=jax.ShapeDtypeStruct((3, 144, HW), BF),
+        out_shape=jax.ShapeDtypeStruct((1, norm.shape[0], HW), BF),
         compiler_params=params(16),
-        cost_estimate=pl.CostEstimate(
-            flops=2 * rows * WIDTH * HW, bytes_accessed=6_000_000, transcendentals=0
-        ),
+        cost_estimate=LIGHT,
         name="queries",
     )(norm, w)
 
@@ -389,7 +430,7 @@
             o_ref[:, i, :, cols] = tn_dot(weights[i], v4).astype(BF).reshape(16, 4, 256)
         return carry
 
-    lax.fori_loop(0, 4, step, 0)
+    lax.fori_loop(0, 4, step, 0, unroll=4)
 
 
 def temporal_attention(scalars, x, w, n):
@@ -435,7 +476,7 @@
         leave(j).start()
         return carry
 
-    lax.fori_loop(0, 3, project, 0)
+    lax.fori_loop(0, 3, project, 0, unroll=3)
     for j in range(3):
         leave(j).wait()
 
@@ -474,23 +515,31 @@
     z = lax.axis_index("space") // 2
     scalars = jnp.stack([first, frame_count[0], z]).astype(jnp.int32)
 
-    frame = lax.all_to_all(
-        video, "space", split_axis=0, concat_axis=0, axis_index_groups=Z_GROUPS, tiled=True
-    )
+    def from_chip(e, sent):
+        return along_z(sent, 4 - e)
+
+    sent = {
+        e: lax.dynamic_index_in_dim(video, lax.rem(z + 4 - e, 4), 0, keepdims=False) for e in (1, 3, 2)
+    }
+    near = [from_chip(e, sent[e]) for e in (1, 3)]
     kv_own, q_own = own_block(scalars, video, qkv_space)
     kv_own_other = lax.ppermute(kv_own, "space", SWAP)
-    frame, kv_own, kv_own_other = lax.optimization_barrier((frame, kv_own, kv_own_other))
-    kv_rest, norm1, w_q = keys_values(scalars, frame, qkv_space)
-    kv_rest_other = lax.ppermute(kv_rest, "space", SWAP)
-    q_rest = queries(norm1, w_q)
-    kvs = (kv_rest, kv_own, kv_rest_other, kv_own_other)
+    late, kv_own, *near = lax.optimization_barrier((sent[2], kv_own, *near))
+    far = from_chip(2, late)
+    kv_near, q_near = near_blocks(near, qkv_space)
+    kv_near_other = lax.ppermute(kv_near, "space", SWAP)
+    far, kv_near = lax.optimization_barrier((far, kv_near))
+    kv_far, norm1, w_q = keys_values(far, qkv_space)
+    kv_far_other = lax.ppermute(kv_far, "space", SWAP)
+    q_far = queries(norm1, w_q)
+    kvs = (kv_near, kv_far, kv_own, kv_near_other, kv_far_other, kv_own_other)
     back = {}
-    for distances in CALLS:
-        results = spatial_attention(q_rest, kvs, [d - 1 for d in distances])
-        q_rest, q_own, *results = lax.optimization_barrier((q_rest, q_own, *results))
-        for d, o in zip(distances, results):
-            back[d] = along_z(o, d)
-    (back[0],) = spatial_attention(q_own, kvs, [0])
+    for blocks in ((1, 3), (2,)):
+        results = spatial_attention(q_near if 1 in blocks else q_far, kvs, range(len(blocks)))
+        q_far, q_own, *results = lax.optimization_barrier((q_far, q_own, *results))
+        for e, o in zip(blocks, results):
+            back[e] = along_z(o, e)
+    (back[0],) = spatial_attention(q_own, kvs, range(1))
     early = tuple(d for d in (0, 1, 2, 3) if d != LATE)
     middle, norm2 = early_rows(scalars, [back[d] for d in early], early, video, out_space)
     late, send = late_rows(scalars, back[LATE], norm2, LATE, video, out_space)

time: 129 us -> 126 us (0.977)
  waiting for transfers between devices: 22.9 us -> 18.9 us
  local copies, waits for them, and re-layouts: 0.04 us -> 1.41 us
    all_to_all x1 -> x0, waiting for transfers between devices: 15 us -> none  [per_device(): lax.all_to_all(video, 'space', split_axis=0, concat_axis=0, axis_index_gr...]
    ppermute x3 -> x6, waiting for transfers between devices: 3.92 us -> 17.5 us  [along_z(): return lax.ppermute(x, 'space', pairs)]
    all_to_all x1 -> x0, starting transfers between devices: 5.39 us -> none  [per_device(): lax.all_to_all(video, 'space', split_axis=0, concat_axis=0, axis_index_gr...]
    ppermute x3 -> x6, starting transfers between devices: 3.39 us -> 7.58 us  [along_z(): return lax.ppermute(x, 'space', pairs)]
    pallas_call x1 -> x2, Pallas kernels: 5.88 us -> 9.24 us  [the longest x1 5.35 us: near_blocks(): pl.pallas_call(functools.partial(near_kernel, count), in_specs=[whole] *...]
    ppermute x1, waiting for transfers between devices: 1.99 us -> 0.01 us  [per_device(): kv_own_other = lax.ppermute(kv_own, 'space', SWAP)]
    pallas_call x1, Pallas kernels: 10.1 us -> 8.6 us  [temporal_attention(): pl.pallas_call(functools.partial(temporal_kernel, n), in_specs=[pl.BlockS...]
    squeeze x0 -> x1, local copies, waits for them, and re-layouts: none -> 1.37 us  [per_device(): lax.dynamic_index_in_dim(video, lax.rem(z + 4 - e, 4), 0, keepdims=False)]
  transfers between devices with their start and end apart: 6 -> 9, of which waited for: 4 -> 5; matrix products, arithmetic and copies ran while one was open for 0% -> 0% of each run, Pallas kernels for 14% -> 21%
where the time goes in v6:
time: 126 us; the launch traced here: 125 us
  blocking collectives  47.8 us (38%)
  Pallas kernels  47.6 us (38%)
  waiting for transfers between devices  18.9 us (15%)
  starting transfers between devices  8.42 us (7%)
  local copies, waits for them, and re-layouts  1.41 us (1%)
    all_to_all x2, blocking collectives, over_tm(): return lax.all_to_all(x, 'tm', split_axis=0, concat_axis=0, tiled=True)  47.8 us
    ppermute x6, waiting for transfers between devices, along_z(): return lax.ppermute(x, 'space', pairs)  17.5 us
    pallas_call x3, Pallas kernels, spatial_attention(): pl.pallas_call(functools.partial(spatial_kernel, which), in_specs=[whole]...  15.9 us
    pallas_call x1, Pallas kernels, temporal_attention(): pl.pallas_call(functools.partial(temporal_kernel, n), in_specs=[pl.BlockS...  8.6 us
    ppermute x6, starting transfers between devices, along_z(): return lax.ppermute(x, 'space', pairs)  7.58 us
    pallas_call x1, Pallas kernels, near_blocks(): pl.pallas_call(functools.partial(near_kernel, count), in_specs=[whole] *...  5.35 us
    pallas_call x1, Pallas kernels, own_block(): pl.pallas_call(own_kernel, in_specs=[pl.BlockSpec(memory_space=pltpu.SMEM...  4.95 us
    pallas_call x1, Pallas kernels, keys_values(): pl.pallas_call(kv_kernel, in_specs=[whole, pl.BlockSpec(memory_space=pltp...  3.89 us
  transfers between devices with their start and end apart: 9, of which 5 were waited for; matrix products, arithmetic and copies ran while one was open for 0% of the time, Pallas kernels for 21%

profile of v6, /device:TPU:0, one launch (start us, length us, event | category | flops | bytes accessed | tf_op | source)
XLA Modules:
  0.0 125.2 jit_solution(610619779673212796)
XLA Ops:
  0.0 1.4 %dynamic-slice_bitcast_fusion = (bf16[144,1536]{1,0:T(8,128)(2,1)S(1)}, bf16[144,1536]{1,0:T(8,128)(2,1)S(1)}, bf16[144,1536]{1,0:T(8,128)(2,1)S(1)}) fusion(bf16[4,144,1536]{2,1,0:T(8,128)(2,1)} %x_ref.1, s32[]{:T(128)S(6)} %select_n.18, s32[]{:T(128)S(6)} %select_n.17, s32[]{:T(128)S(6)} %select_n.16), kind=kLoop, calls=%fused_computation | loop fusion | bytes 2654220 | tf_op jit(solution)/shard_map/jit(dynamic_index_in_dim)/squeeze | solution.py:522
  1.4 4.2 %collective-permute-start = (bf16[144,1536]{1,0:T(8,128)(2,1)S(1)}, bf16[144,1536]{1,0:T(8,128)(2,1)S(1)}, u32[]{:S(2)}, u32[]{:S(2)}) collective-permute-start(bf16[144,1536]{1,0:T(8,128)(2,1)S(1)} %get-tuple-element.56), channel_id=1, source_target_pairs={{0,6},{1,7},{2,0},{3,1},{4,2},{5,3},{6,4},{7,5},{8,14},{9,15},{10,... | collective-permute-start | bytes 1327112 | tf_op jit(solution)/shard_map/ppermute | solution.py:506
  5.6 0.0 collective-permute-start.1
  6.2 0.1 pad_add_fusion.scalars
  6.3 5.0 %own_block.1 = (bf16[144,2048]{1,0:T(8,128)(2,1)S(1)}, bf16[1,144,1024]{2,1,0:T(8,128)(2,1)S(1)}) custom-call(s32[3]{0:T(128)S(1)} %pad_add_fusion.scalars, bf16[4,144,1536]{2,1,0:T(8,128)(2,1)} %x_ref.1, bf16[1536,3072]{1,0:T(8,128)(2,1)} %w_ref.6), custom_call_target="tpu_custom_call" | custom-call | flops 100000000 | bytes 1000000 | tf_op jit(solution)/shard_map/own_block/pallas_call | solution.py:86
  11.3 3.7 %collective-permute-done.refs_0_ = bf16[144,1536]{1,0:T(8,128)(2,1)S(1)} collective-permute-done((bf16[144,1536]{1,0:T(8,128)(2,1)S(1)}, bf16[144,1536]{1,0:T(8,128)(2,1)S(1)}, u32[]{:S(2)}, u32[]{:S(2)}) %collective-permute-start) | collective-permute-done | bytes 442400 | tf_op jit(solution)/shard_map/ppermute | solution.py:506
  15.0 3.4 %collective-permute-done.1.refs_1_ = bf16[144,1536]{1,0:T(8,128)(2,1)S(1)} collective-permute-done((bf16[144,1536]{1,0:T(8,128)(2,1)S(1)}, bf16[144,1536]{1,0:T(8,128)(2,1)S(1)}, u32[]{:S(2)}, u32[]{:S(2)}) %collective-permute-start.1) | collective-permute-done | bytes 442400 | tf_op jit(solution)/shard_map/ppermute | solution.py:506
  18.4 0.0 collective-permute-start.2
  18.4 0.0 collective-permute-start.5
  18.4 5.4 %near_blocks.1 = (bf16[288,2048]{1,0:T(8,128)(2,1)S(1)}, bf16[2,144,1024]{2,1,0:T(8,128)(2,1)S(1)}) custom-call(bf16[144,1536]{1,0:T(8,128)(2,1)S(1)} %collective-permute-done.refs_0_, bf16[144,1536]{1,0:T(8,128)(2,1)S(1)} %collective-permute-done.1.refs_1_, bf16[1536,3072]{1,0:T(8,128)(2,1)} %w_ref.6), custom_call_target="tpu_custom_call" | custom-call | flops 100000000 | bytes 1000000 | tf_op jit(solution)/shard_map/near_blocks/pallas_call | solution.py:152
  23.8 0.6 collective-permute-start.3
  24.3 6.3 %collective-permute-done.2.x_ref = bf16[144,1536]{1,0:T(8,128)(2,1)S(1)} collective-permute-done((bf16[144,1536]{1,0:T(8,128)(2,1)S(1)}, bf16[144,1536]{1,0:T(8,128)(2,1)S(1)}, u32[]{:S(2)}, u32[]{:S(2)}) %collective-permute-start.2) | collective-permute-done | bytes 442400 | tf_op jit(solution)/shard_map/ppermute | solution.py:506
  30.6 3.9 %keys_values.1 = (bf16[144,2048]{1,0:T(8,128)(2,1)S(1)}, bf16[144,1536]{1,0:T(8,128)(2,1)S(1)}, bf16[1536,1024]{1,0:T(8,128)(2,1)S(1)}) custom-call(bf16[144,1536]{1,0:T(8,128)(2,1)S(1)} %collective-permute-done.2.x_ref, bf16[1536,3072]{1,0:T(8,128)(2,1)} %w_ref.6), custom_call_target="tpu_custom_call" | custom-call | flops 20000000000 | bytes 1000000 | tf_op jit(solution)/shard_map/keys_values/pallas_call | solution.py:195
  34.5 0.3 collective-permute-start.4
  34.8 0.6 queries.1.q_ref
  35.4 0.0 collective-permute-done.5.refs_5_
  35.4 1.3 %collective-permute-done.4.refs_4_ = bf16[144,2048]{1,0:T(8,128)(2,1)S(1)} collective-permute-done((bf16[144,2048]{1,0:T(8,128)(2,1)S(1)}, bf16[144,2048]{1,0:T(8,128)(2,1)S(1)}, u32[]{:S(2)}, u32[]{:S(2)}) %collective-permute-start.4) | collective-permute-done | bytes 589856 | tf_op jit(solution)/shard_map/ppermute | solution.py:533
  36.8 0.0 collective-permute-done.3.refs_3_
  36.8 0.0 slice-start
  36.8 7.5 %spatial_attention.3 = (bf16[144,1024]{1,0:T(8,128)(2,1)S(1)}, bf16[144,1024]{1,0:T(8,128)(2,1)S(1)}) custom-call(bf16[2,144,1024]{2,1,0:T(8,128)(2,1)S(1)} %get-tuple-element.39.q_ref, bf16[288,2048]{1,0:T(8,128)(2,1)S(1)} %get-tuple-element.40.refs_0_, bf16[144,2048]{1,0:T(8,128)(2,1)S(1)} %get-tuple-element.41.refs_1_, ...), custom_call_target="tpu_custom_call" | custom-call | flops 339738624 | bytes 1000000 | tf_op jit(solution)/shard_map/spatial_attention/pallas_call | solution.py:306
  44.3 0.1 collective-permute-start.7
  44.4 3.2 %collective-permute-start.8 = (bf16[144,1024]{1,0:T(8,128)(2,1)S(1)}, bf16[144,1024]{1,0:T(8,128)(2,1)S(1)}, u32[]{:S(2)}, u32[]{:S(2)}) collective-permute-start(bf16[144,1024]{1,0:T(8,128)(2,1)S(1)} %get-tuple-element.50), channel_id=1, source_target_pairs={{0,6},{1,7},{2,0},{3,1},{4,2},{5,3},{6,4},{7,5},{8,14},{9,15},{10,... | collective-permute-start | bytes 884744 | tf_op jit(solution)/shard_map/ppermute | solution.py:506
  47.6 4.2 %spatial_attention.4 = bf16[144,1024]{1,0:T(8,128)(2,1)S(1)} custom-call(bf16[1,144,1024]{2,1,0:T(8,128)(2,1)S(1)} %queries.1.q_ref, bf16[288,2048]{1,0:T(8,128)(2,1)S(1)} %get-tuple-element.40.refs_0_, bf16[144,2048]{1,0:T(8,128)(2,1)S(1)} %get-tuple-element.41.refs_1_, bf16[144,2048]{1,0:T(8,128)(2,1)S(1)} %get-tuple-element.42.refs_2_, ...), custom_call_target="tpu_custom_call" | custom-call | flops 169869312 | bytes 1000000 | tf_op jit(solution)/shard_map/spatial_attention/pallas_call | solution.py:306
  51.8 0.0 copy-start
  51.8 0.0 copy-start.1
  51.8 0.0 slice-start.1
  51.8 0.1 collective-permute-start.6
  51.9 4.2 %spatial_attention.5.refs_0_ = bf16[144,1024]{1,0:T(8,128)(2,1)S(1)} custom-call(bf16[1,144,1024]{2,1,0:T(8,128)(2,1)S(1)} %get-tuple-element.48.q_ref, bf16[288,2048]{1,0:T(8,128)(2,1)S(1)} %get-tuple-element.40.refs_0_, bf16[144,2048]{1,0:T(8,128)(2,1)S(1)} %get-tuple-element.41.refs_1_, bf16[144,2048]{1,0:T(8,128)(2,1)S(1)} %get-tuple-element.42.refs_2_, ...), custom_call_target="tpu_custom_call" | custom-call | flops 169869312 | bytes 1000000 | tf_op jit(solution)/shard_map/spatial_attention/pallas_call | solution.py:306
  56.1 0.0 slice-start.2
  56.1 0.0 collective-permute-done.7.refs_1_
  56.1 4.1 %collective-permute-done.8.refs_2_ = bf16[144,1024]{1,0:T(8,128)(2,1)S(1)} collective-permute-done((bf16[144,1024]{1,0:T(8,128)(2,1)S(1)}, bf16[144,1024]{1,0:T(8,128)(2,1)S(1)}, u32[]{:S(2)}, u32[]{:S(2)}) %collective-permute-start.8) | collective-permute-done | bytes 294944 | tf_op jit(solution)/shard_map/ppermute | solution.py:506
  60.2 0.0 copy-done
  60.2 0.0 copy-done.1
  60.2 2.6 %early_rows.1 = (bf16[4,144,1536]{2,1,0:T(8,128)(2,1)S(1)}, bf16[4,144,1536]{2,1,0:T(8,128)(2,1)S(1)}) custom-call(s32[3]{0:T(128)S(1)} %pad_add_fusion.scalars, bf16[144,1024]{1,0:T(8,128)(2,1)S(1)} %spatial_attention.5.refs_0_, bf16[144,1024]{1,0:T(8,128)(2,1)S(1)} %collective-permute-done.7.refs_1_, bf16[144,1024]{1,0:T(8,128)(2,1)S(1)} %collective-permute-done.8.refs_2_, ...), custom_call_target="tpu_custom_call" | custom-call | flops 1358954496 | bytes 8000000 | tf_op jit(solution)/shard_map/early_rows/pallas_call | solution.py:353
  62.8 0.0 collective-permute-done.6.s_ref
  62.8 2.0 %late_rows.1 = (bf16[144,1536]{1,0:T(8,128)(2,1)S(1)}, bf16[144,4,1536]{2,1,0:T(4,128)(2,1)S(1)}) custom-call(s32[3]{0:T(128)S(1)} %pad_add_fusion.scalars, bf16[144,1024]{1,0:T(8,128)(2,1)S(1)} %collective-permute-done.6.s_ref, bf16[4,144,1536]{2,1,0:T(8,128)(2,1)S(1)} %get-tuple-element.51.norm_ref, bf16[4,144,1536]{2,1,0:T(8,128)(2,1)S(1)} %copy-done, ...), custom_call_target="tpu_custom_call" | custom-call | flops 452984832 | bytes 8000000 | tf_op jit(solution)/shard_map/late_rows/pallas_call | solution.py:381
  64.8 29.4 %all_to_all.10.x_ref = bf16[16,9,4,1536]{3,2,1,0:T(4,128)(2,1)S(1)} all-to-all(bf16[16,9,4,1536]{3,2,1,0:T(4,128)(2,1)S(1)} %bitcast.11), channel_id=1, replica_groups=mesh['tm'=16,'space'=8] {'tm'}, dimensions={0} | all-to-all | bytes 3538944 | tf_op jit(solution)/shard_map/all_to_all | solution.py:510
  94.2 0.0 slice-done
  94.2 0.0 slice-done.1
  94.2 0.0 slice-done.2
  94.2 0.0 copy-start.2
  94.3 8.6 %temporal_attention.1 = bf16[16,9,4,1024]{3,2,1,0:T(4,128)(2,1)S(1)} custom-call(s32[3]{0:T(128)S(1)} %pad_add_fusion.scalars, bf16[16,9,4,1536]{3,2,1,0:T(4,128)(2,1)S(1)} %all_to_all.10.x_ref, bf16[1536,3072]{1,0:T(8,128)(2,1)S(1)} %bitcast.13), custom_call_target="tpu_custom_call" | custom-call | flops 5435817984 | bytes 14000000 | tf_op jit(solution)/shard_map/temporal_attention/pallas_call | solution.py:439
  102.9 18.4 %all_to_all.11 = bf16[16,9,4,1024]{3,2,1,0:T(4,128)(2,1)S(1)} all-to-all(bf16[16,9,4,1024]{3,2,1,0:T(4,128)(2,1)S(1)} %temporal_attention.1), channel_id=1, replica_groups=mesh['tm'=16,'space'=8] {'tm'}, dimensions={0} | all-to-all | bytes 2359296 | tf_op jit(solution)/shard_map/all_to_all | solution.py:510
  121.2 0.0 copy-done.2
  121.3 3.8 %encoded_rows.1 = bf16[4,144,1536]{2,1,0:T(8,128)(2,1)} custom-call(s32[3]{0:T(128)S(1)} %pad_add_fusion.scalars, bf16[144,4,1024]{2,1,0:T(4,128)(2,1)S(1)} %bitcast.10, bf16[4,144,1536]{2,1,0:T(8,128)(2,1)S(1)} %get-tuple-element.53.m_ref, bf16[144,1536]{1,0:T(8,128)(2,1)S(1)} %get-tuple-element.54.late_ref, bf16[1024,1536]{1,0:T(8,128)(2,1)S(1)} %copy-done.2), custom_call_target="tpu_custom_call" | custom-call | flops 1811939328 | bytes 8000000 | tf_op jit(solution)/shard_map/encoded_rows/pallas_call | solution.py:486
  (1 shorter events, 0.0 us)
Async XLA Ops:
  1.4 13.6 %collective-permute-start = (bf16[144,1536]{1,0:T(8,128)(2,1)S(1)}, bf16[144,1536]{1,0:T(8,128)(2,1)S(1)}, u32[]{:S(2)}, u32[]{:S(2)}) collective-permute-start(bf16[144,1536]{1,0:T(8,128)(2,1)S(1)} %get-tuple-element.56), channel_id=1, source_target_pairs={{0,6},{1,7},{2,0},{3,1},{4,2},{5,3},{6,4},{7,5},{8,14},{9,15},{10,... | collective-permute-start | bytes 1327112 | tf_op jit(solution)/shard_map/ppermute | solution.py:506
  5.6 12.8 %collective-permute-start.1 = (bf16[144,1536]{1,0:T(8,128)(2,1)S(1)}, bf16[144,1536]{1,0:T(8,128)(2,1)S(1)}, u32[]{:S(2)}, u32[]{:S(2)}) collective-permute-start(bf16[144,1536]{1,0:T(8,128)(2,1)S(1)} %get-tuple-element.55), channel_id=1, source_target_pairs={{0,2},{1,3},{2,4},{3,5},{4,6},{5,7},{6,0},{7,1},{8,10},{9,11},{10,... | collective-permute-start | bytes 1327112 | tf_op jit(solution)/shard_map/ppermute | solution.py:506
  18.4 12.2 %collective-permute-start.2 = (bf16[144,1536]{1,0:T(8,128)(2,1)S(1)}, bf16[144,1536]{1,0:T(8,128)(2,1)S(1)}, u32[]{:S(2)}, u32[]{:S(2)}) collective-permute-start(bf16[144,1536]{1,0:T(8,128)(2,1)S(1)} %get-tuple-element.31), channel_id=1, source_target_pairs={{0,4},{1,5},{2,6},{3,7},{4,0},{5,1},{6,2},{7,3},{8,12},{9,13},{10,... | collective-permute-start | bytes 1327112 | tf_op jit(solution)/shard_map/ppermute | solution.py:506
  18.4 17.0 %collective-permute-start.5 = (bf16[144,2048]{1,0:T(8,128)(2,1)S(1)}, bf16[144,2048]{1,0:T(8,128)(2,1)S(1)}, u32[]{:S(2)}, u32[]{:S(2)}) collective-permute-start(bf16[144,2048]{1,0:T(8,128)(2,1)S(1)} %get-tuple-element.42.refs_2_), channel_id=1, source_target_pairs={{0,1},{1,0},{2,3},{3,2},{4,5},{5,4},{6,7},{7,6},{8,9},{9,8},{10,11... | collective-permute-start | bytes 1769480 | tf_op jit(solution)/shard_map/ppermute | solution.py:526
  23.8 13.0 %collective-permute-start.3 = (bf16[288,2048]{1,0:T(8,128)(2,1)S(1)}, bf16[288,2048]{1,0:T(8,128)(2,1)S(1)}, u32[]{:S(2)}, u32[]{:S(2)}) collective-permute-start(bf16[288,2048]{1,0:T(8,128)(2,1)S(1)} %get-tuple-element.40.refs_0_), channel_id=1, source_target_pairs={{0,1},{1,0},{2,3},{3,2},{4,5},{5,4},{6,7},{7,6},{8,9},{9,8},{10,11... | collective-permute-start | bytes 3538952 | tf_op jit(solution)/shard_map/ppermute | solution.py:530
  34.5 2.3 %collective-permute-start.4 = (bf16[144,2048]{1,0:T(8,128)(2,1)S(1)}, bf16[144,2048]{1,0:T(8,128)(2,1)S(1)}, u32[]{:S(2)}, u32[]{:S(2)}) collective-permute-start(bf16[144,2048]{1,0:T(8,128)(2,1)S(1)} %get-tuple-element.41.refs_1_), channel_id=1, source_target_pairs={{0,1},{1,0},{2,3},{3,2},{4,5},{5,4},{6,7},{7,6},{8,9},{9,8},{10,11... | collective-permute-start | bytes 1769480 | tf_op jit(solution)/shard_map/ppermute | solution.py:533
  36.8 57.4 %slice-start = ((s8[9437184]{0:T(1024)(128)(4,1)}), s8[4194304]{0:T(1024)(128)(4,1)S(1)}, s32[]{:S(2)}) async-start(s8[9437184]{0:T(1024)(128)(4,1)} %bitcast.12), calls=%async_computation.2 | async-start | bytes 8388608
  44.3 11.8 %collective-permute-start.7 = (bf16[144,1024]{1,0:T(8,128)(2,1)S(1)}, bf16[144,1024]{1,0:T(8,128)(2,1)S(1)}, u32[]{:S(2)}, u32[]{:S(2)}) collective-permute-start(bf16[144,1024]{1,0:T(8,128)(2,1)S(1)} %get-tuple-element.49), channel_id=1, source_target_pairs={{0,2},{1,3},{2,4},{3,5},{4,6},{5,7},{6,0},{7,1},{8,10},{9,11},{10,... | collective-permute-start | bytes 884744 | tf_op jit(solution)/shard_map/ppermute | solution.py:506
  44.4 15.9 %collective-permute-start.8 = (bf16[144,1024]{1,0:T(8,128)(2,1)S(1)}, bf16[144,1024]{1,0:T(8,128)(2,1)S(1)}, u32[]{:S(2)}, u32[]{:S(2)}) collective-permute-start(bf16[144,1024]{1,0:T(8,128)(2,1)S(1)} %get-tuple-element.50), channel_id=1, source_target_pairs={{0,6},{1,7},{2,0},{3,1},{4,2},{5,3},{6,4},{7,5},{8,14},{9,15},{10,... | collective-permute-start | bytes 884744 | tf_op jit(solution)/shard_map/ppermute | solution.py:506
  51.8 8.5 %copy-start = (bf16[4,144,1536]{2,1,0:T(8,128)(2,1)S(1)}, bf16[4,144,1536]{2,1,0:T(8,128)(2,1)}, u32[]{:S(2)}) copy-start(bf16[4,144,1536]{2,1,0:T(8,128)(2,1)} %x_ref.1) | copy-start | bytes 5308420
  51.8 8.4 %copy-start.1 = (bf16[1024,1536]{1,0:T(8,128)(2,1)S(1)}, bf16[1024,1536]{1,0:T(8,128)(2,1)}, u32[]{:S(2)}) copy-start(bf16[1024,1536]{1,0:T(8,128)(2,1)} %w_ref.7) | copy-start | bytes 9437188
  51.8 42.4 %slice-start.1 = ((s8[9437184]{0:T(1024)(128)(4,1)}), s8[4194304]{0:T(1024)(128)(4,1)S(1)}, s32[]{:S(2)}) async-start(s8[9437184]{0:T(1024)(128)(4,1)} %bitcast.12), calls=%async_computation.3 | async-start | bytes 8388608
  51.8 11.0 %collective-permute-start.6 = (bf16[144,1024]{1,0:T(8,128)(2,1)S(1)}, bf16[144,1024]{1,0:T(8,128)(2,1)S(1)}, u32[]{:S(2)}, u32[]{:S(2)}) collective-permute-start(bf16[144,1024]{1,0:T(8,128)(2,1)S(1)} %spatial_attention.4), channel_id=1, source_target_pairs={{0,4},{1,5},{2,6},{3,7},{4,0},{5,1},{6,2},{7,3},{8,12},{9,13},{10,... | collective-permute-start | bytes 884744 | tf_op jit(solution)/shard_map/ppermute | solution.py:506
  56.1 38.1 %slice-start.2 = ((s8[9437184]{0:T(1024)(128)(4,1)}), s8[1048576]{0:T(1024)(128)(4,1)S(1)}, s32[]{:S(2)}) async-start(s8[9437184]{0:T(1024)(128)(4,1)} %bitcast.12), calls=%async_computation.4 | async-start | bytes 2097152
  94.2 27.0 %copy-start.2 = (bf16[1024,1536]{1,0:T(8,128)(2,1)S(1)}, bf16[1024,1536]{1,0:T(8,128)(2,1)}, u32[]{:S(2)}) copy-start(bf16[1024,1536]{1,0:T(8,128)(2,1)} %w_ref.9) | copy-start | bytes 9437188

commit v7 on v6

--- a/solution.py
+++ b/solution.py
@@ -108,7 +108,7 @@
 
 
 def near_kernel(count, *refs):
-    x_refs, (w_ref, kv_ref, q_ref, norm_ref, held, sem) = refs[:count], refs[count:]
+    x_refs, (w_ref, kv_ref, q_ref, held, norm_ref, sem) = refs[:count], refs[count:]
 
     def fetch(j):
         return pltpu.make_async_copy(w_ref.at[:, block(j)], held.at[:, block(j)], sem.at[j])
@@ -152,14 +152,14 @@
     return pl.pallas_call(
         functools.partial(near_kernel, count),
         in_specs=[whole] * count + [pl.BlockSpec(memory_space=pltpu.HBM)],
-        out_specs=[whole, whole],
+        out_specs=[whole, whole, whole],
         out_shape=[
             jax.ShapeDtypeStruct((rows, 2 * HW), BF),
             jax.ShapeDtypeStruct((count, 144, HW), BF),
+            jax.ShapeDtypeStruct((WIDTH, 3 * HW), BF),
         ],
         scratch_shapes=[
             pltpu.VMEM((rows, WIDTH), BF),
-            pltpu.VMEM((WIDTH, 3 * HW), BF),
             pltpu.SemaphoreType.DMA((6,)),
         ],
         compiler_params=params(24),
@@ -168,25 +168,15 @@
     )(*blocks, pltpu.with_memory_space_constraint(w, pltpu.HBM))
 
 
-def kv_kernel(x_ref, w_ref, kv_ref, norm_ref, wq_ref, wkv, sem):
-    def fetch(j):
-        source = pl.ds(pl.multiple_of(j * 512 + HW, 128), 512)
-        return pltpu.make_async_copy(w_ref.at[:, source], wkv.at[:, block(j)], sem.at[j])
-
-    for j in range(4):
-        fetch(j).start()
-    for_queries = pltpu.make_async_copy(w_ref.at[:, :HW], wq_ref, sem.at[4])
-    for_queries.start()
+def kv_kernel(x_ref, w_ref, kv_ref, norm_ref):
     normalise_blocks([x_ref], norm_ref)
 
     def step(j, carry):
-        fetch(j).wait()
-        y = jnp.dot(norm_ref[...], wkv[:, block(j)], preferred_element_type=F32)
+        y = jnp.dot(norm_ref[...], w_ref[:, block(j + 2)], preferred_element_type=F32)
         kv_ref[:, block(j)] = y.astype(BF)
         return carry
 
     lax.fori_loop(0, 4, step, 0, unroll=4)
-    for_queries.wait()
 
 
 def keys_values(x, w):
@@ -194,18 +184,16 @@
     whole = pl.BlockSpec(memory_space=pltpu.VMEM)
     return pl.pallas_call(
         kv_kernel,
-        in_specs=[whole, pl.BlockSpec(memory_space=pltpu.HBM)],
-        out_specs=[whole, whole, whole],
+        in_specs=[whole, whole],
+        out_specs=[whole, whole],
         out_shape=[
             jax.ShapeDtypeStruct((rows, 2 * HW), BF),
             jax.ShapeDtypeStruct((rows, WIDTH), BF),
-            jax.ShapeDtypeStruct((WIDTH, HW), BF),
-        ],
-        scratch_shapes=[pltpu.VMEM((WIDTH, 2 * HW), BF), pltpu.SemaphoreType.DMA((5,))],
-        compiler_params=params(24),
+        ],
+        compiler_params=params(16),
         cost_estimate=HEAVY,
         name="keys_values",
-    )(x, pltpu.with_memory_space_constraint(w, pltpu.HBM))
+    )(x, w)
 
 
 def q_kernel(norm_ref, w_ref, q_ref):
@@ -526,12 +514,12 @@
     kv_own_other = lax.ppermute(kv_own, "space", SWAP)
     late, kv_own, *near = lax.optimization_barrier((sent[2], kv_own, *near))
     far = from_chip(2, late)
-    kv_near, q_near = near_blocks(near, qkv_space)
+    kv_near, q_near, w_held = near_blocks(near, qkv_space)
     kv_near_other = lax.ppermute(kv_near, "space", SWAP)
     far, kv_near = lax.optimization_barrier((far, kv_near))
-    kv_far, norm1, w_q = keys_values(far, qkv_space)
+    kv_far, norm1 = keys_values(far, w_held)
     kv_far_other = lax.ppermute(kv_far, "space", SWAP)
-    q_far = queries(norm1, w_q)
+    q_far = queries(norm1, w_held)
     kvs = (kv_near, kv_far, kv_own, kv_near_other, kv_far_other, kv_own_other)
     back = {}
     for blocks in ((1, 3), (2,)):

time: 126 us -> 124 us (0.984)
  Pallas kernels: 47.6 us -> 45.1 us
    pallas_call x1, Pallas kernels: 3.89 us -> 1.33 us  [keys_values(): pl.pallas_call(kv_kernel, in_specs=[whole, whole], out_specs=[whole, whol...]
  transfers between devices with their start and end apart: 9 -> 9, of which waited for: 5 -> 5; matrix products, arithmetic and copies ran while one was open for 0% -> 0% of each run, Pallas kernels for 21% -> 19%
where the time goes in v7:
time: 124 us; the launch traced here: 123 us
  blocking collectives  47.8 us (39%)
  Pallas kernels  45.1 us (36%)
  waiting for transfers between devices  19 us (15%)
  starting transfers between devices  8.45 us (7%)
  local copies, waits for them, and re-layouts  1.41 us (1%)
    all_to_all x2, blocking collectives, over_tm(): return lax.all_to_all(x, 'tm', split_axis=0, concat_axis=0, tiled=True)  47.8 us
    ppermute x6, waiting for transfers between devices, along_z(): return lax.ppermute(x, 'space', pairs)  17.6 us
    pallas_call x3, Pallas kernels, spatial_attention(): pl.pallas_call(functools.partial(spatial_kernel, which), in_specs=[whole]...  15.8 us
    pallas_call x1, Pallas kernels, temporal_attention(): pl.pallas_call(functools.partial(temporal_kernel, n), in_specs=[pl.BlockS...  8.73 us
    ppermute x6, starting transfers between devices, along_z(): return lax.ppermute(x, 'space', pairs)  7.58 us
    pallas_call x1, Pallas kernels, near_blocks(): pl.pallas_call(functools.partial(near_kernel, count), in_specs=[whole] *...  5.23 us
    pallas_call x1, Pallas kernels, own_block(): pl.pallas_call(own_kernel, in_specs=[pl.BlockSpec(memory_space=pltpu.SMEM...  4.95 us
    pallas_call x1, Pallas kernels, encoded_rows(): pl.pallas_call(functools.partial(encoded_kernel, distance), in_specs=[pl....  3.79 us
  transfers between devices with their start and end apart: 9, of which 5 were waited for; matrix products, arithmetic and copies ran while one was open for 0% of the time, Pallas kernels for 19%

profile of v7, /device:TPU:0, one launch (start us, length us, event | category | flops | bytes accessed | tf_op | source)
XLA Modules:
  0.0 122.8 jit_solution(9376594949154195617)
XLA Ops:
  0.0 1.4 %dynamic-slice_bitcast_fusion = (bf16[144,1536]{1,0:T(8,128)(2,1)S(1)}, bf16[144,1536]{1,0:T(8,128)(2,1)S(1)}, bf16[144,1536]{1,0:T(8,128)(2,1)S(1)}) fusion(bf16[4,144,1536]{2,1,0:T(8,128)(2,1)} %x_ref.1, s32[]{:T(128)S(6)} %select_n.18, s32[]{:T(128)S(6)} %select_n.17, s32[]{:T(128)S(6)} %select_n.16), kind=kLoop, calls=%fused_computation | loop fusion | bytes 2654220 | tf_op jit(solution)/shard_map/jit(dynamic_index_in_dim)/squeeze | solution.py:510
  1.4 4.2 %collective-permute-start = (bf16[144,1536]{1,0:T(8,128)(2,1)S(1)}, bf16[144,1536]{1,0:T(8,128)(2,1)S(1)}, u32[]{:S(2)}, u32[]{:S(2)}) collective-permute-start(bf16[144,1536]{1,0:T(8,128)(2,1)S(1)} %get-tuple-element.56), channel_id=1, source_target_pairs={{0,6},{1,7},{2,0},{3,1},{4,2},{5,3},{6,4},{7,5},{8,14},{9,15},{10,... | collective-permute-start | bytes 1327112 | tf_op jit(solution)/shard_map/ppermute | solution.py:494
  5.6 0.0 collective-permute-start.1
  6.2 0.1 pad_add_fusion.scalars
  6.3 5.0 %own_block.1 = (bf16[144,2048]{1,0:T(8,128)(2,1)S(1)}, bf16[1,144,1024]{2,1,0:T(8,128)(2,1)S(1)}) custom-call(s32[3]{0:T(128)S(1)} %pad_add_fusion.scalars, bf16[4,144,1536]{2,1,0:T(8,128)(2,1)} %x_ref.1, bf16[1536,3072]{1,0:T(8,128)(2,1)} %refs_2_.1), custom_call_target="tpu_custom_call" | custom-call | flops 100000000 | bytes 1000000 | tf_op jit(solution)/shard_map/own_block/pallas_call | solution.py:86
  11.3 3.7 %collective-permute-done.refs_0_ = bf16[144,1536]{1,0:T(8,128)(2,1)S(1)} collective-permute-done((bf16[144,1536]{1,0:T(8,128)(2,1)S(1)}, bf16[144,1536]{1,0:T(8,128)(2,1)S(1)}, u32[]{:S(2)}, u32[]{:S(2)}) %collective-permute-start) | collective-permute-done | bytes 442400 | tf_op jit(solution)/shard_map/ppermute | solution.py:494
  15.0 3.4 %collective-permute-done.1.refs_1_ = bf16[144,1536]{1,0:T(8,128)(2,1)S(1)} collective-permute-done((bf16[144,1536]{1,0:T(8,128)(2,1)S(1)}, bf16[144,1536]{1,0:T(8,128)(2,1)S(1)}, u32[]{:S(2)}, u32[]{:S(2)}) %collective-permute-start.1) | collective-permute-done | bytes 442400 | tf_op jit(solution)/shard_map/ppermute | solution.py:494
  18.4 0.0 collective-permute-start.2
  18.4 0.0 collective-permute-start.5
  18.4 5.2 %near_blocks.1 = (bf16[288,2048]{1,0:T(8,128)(2,1)S(1)}, bf16[2,144,1024]{2,1,0:T(8,128)(2,1)S(1)}, bf16[1536,3072]{1,0:T(8,128)(2,1)S(1)}) custom-call(bf16[144,1536]{1,0:T(8,128)(2,1)S(1)} %collective-permute-done.refs_0_, bf16[144,1536]{1,0:T(8,128)(2,1)S(1)} %collective-permute-done.1.refs_1_, bf16[1536,3072]{1,0:T(8,128)(2,1)} %refs_2_.1), custom_call_target="tpu_custom_call" | custom-call | flops 100000000 | bytes 1000000 | tf_op jit(solution)/shard_map/near_blocks/pallas_call | solution.py:152
  23.7 0.6 collective-permute-start.3
  24.3 6.4 %collective-permute-done.2.x_ref = bf16[144,1536]{1,0:T(8,128)(2,1)S(1)} collective-permute-done((bf16[144,1536]{1,0:T(8,128)(2,1)S(1)}, bf16[144,1536]{1,0:T(8,128)(2,1)S(1)}, u32[]{:S(2)}, u32[]{:S(2)}) %collective-permute-start.2) | collective-permute-done | bytes 442400 | tf_op jit(solution)/shard_map/ppermute | solution.py:494
  30.6 1.3 %keys_values.1 = (bf16[144,2048]{1,0:T(8,128)(2,1)S(1)}, bf16[144,1536]{1,0:T(8,128)(2,1)S(1)}) custom-call(bf16[144,1536]{1,0:T(8,128)(2,1)S(1)} %collective-permute-done.2.x_ref, bf16[1536,3072]{1,0:T(8,128)(2,1)S(1)} %get-tuple-element.36.w_ref), custom_call_target="tpu_custom_call" | custom-call | flops 20000000000 | bytes 1000000 | tf_op jit(solution)/shard_map/keys_values/pallas_call | solution.py:185
  32.0 0.3 collective-permute-start.4
  32.2 0.6 queries.1.q_ref
  32.9 0.0 collective-permute-done.5.refs_5_
  32.9 1.3 %collective-permute-done.4.refs_4_ = bf16[144,2048]{1,0:T(8,128)(2,1)S(1)} collective-permute-done((bf16[144,2048]{1,0:T(8,128)(2,1)S(1)}, bf16[144,2048]{1,0:T(8,128)(2,1)S(1)}, u32[]{:S(2)}, u32[]{:S(2)}) %collective-permute-start.4) | collective-permute-done | bytes 589856 | tf_op jit(solution)/shard_map/ppermute | solution.py:521
  34.2 0.0 collective-permute-done.3.refs_3_
  34.2 0.0 slice-start
  34.2 7.5 %spatial_attention.3 = (bf16[144,1024]{1,0:T(8,128)(2,1)S(1)}, bf16[144,1024]{1,0:T(8,128)(2,1)S(1)}) custom-call(bf16[2,144,1024]{2,1,0:T(8,128)(2,1)S(1)} %get-tuple-element.39.q_ref, bf16[288,2048]{1,0:T(8,128)(2,1)S(1)} %get-tuple-element.40.refs_0_, bf16[144,2048]{1,0:T(8,128)(2,1)S(1)} %get-tuple-element.41.refs_1_, ...), custom_call_target="tpu_custom_call" | custom-call | flops 339738624 | bytes 1000000 | tf_op jit(solution)/shard_map/spatial_attention/pallas_call | solution.py:294
  41.7 0.1 collective-permute-start.7
  41.8 3.2 %collective-permute-start.8 = (bf16[144,1024]{1,0:T(8,128)(2,1)S(1)}, bf16[144,1024]{1,0:T(8,128)(2,1)S(1)}, u32[]{:S(2)}, u32[]{:S(2)}) collective-permute-start(bf16[144,1024]{1,0:T(8,128)(2,1)S(1)} %get-tuple-element.50), channel_id=1, source_target_pairs={{0,6},{1,7},{2,0},{3,1},{4,2},{5,3},{6,4},{7,5},{8,14},{9,15},{10,... | collective-permute-start | bytes 884744 | tf_op jit(solution)/shard_map/ppermute | solution.py:494
  45.0 4.2 %spatial_attention.4 = bf16[144,1024]{1,0:T(8,128)(2,1)S(1)} custom-call(bf16[1,144,1024]{2,1,0:T(8,128)(2,1)S(1)} %queries.1.q_ref, bf16[288,2048]{1,0:T(8,128)(2,1)S(1)} %get-tuple-element.40.refs_0_, bf16[144,2048]{1,0:T(8,128)(2,1)S(1)} %get-tuple-element.41.refs_1_, bf16[144,2048]{1,0:T(8,128)(2,1)S(1)} %get-tuple-element.42.refs_2_, ...), custom_call_target="tpu_custom_call" | custom-call | flops 169869312 | bytes 1000000 | tf_op jit(solution)/shard_map/spatial_attention/pallas_call | solution.py:294
  49.2 0.0 copy-start
  49.2 0.0 copy-start.1
  49.2 0.0 slice-start.1
  49.3 0.1 collective-permute-start.6
  49.4 4.2 %spatial_attention.5.refs_0_ = bf16[144,1024]{1,0:T(8,128)(2,1)S(1)} custom-call(bf16[1,144,1024]{2,1,0:T(8,128)(2,1)S(1)} %get-tuple-element.48.q_ref, bf16[288,2048]{1,0:T(8,128)(2,1)S(1)} %get-tuple-element.40.refs_0_, bf16[144,2048]{1,0:T(8,128)(2,1)S(1)} %get-tuple-element.41.refs_1_, bf16[144,2048]{1,0:T(8,128)(2,1)S(1)} %get-tuple-element.42.refs_2_, ...), custom_call_target="tpu_custom_call" | custom-call | flops 169869312 | bytes 1000000 | tf_op jit(solution)/shard_map/spatial_attention/pallas_call | solution.py:294
  53.5 0.0 slice-start.2
  53.5 0.0 collective-permute-done.7.refs_1_
  53.6 4.1 %collective-permute-done.8.refs_2_ = bf16[144,1024]{1,0:T(8,128)(2,1)S(1)} collective-permute-done((bf16[144,1024]{1,0:T(8,128)(2,1)S(1)}, bf16[144,1024]{1,0:T(8,128)(2,1)S(1)}, u32[]{:S(2)}, u32[]{:S(2)}) %collective-permute-start.8) | collective-permute-done | bytes 294944 | tf_op jit(solution)/shard_map/ppermute | solution.py:494
  57.7 0.0 copy-done
  57.7 0.0 copy-done.1
  57.7 2.6 %early_rows.1 = (bf16[4,144,1536]{2,1,0:T(8,128)(2,1)S(1)}, bf16[4,144,1536]{2,1,0:T(8,128)(2,1)S(1)}) custom-call(s32[3]{0:T(128)S(1)} %pad_add_fusion.scalars, bf16[144,1024]{1,0:T(8,128)(2,1)S(1)} %spatial_attention.5.refs_0_, bf16[144,1024]{1,0:T(8,128)(2,1)S(1)} %collective-permute-done.7.refs_1_, bf16[144,1024]{1,0:T(8,128)(2,1)S(1)} %collective-permute-done.8.refs_2_, ...), custom_call_target="tpu_custom_call" | custom-call | flops 1358954496 | bytes 8000000 | tf_op jit(solution)/shard_map/early_rows/pallas_call | solution.py:341
  60.3 0.0 collective-permute-done.6.s_ref
  60.3 2.0 %late_rows.1 = (bf16[144,1536]{1,0:T(8,128)(2,1)S(1)}, bf16[144,4,1536]{2,1,0:T(4,128)(2,1)S(1)}) custom-call(s32[3]{0:T(128)S(1)} %pad_add_fusion.scalars, bf16[144,1024]{1,0:T(8,128)(2,1)S(1)} %collective-permute-done.6.s_ref, bf16[4,144,1536]{2,1,0:T(8,128)(2,1)S(1)} %get-tuple-element.51.norm_ref, bf16[4,144,1536]{2,1,0:T(8,128)(2,1)S(1)} %copy-done, ...), custom_call_target="tpu_custom_call" | custom-call | flops 452984832 | bytes 8000000 | tf_op jit(solution)/shard_map/late_rows/pallas_call | solution.py:369
  62.3 29.4 %all_to_all.10.x_ref = bf16[16,9,4,1536]{3,2,1,0:T(4,128)(2,1)S(1)} all-to-all(bf16[16,9,4,1536]{3,2,1,0:T(4,128)(2,1)S(1)} %bitcast.11), channel_id=1, replica_groups=mesh['tm'=16,'space'=8] {'tm'}, dimensions={0} | all-to-all | bytes 3538944 | tf_op jit(solution)/shard_map/all_to_all | solution.py:498
  91.7 0.0 slice-done
  91.7 0.0 slice-done.1
  91.7 0.0 slice-done.2
  91.7 0.0 copy-start.2
  91.7 8.7 %temporal_attention.1 = bf16[16,9,4,1024]{3,2,1,0:T(4,128)(2,1)S(1)} custom-call(s32[3]{0:T(128)S(1)} %pad_add_fusion.scalars, bf16[16,9,4,1536]{3,2,1,0:T(4,128)(2,1)S(1)} %all_to_all.10.x_ref, bf16[1536,3072]{1,0:T(8,128)(2,1)S(1)} %bitcast.13), custom_call_target="tpu_custom_call" | custom-call | flops 5435817984 | bytes 14000000 | tf_op jit(solution)/shard_map/temporal_attention/pallas_call | solution.py:427
  100.4 18.4 %all_to_all.11 = bf16[16,9,4,1024]{3,2,1,0:T(4,128)(2,1)S(1)} all-to-all(bf16[16,9,4,1024]{3,2,1,0:T(4,128)(2,1)S(1)} %temporal_attention.1), channel_id=1, replica_groups=mesh['tm'=16,'space'=8] {'tm'}, dimensions={0} | all-to-all | bytes 2359296 | tf_op jit(solution)/shard_map/all_to_all | solution.py:498
  118.8 0.0 copy-done.2
  118.8 3.8 %encoded_rows.1 = bf16[4,144,1536]{2,1,0:T(8,128)(2,1)} custom-call(s32[3]{0:T(128)S(1)} %pad_add_fusion.scalars, bf16[144,4,1024]{2,1,0:T(4,128)(2,1)S(1)} %bitcast.10, bf16[4,144,1536]{2,1,0:T(8,128)(2,1)S(1)} %get-tuple-element.53.m_ref, bf16[144,1536]{1,0:T(8,128)(2,1)S(1)} %get-tuple-element.54.late_ref, bf16[1024,1536]{1,0:T(8,128)(2,1)S(1)} %copy-done.2), custom_call_target="tpu_custom_call" | custom-call | flops 1811939328 | bytes 8000000 | tf_op jit(solution)/shard_map/encoded_rows/pallas_call | solution.py:474
  (1 shorter events, 0.0 us)
Async XLA Ops:
  1.4 13.6 %collective-permute-start = (bf16[144,1536]{1,0:T(8,128)(2,1)S(1)}, bf16[144,1536]{1,0:T(8,128)(2,1)S(1)}, u32[]{:S(2)}, u32[]{:S(2)}) collective-permute-start(bf16[144,1536]{1,0:T(8,128)(2,1)S(1)} %get-tuple-element.56), channel_id=1, source_target_pairs={{0,6},{1,7},{2,0},{3,1},{4,2},{5,3},{6,4},{7,5},{8,14},{9,15},{10,... | collective-permute-start | bytes 1327112 | tf_op jit(solution)/shard_map/ppermute | solution.py:494
  5.6 12.8 %collective-permute-start.1 = (bf16[144,1536]{1,0:T(8,128)(2,1)S(1)}, bf16[144,1536]{1,0:T(8,128)(2,1)S(1)}, u32[]{:S(2)}, u32[]{:S(2)}) collective-permute-start(bf16[144,1536]{1,0:T(8,128)(2,1)S(1)} %get-tuple-element.55), channel_id=1, source_target_pairs={{0,2},{1,3},{2,4},{3,5},{4,6},{5,7},{6,0},{7,1},{8,10},{9,11},{10,... | collective-permute-start | bytes 1327112 | tf_op jit(solution)/shard_map/ppermute | solution.py:494
  18.4 12.2 %collective-permute-start.2 = (bf16[144,1536]{1,0:T(8,128)(2,1)S(1)}, bf16[144,1536]{1,0:T(8,128)(2,1)S(1)}, u32[]{:S(2)}, u32[]{:S(2)}) collective-permute-start(bf16[144,1536]{1,0:T(8,128)(2,1)S(1)} %get-tuple-element.31), channel_id=1, source_target_pairs={{0,4},{1,5},{2,6},{3,7},{4,0},{5,1},{6,2},{7,3},{8,12},{9,13},{10,... | collective-permute-start | bytes 1327112 | tf_op jit(solution)/shard_map/ppermute | solution.py:494
  18.4 14.5 %collective-permute-start.5 = (bf16[144,2048]{1,0:T(8,128)(2,1)S(1)}, bf16[144,2048]{1,0:T(8,128)(2,1)S(1)}, u32[]{:S(2)}, u32[]{:S(2)}) collective-permute-start(bf16[144,2048]{1,0:T(8,128)(2,1)S(1)} %get-tuple-element.42.refs_2_), channel_id=1, source_target_pairs={{0,1},{1,0},{2,3},{3,2},{4,5},{5,4},{6,7},{7,6},{8,9},{9,8},{10,11... | collective-permute-start | bytes 1769480 | tf_op jit(solution)/shard_map/ppermute | solution.py:514
  23.7 10.6 %collective-permute-start.3 = (bf16[288,2048]{1,0:T(8,128)(2,1)S(1)}, bf16[288,2048]{1,0:T(8,128)(2,1)S(1)}, u32[]{:S(2)}, u32[]{:S(2)}) collective-permute-start(bf16[288,2048]{1,0:T(8,128)(2,1)S(1)} %get-tuple-element.40.refs_0_), channel_id=1, source_target_pairs={{0,1},{1,0},{2,3},{3,2},{4,5},{5,4},{6,7},{7,6},{8,9},{9,8},{10,11... | collective-permute-start | bytes 3538952 | tf_op jit(solution)/shard_map/ppermute | solution.py:518
  32.0 2.3 %collective-permute-start.4 = (bf16[144,2048]{1,0:T(8,128)(2,1)S(1)}, bf16[144,2048]{1,0:T(8,128)(2,1)S(1)}, u32[]{:S(2)}, u32[]{:S(2)}) collective-permute-start(bf16[144,2048]{1,0:T(8,128)(2,1)S(1)} %get-tuple-element.41.refs_1_), channel_id=1, source_target_pairs={{0,1},{1,0},{2,3},{3,2},{4,5},{5,4},{6,7},{7,6},{8,9},{9,8},{10,11... | collective-permute-start | bytes 1769480 | tf_op jit(solution)/shard_map/ppermute | solution.py:521
  34.2 57.4 %slice-start = ((s8[9437184]{0:T(1024)(128)(4,1)}), s8[4194304]{0:T(1024)(128)(4,1)S(1)}, s32[]{:S(2)}) async-start(s8[9437184]{0:T(1024)(128)(4,1)} %bitcast.12), calls=%async_computation.2 | async-start | bytes 8388608
  41.7 11.8 %collective-permute-start.7 = (bf16[144,1024]{1,0:T(8,128)(2,1)S(1)}, bf16[144,1024]{1,0:T(8,128)(2,1)S(1)}, u32[]{:S(2)}, u32[]{:S(2)}) collective-permute-start(bf16[144,1024]{1,0:T(8,128)(2,1)S(1)} %get-tuple-element.49), channel_id=1, source_target_pairs={{0,2},{1,3},{2,4},{3,5},{4,6},{5,7},{6,0},{7,1},{8,10},{9,11},{10,... | collective-permute-start | bytes 884744 | tf_op jit(solution)/shard_map/ppermute | solution.py:494
  41.8 15.9 %collective-permute-start.8 = (bf16[144,1024]{1,0:T(8,128)(2,1)S(1)}, bf16[144,1024]{1,0:T(8,128)(2,1)S(1)}, u32[]{:S(2)}, u32[]{:S(2)}) collective-permute-start(bf16[144,1024]{1,0:T(8,128)(2,1)S(1)} %get-tuple-element.50), channel_id=1, source_target_pairs={{0,6},{1,7},{2,0},{3,1},{4,2},{5,3},{6,4},{7,5},{8,14},{9,15},{10,... | collective-permute-start | bytes 884744 | tf_op jit(solution)/shard_map/ppermute | solution.py:494
  49.2 8.5 %copy-start = (bf16[4,144,1536]{2,1,0:T(8,128)(2,1)S(1)}, bf16[4,144,1536]{2,1,0:T(8,128)(2,1)}, u32[]{:S(2)}) copy-start(bf16[4,144,1536]{2,1,0:T(8,128)(2,1)} %x_ref.1) | copy-start | bytes 5308420
  49.2 8.5 %copy-start.1 = (bf16[1024,1536]{1,0:T(8,128)(2,1)S(1)}, bf16[1024,1536]{1,0:T(8,128)(2,1)}, u32[]{:S(2)}) copy-start(bf16[1024,1536]{1,0:T(8,128)(2,1)} %w_ref.5) | copy-start | bytes 9437188
  49.2 42.4 %slice-start.1 = ((s8[9437184]{0:T(1024)(128)(4,1)}), s8[4194304]{0:T(1024)(128)(4,1)S(1)}, s32[]{:S(2)}) async-start(s8[9437184]{0:T(1024)(128)(4,1)} %bitcast.12), calls=%async_computation.3 | async-start | bytes 8388608
  49.3 11.0 %collective-permute-start.6 = (bf16[144,1024]{1,0:T(8,128)(2,1)S(1)}, bf16[144,1024]{1,0:T(8,128)(2,1)S(1)}, u32[]{:S(2)}, u32[]{:S(2)}) collective-permute-start(bf16[144,1024]{1,0:T(8,128)(2,1)S(1)} %spatial_attention.4), channel_id=1, source_target_pairs={{0,4},{1,5},{2,6},{3,7},{4,0},{5,1},{6,2},{7,3},{8,12},{9,13},{10,... | collective-permute-start | bytes 884744 | tf_op jit(solution)/shard_map/ppermute | solution.py:494
  53.5 38.1 %slice-start.2 = ((s8[9437184]{0:T(1024)(128)(4,1)}), s8[1048576]{0:T(1024)(128)(4,1)S(1)}, s32[]{:S(2)}) async-start(s8[9437184]{0:T(1024)(128)(4,1)} %bitcast.12), calls=%async_computation.4 | async-start | bytes 2097152
  91.7 27.1 %copy-start.2 = (bf16[1024,1536]{1,0:T(8,128)(2,1)S(1)}, bf16[1024,1536]{1,0:T(8,128)(2,1)}, u32[]{:S(2)}) copy-start(bf16[1024,1536]{1,0:T(8,128)(2,1)} %w_ref.7) | copy-start | bytes 9437188

commit v8 on v7

--- a/solution.py
+++ b/solution.py
@@ -288,7 +288,7 @@
 
 def spatial_attention(q, kvs, which):
     rows, total, count = q.shape[1], sum(kv.shape[0] for kv in kvs), len(which)
-    width = 4 // count
+    width = 4
     heads = 2 * width * count
     whole = pl.BlockSpec(memory_space=pltpu.VMEM)
     return pl.pallas_call(
@@ -299,7 +299,7 @@
         scratch_shapes=[pltpu.VMEM((width, total, 128), BF), pltpu.VMEM((width, total, 256), BF)]
         + [pltpu.VMEM((heads, rows, total), F32)] * 2
         + [pltpu.VMEM((heads, rows, 128), F32)] * 2,
-        compiler_params=params(24),
+        compiler_params=params(36),
         cost_estimate=pl.CostEstimate(
             flops=count * rows * total * HW,
             bytes_accessed=1_000_000,
@@ -450,11 +450,11 @@
     first, limit = scalars[0], scalars[1]
 
     def leave(j):
-        cols = pl.ds(pl.multiple_of(j * 512, 128), 512)
+        cols = pl.ds(pl.multiple_of(j * 256, 128), 256)
         return pltpu.make_async_copy(held.at[:, :, cols], o_ref.at[:, :, cols], sem.at[j])
 
     def project(j, carry):
-        cols = pl.ds(pl.multiple_of(j * 512, 128), 512)
+        cols = pl.ds(pl.multiple_of(j * 256, 128), 256)
         branch = jnp.dot(rows_ref[...], w_ref[:, cols], preferred_element_type=F32)
         for f in range(4):
             valid = (first + f < limit).astype(F32)
@@ -464,8 +464,8 @@
         leave(j).start()
         return carry
 
-    lax.fori_loop(0, 3, project, 0, unroll=3)
-    for j in range(3):
+    lax.fori_loop(0, 6, project, 0, unroll=3)
+    for j in range(6):
         leave(j).wait()
 
 
@@ -479,7 +479,7 @@
         scratch_shapes=[
             pltpu.VMEM((4 * 144, HW), BF),
             pltpu.VMEM((4, 144, WIDTH), BF),
-            pltpu.SemaphoreType.DMA((3,)),
+            pltpu.SemaphoreType.DMA((6,)),
         ],
         compiler_params=params(24),
         cost_estimate=pl.CostEstimate(

time: 124 us -> 124 us (level)
  no operation moved by 1% of the time
where the time goes in v8:
time: 124 us; the launch traced here: 123 us
  blocking collectives  47.8 us (39%)
  Pallas kernels  45.3 us (37%)
  waiting for transfers between devices  19 us (15%)
  starting transfers between devices  8.45 us (7%)
  local copies, waits for them, and re-layouts  1.41 us (1%)
    all_to_all x2, blocking collectives, over_tm(): return lax.all_to_all(x, 'tm', split_axis=0, concat_axis=0, tiled=True)  47.8 us
    ppermute x6, waiting for transfers between devices, along_z(): return lax.ppermute(x, 'space', pairs)  17.7 us
    pallas_call x3, Pallas kernels, spatial_attention(): pl.pallas_call(functools.partial(spatial_kernel, which), in_specs=[whole]...  15.9 us
    pallas_call x1, Pallas kernels, temporal_attention(): pl.pallas_call(functools.partial(temporal_kernel, n), in_specs=[pl.BlockS...  8.6 us
    ppermute x6, starting transfers between devices, along_z(): return lax.ppermute(x, 'space', pairs)  7.58 us
    pallas_call x1, Pallas kernels, near_blocks(): pl.pallas_call(functools.partial(near_kernel, count), in_specs=[whole] *...  5.23 us
    pallas_call x1, Pallas kernels, own_block(): pl.pallas_call(own_kernel, in_specs=[pl.BlockSpec(memory_space=pltpu.SMEM...  4.95 us
    pallas_call x1, Pallas kernels, encoded_rows(): pl.pallas_call(functools.partial(encoded_kernel, distance), in_specs=[pl....  4.08 us
  transfers between devices with their start and end apart: 9, of which 5 were waited for; matrix products, arithmetic and copies ran while one was open for 0% of the time, Pallas kernels for 19%

profile of v8, /device:TPU:0, one launch (start us, length us, event | category | flops | bytes accessed | tf_op | source)
XLA Modules:
  0.0 123.1 jit_solution(9090246079075013064)
XLA Ops:
  0.0 1.4 %dynamic-slice_bitcast_fusion = (bf16[144,1536]{1,0:T(8,128)(2,1)S(1)}, bf16[144,1536]{1,0:T(8,128)(2,1)S(1)}, bf16[144,1536]{1,0:T(8,128)(2,1)S(1)}) fusion(bf16[4,144,1536]{2,1,0:T(8,128)(2,1)} %x_ref.1, s32[]{:T(128)S(6)} %select_n.18, s32[]{:T(128)S(6)} %select_n.17, s32[]{:T(128)S(6)} %select_n.16), kind=kLoop, calls=%fused_computation | loop fusion | bytes 2654220 | tf_op jit(solution)/shard_map/jit(dynamic_index_in_dim)/squeeze | solution.py:510
  1.4 4.2 %collective-permute-start = (bf16[144,1536]{1,0:T(8,128)(2,1)S(1)}, bf16[144,1536]{1,0:T(8,128)(2,1)S(1)}, u32[]{:S(2)}, u32[]{:S(2)}) collective-permute-start(bf16[144,1536]{1,0:T(8,128)(2,1)S(1)} %get-tuple-element.56), channel_id=1, source_target_pairs={{0,6},{1,7},{2,0},{3,1},{4,2},{5,3},{6,4},{7,5},{8,14},{9,15},{10,... | collective-permute-start | bytes 1327112 | tf_op jit(solution)/shard_map/ppermute | solution.py:494
  5.6 0.0 collective-permute-start.1
  6.2 0.1 pad_add_fusion.scalars
  6.3 5.0 %own_block.1 = (bf16[144,2048]{1,0:T(8,128)(2,1)S(1)}, bf16[1,144,1024]{2,1,0:T(8,128)(2,1)S(1)}) custom-call(s32[3]{0:T(128)S(1)} %pad_add_fusion.scalars, bf16[4,144,1536]{2,1,0:T(8,128)(2,1)} %x_ref.1, bf16[1536,3072]{1,0:T(8,128)(2,1)} %refs_2_.1), custom_call_target="tpu_custom_call" | custom-call | flops 100000000 | bytes 1000000 | tf_op jit(solution)/shard_map/own_block/pallas_call | solution.py:86
  11.3 3.7 %collective-permute-done.refs_0_ = bf16[144,1536]{1,0:T(8,128)(2,1)S(1)} collective-permute-done((bf16[144,1536]{1,0:T(8,128)(2,1)S(1)}, bf16[144,1536]{1,0:T(8,128)(2,1)S(1)}, u32[]{:S(2)}, u32[]{:S(2)}) %collective-permute-start) | collective-permute-done | bytes 442400 | tf_op jit(solution)/shard_map/ppermute | solution.py:494
  15.0 3.4 %collective-permute-done.1.refs_1_ = bf16[144,1536]{1,0:T(8,128)(2,1)S(1)} collective-permute-done((bf16[144,1536]{1,0:T(8,128)(2,1)S(1)}, bf16[144,1536]{1,0:T(8,128)(2,1)S(1)}, u32[]{:S(2)}, u32[]{:S(2)}) %collective-permute-start.1) | collective-permute-done | bytes 442400 | tf_op jit(solution)/shard_map/ppermute | solution.py:494
  18.4 0.0 collective-permute-start.2
  18.4 0.0 collective-permute-start.5
  18.4 5.2 %near_blocks.1 = (bf16[288,2048]{1,0:T(8,128)(2,1)S(1)}, bf16[2,144,1024]{2,1,0:T(8,128)(2,1)S(1)}, bf16[1536,3072]{1,0:T(8,128)(2,1)S(1)}) custom-call(bf16[144,1536]{1,0:T(8,128)(2,1)S(1)} %collective-permute-done.refs_0_, bf16[144,1536]{1,0:T(8,128)(2,1)S(1)} %collective-permute-done.1.refs_1_, bf16[1536,3072]{1,0:T(8,128)(2,1)} %refs_2_.1), custom_call_target="tpu_custom_call" | custom-call | flops 100000000 | bytes 1000000 | tf_op jit(solution)/shard_map/near_blocks/pallas_call | solution.py:152
  23.7 0.6 collective-permute-start.3
  24.3 6.4 %collective-permute-done.2.x_ref = bf16[144,1536]{1,0:T(8,128)(2,1)S(1)} collective-permute-done((bf16[144,1536]{1,0:T(8,128)(2,1)S(1)}, bf16[144,1536]{1,0:T(8,128)(2,1)S(1)}, u32[]{:S(2)}, u32[]{:S(2)}) %collective-permute-start.2) | collective-permute-done | bytes 442400 | tf_op jit(solution)/shard_map/ppermute | solution.py:494
  30.6 1.3 %keys_values.1 = (bf16[144,2048]{1,0:T(8,128)(2,1)S(1)}, bf16[144,1536]{1,0:T(8,128)(2,1)S(1)}) custom-call(bf16[144,1536]{1,0:T(8,128)(2,1)S(1)} %collective-permute-done.2.x_ref, bf16[1536,3072]{1,0:T(8,128)(2,1)S(1)} %get-tuple-element.36.w_ref), custom_call_target="tpu_custom_call" | custom-call | flops 20000000000 | bytes 1000000 | tf_op jit(solution)/shard_map/keys_values/pallas_call | solution.py:185
  32.0 0.3 collective-permute-start.4
  32.2 0.6 queries.1.q_ref
  32.9 0.0 collective-permute-done.5.refs_5_
  32.9 1.3 %collective-permute-done.4.refs_4_ = bf16[144,2048]{1,0:T(8,128)(2,1)S(1)} collective-permute-done((bf16[144,2048]{1,0:T(8,128)(2,1)S(1)}, bf16[144,2048]{1,0:T(8,128)(2,1)S(1)}, u32[]{:S(2)}, u32[]{:S(2)}) %collective-permute-start.4) | collective-permute-done | bytes 589856 | tf_op jit(solution)/shard_map/ppermute | solution.py:521
  34.2 0.0 collective-permute-done.3.refs_3_
  34.2 7.6 %spatial_attention.3 = (bf16[144,1024]{1,0:T(8,128)(2,1)S(1)}, bf16[144,1024]{1,0:T(8,128)(2,1)S(1)}) custom-call(bf16[2,144,1024]{2,1,0:T(8,128)(2,1)S(1)} %get-tuple-element.39.q_ref, bf16[288,2048]{1,0:T(8,128)(2,1)S(1)} %get-tuple-element.40.refs_0_, bf16[144,2048]{1,0:T(8,128)(2,1)S(1)} %get-tuple-element.41.refs_1_, ...), custom_call_target="tpu_custom_call" | custom-call | flops 339738624 | bytes 1000000 | tf_op jit(solution)/shard_map/spatial_attention/pallas_call | solution.py:294
  41.8 0.1 collective-permute-start.7
  41.9 3.2 %collective-permute-start.8 = (bf16[144,1024]{1,0:T(8,128)(2,1)S(1)}, bf16[144,1024]{1,0:T(8,128)(2,1)S(1)}, u32[]{:S(2)}, u32[]{:S(2)}) collective-permute-start(bf16[144,1024]{1,0:T(8,128)(2,1)S(1)} %get-tuple-element.50), channel_id=1, source_target_pairs={{0,6},{1,7},{2,0},{3,1},{4,2},{5,3},{6,4},{7,5},{8,14},{9,15},{10,... | collective-permute-start | bytes 884744 | tf_op jit(solution)/shard_map/ppermute | solution.py:494
  45.1 0.0 slice-start
  45.1 4.2 %spatial_attention.4 = bf16[144,1024]{1,0:T(8,128)(2,1)S(1)} custom-call(bf16[1,144,1024]{2,1,0:T(8,128)(2,1)S(1)} %queries.1.q_ref, bf16[288,2048]{1,0:T(8,128)(2,1)S(1)} %get-tuple-element.40.refs_0_, bf16[144,2048]{1,0:T(8,128)(2,1)S(1)} %get-tuple-element.41.refs_1_, bf16[144,2048]{1,0:T(8,128)(2,1)S(1)} %get-tuple-element.42.refs_2_, ...), custom_call_target="tpu_custom_call" | custom-call | flops 169869312 | bytes 1000000 | tf_op jit(solution)/shard_map/spatial_attention/pallas_call | solution.py:294
  49.3 0.0 copy-start
  49.3 0.0 copy-start.1
  49.3 0.0 slice-start.1
  49.3 0.1 collective-permute-start.6
  49.4 4.2 %spatial_attention.5.refs_0_ = bf16[144,1024]{1,0:T(8,128)(2,1)S(1)} custom-call(bf16[1,144,1024]{2,1,0:T(8,128)(2,1)S(1)} %get-tuple-element.48.q_ref, bf16[288,2048]{1,0:T(8,128)(2,1)S(1)} %get-tuple-element.40.refs_0_, bf16[144,2048]{1,0:T(8,128)(2,1)S(1)} %get-tuple-element.41.refs_1_, bf16[144,2048]{1,0:T(8,128)(2,1)S(1)} %get-tuple-element.42.refs_2_, ...), custom_call_target="tpu_custom_call" | custom-call | flops 169869312 | bytes 1000000 | tf_op jit(solution)/shard_map/spatial_attention/pallas_call | solution.py:294
  53.6 0.0 collective-permute-done.7.refs_1_
  53.6 4.1 %collective-permute-done.8.refs_2_ = bf16[144,1024]{1,0:T(8,128)(2,1)S(1)} collective-permute-done((bf16[144,1024]{1,0:T(8,128)(2,1)S(1)}, bf16[144,1024]{1,0:T(8,128)(2,1)S(1)}, u32[]{:S(2)}, u32[]{:S(2)}) %collective-permute-start.8) | collective-permute-done | bytes 294944 | tf_op jit(solution)/shard_map/ppermute | solution.py:494
  57.8 0.0 copy-done
  57.8 0.0 copy-done.1
  57.8 2.6 %early_rows.1 = (bf16[4,144,1536]{2,1,0:T(8,128)(2,1)S(1)}, bf16[4,144,1536]{2,1,0:T(8,128)(2,1)S(1)}) custom-call(s32[3]{0:T(128)S(1)} %pad_add_fusion.scalars, bf16[144,1024]{1,0:T(8,128)(2,1)S(1)} %spatial_attention.5.refs_0_, bf16[144,1024]{1,0:T(8,128)(2,1)S(1)} %collective-permute-done.7.refs_1_, bf16[144,1024]{1,0:T(8,128)(2,1)S(1)} %collective-permute-done.8.refs_2_, ...), custom_call_target="tpu_custom_call" | custom-call | flops 1358954496 | bytes 8000000 | tf_op jit(solution)/shard_map/early_rows/pallas_call | solution.py:341
  60.3 0.0 collective-permute-done.6.s_ref
  60.3 0.0 slice-start.2
  60.4 2.0 %late_rows.1 = (bf16[144,1536]{1,0:T(8,128)(2,1)S(1)}, bf16[144,4,1536]{2,1,0:T(4,128)(2,1)S(1)}) custom-call(s32[3]{0:T(128)S(1)} %pad_add_fusion.scalars, bf16[144,1024]{1,0:T(8,128)(2,1)S(1)} %collective-permute-done.6.s_ref, bf16[4,144,1536]{2,1,0:T(8,128)(2,1)S(1)} %get-tuple-element.51.norm_ref, bf16[4,144,1536]{2,1,0:T(8,128)(2,1)S(1)} %copy-done, ...), custom_call_target="tpu_custom_call" | custom-call | flops 452984832 | bytes 8000000 | tf_op jit(solution)/shard_map/late_rows/pallas_call | solution.py:369
  62.4 29.4 %all_to_all.10.x_ref = bf16[16,9,4,1536]{3,2,1,0:T(4,128)(2,1)S(1)} all-to-all(bf16[16,9,4,1536]{3,2,1,0:T(4,128)(2,1)S(1)} %bitcast.11), channel_id=1, replica_groups=mesh['tm'=16,'space'=8] {'tm'}, dimensions={0} | all-to-all | bytes 3538944 | tf_op jit(solution)/shard_map/all_to_all | solution.py:498
  91.8 0.0 slice-done
  91.8 0.0 slice-done.1
  91.8 0.0 slice-done.2
  91.8 0.0 copy-start.2
  91.8 8.6 %temporal_attention.1 = bf16[16,9,4,1024]{3,2,1,0:T(4,128)(2,1)S(1)} custom-call(s32[3]{0:T(128)S(1)} %pad_add_fusion.scalars, bf16[16,9,4,1536]{3,2,1,0:T(4,128)(2,1)S(1)} %all_to_all.10.x_ref, bf16[1536,3072]{1,0:T(8,128)(2,1)S(1)} %bitcast.13), custom_call_target="tpu_custom_call" | custom-call | flops 5435817984 | bytes 14000000 | tf_op jit(solution)/shard_map/temporal_attention/pallas_call | solution.py:427
  100.4 18.4 %all_to_all.11 = bf16[16,9,4,1024]{3,2,1,0:T(4,128)(2,1)S(1)} all-to-all(bf16[16,9,4,1024]{3,2,1,0:T(4,128)(2,1)S(1)} %temporal_attention.1), channel_id=1, replica_groups=mesh['tm'=16,'space'=8] {'tm'}, dimensions={0} | all-to-all | bytes 2359296 | tf_op jit(solution)/shard_map/all_to_all | solution.py:498
  118.8 0.0 copy-done.2
  118.8 4.1 %encoded_rows.1 = bf16[4,144,1536]{2,1,0:T(8,128)(2,1)} custom-call(s32[3]{0:T(128)S(1)} %pad_add_fusion.scalars, bf16[144,4,1024]{2,1,0:T(4,128)(2,1)S(1)} %bitcast.10, bf16[4,144,1536]{2,1,0:T(8,128)(2,1)S(1)} %get-tuple-element.53.m_ref, bf16[144,1536]{1,0:T(8,128)(2,1)S(1)} %get-tuple-element.54.late_ref, bf16[1024,1536]{1,0:T(8,128)(2,1)S(1)} %copy-done.2), custom_call_target="tpu_custom_call" | custom-call | flops 1811939328 | bytes 8000000 | tf_op jit(solution)/shard_map/encoded_rows/pallas_call | solution.py:474
  (1 shorter events, 0.0 us)
Async XLA Ops:
  1.4 13.6 %collective-permute-start = (bf16[144,1536]{1,0:T(8,128)(2,1)S(1)}, bf16[144,1536]{1,0:T(8,128)(2,1)S(1)}, u32[]{:S(2)}, u32[]{:S(2)}) collective-permute-start(bf16[144,1536]{1,0:T(8,128)(2,1)S(1)} %get-tuple-element.56), channel_id=1, source_target_pairs={{0,6},{1,7},{2,0},{3,1},{4,2},{5,3},{6,4},{7,5},{8,14},{9,15},{10,... | collective-permute-start | bytes 1327112 | tf_op jit(solution)/shard_map/ppermute | solution.py:494
  5.6 12.8 %collective-permute-start.1 = (bf16[144,1536]{1,0:T(8,128)(2,1)S(1)}, bf16[144,1536]{1,0:T(8,128)(2,1)S(1)}, u32[]{:S(2)}, u32[]{:S(2)}) collective-permute-start(bf16[144,1536]{1,0:T(8,128)(2,1)S(1)} %get-tuple-element.55), channel_id=1, source_target_pairs={{0,2},{1,3},{2,4},{3,5},{4,6},{5,7},{6,0},{7,1},{8,10},{9,11},{10,... | collective-permute-start | bytes 1327112 | tf_op jit(solution)/shard_map/ppermute | solution.py:494
  18.4 12.2 %collective-permute-start.2 = (bf16[144,1536]{1,0:T(8,128)(2,1)S(1)}, bf16[144,1536]{1,0:T(8,128)(2,1)S(1)}, u32[]{:S(2)}, u32[]{:S(2)}) collective-permute-start(bf16[144,1536]{1,0:T(8,128)(2,1)S(1)} %get-tuple-element.31), channel_id=1, source_target_pairs={{0,4},{1,5},{2,6},{3,7},{4,0},{5,1},{6,2},{7,3},{8,12},{9,13},{10,... | collective-permute-start | bytes 1327112 | tf_op jit(solution)/shard_map/ppermute | solution.py:494
  18.4 14.5 %collective-permute-start.5 = (bf16[144,2048]{1,0:T(8,128)(2,1)S(1)}, bf16[144,2048]{1,0:T(8,128)(2,1)S(1)}, u32[]{:S(2)}, u32[]{:S(2)}) collective-permute-start(bf16[144,2048]{1,0:T(8,128)(2,1)S(1)} %get-tuple-element.42.refs_2_), channel_id=1, source_target_pairs={{0,1},{1,0},{2,3},{3,2},{4,5},{5,4},{6,7},{7,6},{8,9},{9,8},{10,11... | collective-permute-start | bytes 1769480 | tf_op jit(solution)/shard_map/ppermute | solution.py:514
  23.7 10.6 %collective-permute-start.3 = (bf16[288,2048]{1,0:T(8,128)(2,1)S(1)}, bf16[288,2048]{1,0:T(8,128)(2,1)S(1)}, u32[]{:S(2)}, u32[]{:S(2)}) collective-permute-start(bf16[288,2048]{1,0:T(8,128)(2,1)S(1)} %get-tuple-element.40.refs_0_), channel_id=1, source_target_pairs={{0,1},{1,0},{2,3},{3,2},{4,5},{5,4},{6,7},{7,6},{8,9},{9,8},{10,11... | collective-permute-start | bytes 3538952 | tf_op jit(solution)/shard_map/ppermute | solution.py:518
  32.0 2.3 %collective-permute-start.4 = (bf16[144,2048]{1,0:T(8,128)(2,1)S(1)}, bf16[144,2048]{1,0:T(8,128)(2,1)S(1)}, u32[]{:S(2)}, u32[]{:S(2)}) collective-permute-start(bf16[144,2048]{1,0:T(8,128)(2,1)S(1)} %get-tuple-element.41.refs_1_), channel_id=1, source_target_pairs={{0,1},{1,0},{2,3},{3,2},{4,5},{5,4},{6,7},{7,6},{8,9},{9,8},{10,11... | collective-permute-start | bytes 1769480 | tf_op jit(solution)/shard_map/ppermute | solution.py:521
  41.8 11.8 %collective-permute-start.7 = (bf16[144,1024]{1,0:T(8,128)(2,1)S(1)}, bf16[144,1024]{1,0:T(8,128)(2,1)S(1)}, u32[]{:S(2)}, u32[]{:S(2)}) collective-permute-start(bf16[144,1024]{1,0:T(8,128)(2,1)S(1)} %get-tuple-element.49), channel_id=1, source_target_pairs={{0,2},{1,3},{2,4},{3,5},{4,6},{5,7},{6,0},{7,1},{8,10},{9,11},{10,... | collective-permute-start | bytes 884744 | tf_op jit(solution)/shard_map/ppermute | solution.py:494
  41.9 15.9 %collective-permute-start.8 = (bf16[144,1024]{1,0:T(8,128)(2,1)S(1)}, bf16[144,1024]{1,0:T(8,128)(2,1)S(1)}, u32[]{:S(2)}, u32[]{:S(2)}) collective-permute-start(bf16[144,1024]{1,0:T(8,128)(2,1)S(1)} %get-tuple-element.50), channel_id=1, source_target_pairs={{0,6},{1,7},{2,0},{3,1},{4,2},{5,3},{6,4},{7,5},{8,14},{9,15},{10,... | collective-permute-start | bytes 884744 | tf_op jit(solution)/shard_map/ppermute | solution.py:494
  45.1 46.6 %slice-start = ((s8[9437184]{0:T(1024)(128)(4,1)}), s8[1048576]{0:T(1024)(128)(4,1)S(1)}, s32[]{:S(2)}) async-start(s8[9437184]{0:T(1024)(128)(4,1)} %bitcast.12), calls=%async_computation.2 | async-start | bytes 2097152
  49.3 8.5 %copy-start = (bf16[4,144,1536]{2,1,0:T(8,128)(2,1)S(1)}, bf16[4,144,1536]{2,1,0:T(8,128)(2,1)}, u32[]{:S(2)}) copy-start(bf16[4,144,1536]{2,1,0:T(8,128)(2,1)} %x_ref.1) | copy-start | bytes 5308420
  49.3 8.5 %copy-start.1 = (bf16[1024,1536]{1,0:T(8,128)(2,1)S(1)}, bf16[1024,1536]{1,0:T(8,128)(2,1)}, u32[]{:S(2)}) copy-start(bf16[1024,1536]{1,0:T(8,128)(2,1)} %w_ref.5) | copy-start | bytes 9437188
  49.3 42.4 %slice-start.1 = ((s8[9437184]{0:T(1024)(128)(4,1)}), s8[4194304]{0:T(1024)(128)(4,1)S(1)}, s32[]{:S(2)}) async-start(s8[9437184]{0:T(1024)(128)(4,1)} %bitcast.12), calls=%async_computation.3 | async-start | bytes 8388608
  49.3 11.0 %collective-permute-start.6 = (bf16[144,1024]{1,0:T(8,128)(2,1)S(1)}, bf16[144,1024]{1,0:T(8,128)(2,1)S(1)}, u32[]{:S(2)}, u32[]{:S(2)}) collective-permute-start(bf16[144,1024]{1,0:T(8,128)(2,1)S(1)} %spatial_attention.4), channel_id=1, source_target_pairs={{0,4},{1,5},{2,6},{3,7},{4,0},{5,1},{6,2},{7,3},{8,12},{9,13},{10,... | collective-permute-start | bytes 884744 | tf_op jit(solution)/shard_map/ppermute | solution.py:494
  60.3 31.4 %slice-start.2 = ((s8[9437184]{0:T(1024)(128)(4,1)}), s8[4194304]{0:T(1024)(128)(4,1)S(1)}, s32[]{:S(2)}) async-start(s8[9437184]{0:T(1024)(128)(4,1)} %bitcast.12), calls=%async_computation.4 | async-start | bytes 8388608
  91.8 27.0 %copy-start.2 = (bf16[1024,1536]{1,0:T(8,128)(2,1)S(1)}, bf16[1024,1536]{1,0:T(8,128)(2,1)}, u32[]{:S(2)}) copy-start(bf16[1024,1536]{1,0:T(8,128)(2,1)} %w_ref.7) | copy-start | bytes 9437188
